TPU v7x, 32 devices: a whole 2x2x4 slice. The times are simulated.
32 devices in a mesh: space: 16 (over z, x, core), filt: 2 (over y).
Axes of the slice: x: 2, y: 2, z: 4, core: 2. Of those that a mesh axis runs over, the one named last changes fastest.
Arguments:
- volume: bfloat16 [32, 32, 32, 128], P('space', 'filt'), may hold values from -6 to 6
- kernel: bfloat16 [3, 3, 3, 256, 128], P(None, None, None, 'filt'), may hold values from -0.109375 to 0.109375
- out_grad: bfloat16 [16, 16, 16, 256], P('space', None, None, 'filt'), may hold values from -6 to 6
Outputs:
- features: bfloat16 [16, 16, 16, 256], P('space', None, None, 'filt')
- in_grad: bfloat16 [32, 32, 32, 128], P('space', 'filt')
- kernel_grad: float32 [3, 3, 3, 256, 128], P(None, None, None, 'filt')
All inputs are finite; a program needn't handle non-finite values.
Results may differ from a plain program's by a relative error of at most 0.001.
Values may be sent and summed in bfloat16 or wider, within the bound.
No kernel may reach another device: no remote copies, remote signals or barrier semaphores. Data moves between devices by JAX's collectives and lax.ppermute only.
A program may use at most 64 MiB of HBM per device.

v0:
```python
import jax
import jax.numpy as jnp
from jax import lax
from jax.sharding import PartitionSpec as P


def from_behind(shard, axis, by):
    peers = lax.axis_size(axis)
    pairs = [(i, i + by) for i in range(peers) if 0 <= i + by < peers]
    return lax.ppermute(shard, axis, pairs)


def take_patch(padded, a, b, c, dims):
    ox, oy, oz = dims
    chan = padded.shape[3]
    return lax.slice(
        padded, (a, b, c, 0), (a + 2 * ox - 1, b + 2 * oy - 1, c + 2 * oz - 1, chan), (2, 2, 2, 1)
    )


def conv_out(padded, weights, dims):
    chan = padded.shape[3]
    total = jnp.zeros((dims[0] * dims[1] * dims[2], weights.shape[3]), jnp.float32)
    for a in range(3):
        for b in range(3):
            for c in range(3):
                patch = take_patch(padded, a, b, c, dims).reshape(-1, chan)
                total = total + lax.dot_general(
                    patch,
                    weights[a, b, c],
                    (((1,), (1,)), ((), ())),
                    preferred_element_type=jnp.float32,
                )
    return total


def weight_terms(padded, grad_rows, dims):
    chan = padded.shape[3]
    pieces = []
    for a in range(3):
        for b in range(3):
            for c in range(3):
                patch = take_patch(padded, a, b, c, dims).reshape(-1, chan)
                pieces.append(
                    lax.dot_general(
                        grad_rows,
                        patch,
                        (((0,), (0,)), ((), ())),
                        preferred_element_type=jnp.float32,
                    )
                )
    return jnp.stack(pieces).reshape(3, 3, 3, grad_rows.shape[1], chan)


def parity_transpose(grad_window, weights):
    extent_x, extent_y, extent_z, channels_out = grad_window.shape
    channels_in = weights.shape[4]
    grad_padded = jnp.pad(grad_window, ((1, 1), (1, 1), (1, 1), (0, 0)))
    tap_table = (((0, 1), (2, 0)), ((1, 1),))
    shape_out = (extent_x + 1, extent_y + 1, extent_z + 1)
    plane_list = []
    for parity_x in range(2):
        row_list = []
        for parity_y in range(2):
            depth_list = []
            for parity_z in range(2):
                summed = jnp.zeros(
                    (shape_out[0] * shape_out[1] * shape_out[2], channels_in), jnp.float32
                )
                for a, shift_x in tap_table[parity_x]:
                    for b, shift_y in tap_table[parity_y]:
                        for c, shift_z in tap_table[parity_z]:
                            window_piece = lax.slice(
                                grad_padded,
                                (shift_x, shift_y, shift_z, 0),
                                (
                                    shift_x + shape_out[0],
                                    shift_y + shape_out[1],
                                    shift_z + shape_out[2],
                                    channels_out,
                                ),
                            ).reshape(-1, channels_out)
                            summed = summed + jnp.dot(
                                window_piece, weights[a, b, c], preferred_element_type=jnp.float32
                            )
                depth_list.append(
                    summed.reshape(shape_out[0], shape_out[1], shape_out[2], channels_in)
                )
            joined = jnp.stack(depth_list, axis=3).reshape(
                shape_out[0], shape_out[1], 2 * shape_out[2], channels_in
            )
            row_list.append(joined)
        joined = jnp.stack(row_list, axis=2).reshape(
            shape_out[0], 2 * shape_out[1], 2 * shape_out[2], channels_in
        )
        plane_list.append(joined)
    return jnp.stack(plane_list, axis=1).reshape(
        2 * shape_out[0], 2 * shape_out[1], 2 * shape_out[2], channels_in
    )


def on_device(volume, kernel, out_grad):
    planes, rows, depth, cin = volume.shape
    grad_all, kern_all = (
        lax.all_gather(out_grad, "filt", axis=3, tiled=True),
        lax.all_gather(kernel, "filt", axis=3, tiled=True),
    )
    nfilt = lax.axis_size("filt")
    ox = planes // 2
    oz = depth // 2
    oy_dev = rows // 2
    oy_all = rows * nfilt // 2
    row_id = lax.axis_index("filt")
    whole = lax.all_gather(volume, "filt", axis=1, tiled=True)
    lower = from_behind(whole[planes - 1 :], "space", 1)
    padded = jnp.pad(jnp.concatenate([lower, whole], axis=0), ((0, 0), (1, 1), (1, 1), (0, 0)))
    dims = (ox, oy_all, oz)
    features = (
        conv_out(padded, kernel, dims).reshape(ox, oy_all, oz, kernel.shape[3]).astype(jnp.bfloat16)
    )
    kgrad = weight_terms(padded, out_grad.reshape(-1, out_grad.shape[3]), dims)
    factor = float(ox * lax.axis_size("space") * oy_all * oz) ** (-0.5)
    kernel_grad = lax.psum(kgrad, "space") * factor
    grad_pad = jnp.pad(grad_all, ((0, 0), (0, 1), (0, 0), (0, 0)))
    window = lax.dynamic_slice_in_dim(grad_pad, row_id * oy_dev, oy_dev + 1, 1)
    scatter = parity_transpose(window, kern_all)
    face = scatter[0:1, 1 : rows + 1, 1 : depth + 1]
    above = from_behind(face, "space", -1)
    gradient = scatter[1 : planes + 1, 1 : rows + 1, 1 : depth + 1]
    gradient = gradient.at[planes - 1 :].add(above)
    return (features, gradient.astype(jnp.bfloat16), kernel_grad)


def solution(mesh):
    return jax.shard_map(
        on_device,
        mesh=mesh,
        in_specs=(
            P("space", "filt", None, None),
            P(None, None, None, "filt", None),
            P("space", None, None, "filt"),
        ),
        out_specs=(
            P("space", None, None, "filt"),
            P("space", "filt", None, None),
            P(None, None, None, "filt", None),
        ),
        check_vma=False,
    )
```

profile of v0, /device:TPU:0, one launch (start us, length us, event | category | flops | bytes accessed | tf_op | source)
XLA Modules:
  0.0 300.1 jit_solution(8022967536255415456)
XLA Ops:
  8.1 10.2 %all_gather.9 = bf16[2,32,32,128]{3,2,1,0:T(8,128)(2,1)S(1)} all-gather(bf16[2,16,32,128]{3,2,1,0:T(8,128)(2,1)} %param.5), channel_id=1, replica_groups=mesh['space'=16,'filt'=2] {'filt'}, dimensions={1}, use_global_device_ids=true | all-gather | bytes 786432 | tf_op jit(solution)/shard_map/all_gather | solution.py:114
  18.3 1.3 collective-permute-start
  19.7 5.0 %all_gather.10 = bf16[1,16,16,256]{3,2,1,0:T(8,128)(2,1)S(1)} all-gather(bf16[1,16,16,128]{3,2,1,0:T(8,128)(2,1)S(1)} %copy-done.50), channel_id=1, replica_groups=mesh['space'=16,'filt'=2] {'filt'}, dimensions={3}, use_global_device_ids=true | all-gather | bytes 196608 | tf_op jit(solution)/shard_map/all_gather | solution.py:105
  27.9 4.9 %slice.380 = bf16[1,16,16,128]{3,2,1,0:T(8,128)(2,1)} slice(bf16[3,34,34,128]{3,2,1,0:T(8,128)(2,1)S(1)} %fusion.34), slice={[0:1:1], [0:31:2], [0:31:2], [0:128:1]} | slice | bytes 131072 | tf_op jit(solution)/shard_map/slice | solution.py:16
  32.8 4.8 %slice.382 = bf16[1,16,16,128]{3,2,1,0:T(8,128)(2,1)} slice(bf16[3,34,34,128]{3,2,1,0:T(8,128)(2,1)S(1)} %fusion.34), slice={[0:1:1], [0:31:2], [1:32:2], [0:128:1]} | slice | bytes 131072 | tf_op jit(solution)/shard_map/slice | solution.py:16
  37.6 4.8 %slice.384 = bf16[1,16,16,128]{3,2,1,0:T(8,128)(2,1)} slice(bf16[3,34,34,128]{3,2,1,0:T(8,128)(2,1)S(1)} %fusion.34), slice={[0:1:1], [0:31:2], [2:33:2], [0:128:1]} | slice | bytes 131072 | tf_op jit(solution)/shard_map/slice | solution.py:16
  42.4 4.8 %slice.386 = bf16[1,16,16,128]{3,2,1,0:T(8,128)(2,1)} slice(bf16[3,34,34,128]{3,2,1,0:T(8,128)(2,1)S(1)} %fusion.34), slice={[0:1:1], [1:32:2], [0:31:2], [0:128:1]} | slice | bytes 131072 | tf_op jit(solution)/shard_map/slice | solution.py:16
  47.3 4.8 %slice.388 = bf16[1,16,16,128]{3,2,1,0:T(8,128)(2,1)} slice(bf16[3,34,34,128]{3,2,1,0:T(8,128)(2,1)S(1)} %fusion.34), slice={[0:1:1], [1:32:2], [1:32:2], [0:128:1]} | slice | bytes 131072 | tf_op jit(solution)/shard_map/slice | solution.py:16
  52.1 4.8 %slice.390 = bf16[1,16,16,128]{3,2,1,0:T(8,128)(2,1)} slice(bf16[3,34,34,128]{3,2,1,0:T(8,128)(2,1)S(1)} %fusion.34), slice={[0:1:1], [1:32:2], [2:33:2], [0:128:1]} | slice | bytes 131072 | tf_op jit(solution)/shard_map/slice | solution.py:16
  56.9 4.8 %slice.392 = bf16[1,16,16,128]{3,2,1,0:T(8,128)(2,1)} slice(bf16[3,34,34,128]{3,2,1,0:T(8,128)(2,1)S(1)} %fusion.34), slice={[0:1:1], [2:33:2], [0:31:2], [0:128:1]} | slice | bytes 131072 | tf_op jit(solution)/shard_map/slice | solution.py:16
  61.7 4.8 %slice.394 = bf16[1,16,16,128]{3,2,1,0:T(8,128)(2,1)} slice(bf16[3,34,34,128]{3,2,1,0:T(8,128)(2,1)S(1)} %fusion.34), slice={[0:1:1], [2:33:2], [1:32:2], [0:128:1]} | slice | bytes 131072 | tf_op jit(solution)/shard_map/slice | solution.py:16
  66.5 4.8 %slice.396 = bf16[1,16,16,128]{3,2,1,0:T(8,128)(2,1)} slice(bf16[3,34,34,128]{3,2,1,0:T(8,128)(2,1)S(1)} %fusion.34), slice={[0:1:1], [2:33:2], [2:33:2], [0:128:1]} | slice | bytes 131072 | tf_op jit(solution)/shard_map/slice | solution.py:16
  71.3 4.8 %slice.398 = bf16[1,16,16,128]{3,2,1,0:T(8,128)(2,1)} slice(bf16[3,34,34,128]{3,2,1,0:T(8,128)(2,1)S(1)} %fusion.34), slice={[1:2:1], [0:31:2], [0:31:2], [0:128:1]} | slice | bytes 131072 | tf_op jit(solution)/shard_map/slice | solution.py:16
  76.2 4.8 %slice.400 = bf16[1,16,16,128]{3,2,1,0:T(8,128)(2,1)} slice(bf16[3,34,34,128]{3,2,1,0:T(8,128)(2,1)S(1)} %fusion.34), slice={[1:2:1], [0:31:2], [1:32:2], [0:128:1]} | slice | bytes 131072 | tf_op jit(solution)/shard_map/slice | solution.py:16
  81.0 4.8 %slice.402 = bf16[1,16,16,128]{3,2,1,0:T(8,128)(2,1)} slice(bf16[3,34,34,128]{3,2,1,0:T(8,128)(2,1)S(1)} %fusion.34), slice={[1:2:1], [0:31:2], [2:33:2], [0:128:1]} | slice | bytes 131072 | tf_op jit(solution)/shard_map/slice | solution.py:16
  85.8 4.8 %slice.404 = bf16[1,16,16,128]{3,2,1,0:T(8,128)(2,1)} slice(bf16[3,34,34,128]{3,2,1,0:T(8,128)(2,1)S(1)} %fusion.34), slice={[1:2:1], [1:32:2], [0:31:2], [0:128:1]} | slice | bytes 131072 | tf_op jit(solution)/shard_map/slice | solution.py:16
  90.6 4.8 %slice.406 = bf16[1,16,16,128]{3,2,1,0:T(8,128)(2,1)} slice(bf16[3,34,34,128]{3,2,1,0:T(8,128)(2,1)S(1)} %fusion.34), slice={[1:2:1], [1:32:2], [1:32:2], [0:128:1]} | slice | bytes 131072 | tf_op jit(solution)/shard_map/slice | solution.py:16
  95.5 4.8 %slice.408 = bf16[1,16,16,128]{3,2,1,0:T(8,128)(2,1)} slice(bf16[3,34,34,128]{3,2,1,0:T(8,128)(2,1)S(1)} %fusion.34), slice={[1:2:1], [1:32:2], [2:33:2], [0:128:1]} | slice | bytes 131072 | tf_op jit(solution)/shard_map/slice | solution.py:16
  100.3 4.8 %slice.410 = bf16[1,16,16,128]{3,2,1,0:T(8,128)(2,1)} slice(bf16[3,34,34,128]{3,2,1,0:T(8,128)(2,1)S(1)} %fusion.34), slice={[1:2:1], [2:33:2], [0:31:2], [0:128:1]} | slice | bytes 131072 | tf_op jit(solution)/shard_map/slice | solution.py:16
  105.1 4.8 %slice.412 = bf16[1,16,16,128]{3,2,1,0:T(8,128)(2,1)} slice(bf16[3,34,34,128]{3,2,1,0:T(8,128)(2,1)S(1)} %fusion.34), slice={[1:2:1], [2:33:2], [1:32:2], [0:128:1]} | slice | bytes 131072 | tf_op jit(solution)/shard_map/slice | solution.py:16
  109.9 4.8 %slice.414 = bf16[1,16,16,128]{3,2,1,0:T(8,128)(2,1)} slice(bf16[3,34,34,128]{3,2,1,0:T(8,128)(2,1)S(1)} %fusion.34), slice={[1:2:1], [2:33:2], [2:33:2], [0:128:1]} | slice | bytes 131072 | tf_op jit(solution)/shard_map/slice | solution.py:16
  114.8 4.8 %slice.416 = bf16[1,16,16,128]{3,2,1,0:T(8,128)(2,1)} slice(bf16[3,34,34,128]{3,2,1,0:T(8,128)(2,1)S(1)} %fusion.34), slice={[2:3:1], [0:31:2], [0:31:2], [0:128:1]} | slice | bytes 131072 | tf_op jit(solution)/shard_map/slice | solution.py:16
  119.6 4.8 %slice.418 = bf16[1,16,16,128]{3,2,1,0:T(8,128)(2,1)} slice(bf16[3,34,34,128]{3,2,1,0:T(8,128)(2,1)S(1)} %fusion.34), slice={[2:3:1], [0:31:2], [1:32:2], [0:128:1]} | slice | bytes 131072 | tf_op jit(solution)/shard_map/slice | solution.py:16
  124.4 4.8 %slice.420 = bf16[1,16,16,128]{3,2,1,0:T(8,128)(2,1)} slice(bf16[3,34,34,128]{3,2,1,0:T(8,128)(2,1)S(1)} %fusion.34), slice={[2:3:1], [0:31:2], [2:33:2], [0:128:1]} | slice | bytes 131072 | tf_op jit(solution)/shard_map/slice | solution.py:16
  129.2 4.8 %slice.422 = bf16[1,16,16,128]{3,2,1,0:T(8,128)(2,1)} slice(bf16[3,34,34,128]{3,2,1,0:T(8,128)(2,1)S(1)} %fusion.34), slice={[2:3:1], [1:32:2], [0:31:2], [0:128:1]} | slice | bytes 131072 | tf_op jit(solution)/shard_map/slice | solution.py:16
  134.1 4.8 %slice.424 = bf16[1,16,16,128]{3,2,1,0:T(8,128)(2,1)} slice(bf16[3,34,34,128]{3,2,1,0:T(8,128)(2,1)S(1)} %fusion.34), slice={[2:3:1], [1:32:2], [1:32:2], [0:128:1]} | slice | bytes 131072 | tf_op jit(solution)/shard_map/slice | solution.py:16
  138.9 4.8 %slice.426 = bf16[1,16,16,128]{3,2,1,0:T(8,128)(2,1)} slice(bf16[3,34,34,128]{3,2,1,0:T(8,128)(2,1)S(1)} %fusion.34), slice={[2:3:1], [1:32:2], [2:33:2], [0:128:1]} | slice | bytes 131072 | tf_op jit(solution)/shard_map/slice | solution.py:16
  143.7 4.8 %slice.428 = bf16[1,16,16,128]{3,2,1,0:T(8,128)(2,1)} slice(bf16[3,34,34,128]{3,2,1,0:T(8,128)(2,1)S(1)} %fusion.34), slice={[2:3:1], [2:33:2], [0:31:2], [0:128:1]} | slice | bytes 131072 | tf_op jit(solution)/shard_map/slice | solution.py:16
  148.5 4.8 %slice.430 = bf16[1,16,16,128]{3,2,1,0:T(8,128)(2,1)} slice(bf16[3,34,34,128]{3,2,1,0:T(8,128)(2,1)S(1)} %fusion.34), slice={[2:3:1], [2:33:2], [1:32:2], [0:128:1]} | slice | bytes 131072 | tf_op jit(solution)/shard_map/slice | solution.py:16
  153.4 4.8 %slice.432 = bf16[1,16,16,128]{3,2,1,0:T(8,128)(2,1)} slice(bf16[3,34,34,128]{3,2,1,0:T(8,128)(2,1)S(1)} %fusion.34), slice={[2:3:1], [2:33:2], [2:33:2], [0:128:1]} | slice | bytes 131072 | tf_op jit(solution)/shard_map/slice | solution.py:16
  158.2 1.1 fusion.32
  159.3 1.7 fusion.123
  161.0 1.1 fusion.31
  162.1 1.1 fusion.30
  163.2 1.1 fusion.29
  164.3 1.1 fusion.28
  165.4 1.1 fusion.27
  166.5 1.1 fusion.26
  171.8 2.0 copy.26
  173.9 1.1 convolution_add_fusion.44
  183.8 1.2 fusion.36
  186.0 1.1 convolution_bitcast_fusion
  190.9 1.6 stack_reshape.47
  197.2 1.3 pad_maximum_fusion.2
  205.3 1.3 collective-permute-start.1
  206.6 75.9 %all-reduce.5.cloned.1.call-done = f32[3,3,3,128,128]{4,3,2,1,0:T(8,128)} async-done(((f32[3,3,3,128,128]{4,3,2,1,0:T(8,128)}), f32[3,3,3,128,128]{4,3,2,1,0:T(8,128)}) %all-reduce.5.cloned.1.call-update) | async-done | bytes 1769488 | tf_op jit(solution)/shard_map/psum | solution.py:123
  282.5 2.9 broadcast_multiply_fusion
  286.1 5.8 %scatter-add.4 = bf16[2,16,32,128]{3,0,2,1:T(2,128)(2,1)S(1)} dynamic-update-slice(bf16[2,16,32,128]{3,0,2,1:T(2,128)(2,1)S(1)} %slice.500, bf16[1,16,32,128]{3,0,2,1:T(2,128)(2,1)S(1)} %slice_add_fusion, s32[]{:T(128)} %constant.40.clone.1, s32[]{:T(128)} %constant.36.clone.1, s32[]{:T(128)} %constant.36.clone.1, s32[]{:T(128)} %constant.36.clone.1) | dynamic-update-slice | bytes 262148 | tf_op jit(solution)/shard_map/scatter-add | solution.py:130
  (216 shorter events, 33.1 us)
Async XLA Ops:
  8.0 11.7 %copy-start.50 = (bf16[1,16,16,128]{3,2,1,0:T(8,128)(2,1)S(1)}, bf16[1,16,16,128]{3,2,1,0:T(8,128)(2,1)}, u32[]{:S(2)}) copy-start(bf16[1,16,16,128]{3,2,1,0:T(8,128)(2,1)} %param.7) | copy-start | bytes 196612
  8.0 175.7 %all-gather.2.cloned.1.call-start = ((), (), s32[]{:S(2)}) async-start(), calls=%async_computation | async-start | bytes 2654208 | tf_op jit(solution)/shard_map/all_gather | solution.py:106
  18.3 9.2 %collective-permute-start = (bf16[1,32,32,128]{3,2,1,0:T(8,128)(2,1)S(1)}, bf16[1,32,32,128]{3,2,1,0:T(8,128)(2,1)S(1)}, u32[]{:S(2)}, u32[]{:S(2)}) collective-permute-start(bf16[1,32,32,128]{3,2,1,0:T(8,128)(2,1)S(1)} %slice.472), channel_id=1, source_target_pairs={{0,2},{2,4},{4,6},{6,8},{8,10},{10,12},{12,14},{14,16},{16,18},{18... | collective-permute-start | bytes 786440 | tf_op jit(solution)/shard_map/ppermute | solution.py:10
  19.6 262.9 %all-reduce.5.cloned.1.call-start = ((), (), s32[]{:S(2)}) async-start(), calls=%async_computation.1 | async-start | bytes 3538944 | tf_op jit(solution)/shard_map/psum | solution.py:123
  47.3 112.0 %copy-start = (bf16[3,3,3,128,128]{4,3,2,1,0:T(8,128)(2,1)S(1)}, bf16[3,3,3,128,128]{4,3,2,1,0:T(8,128)(2,1)}, u32[]{:S(2)}) copy-start(bf16[3,3,3,128,128]{4,3,2,1,0:T(8,128)(2,1)} %param.6) | copy-start | bytes 2654212
  158.2 9.5 %copy-start.47 = (bf16[1,16,16,128]{3,2,1,0:T(8,128)(2,1)S(1)}, bf16[1,16,16,128]{3,2,1,0:T(8,128)(2,1)}, u32[]{:S(2)}) copy-start(bf16[1,16,16,128]{3,2,1,0:T(8,128)(2,1)} %slice.394) | copy-start | bytes 196612
  158.2 9.5 %copy-start.51 = (bf16[1,16,16,128]{3,2,1,0:T(8,128)(2,1)S(1)}, bf16[1,16,16,128]{3,2,1,0:T(8,128)(2,1)}, u32[]{:S(2)}) copy-start(bf16[1,16,16,128]{3,2,1,0:T(8,128)(2,1)} %param.7) | copy-start | bytes 196612
  159.3 8.6 %copy-start.45 = (bf16[1,16,16,128]{3,2,1,0:T(8,128)(2,1)S(1)}, bf16[1,16,16,128]{3,2,1,0:T(8,128)(2,1)}, u32[]{:S(2)}) copy-start(bf16[1,16,16,128]{3,2,1,0:T(8,128)(2,1)} %slice.396) | copy-start | bytes 196612
  161.0 7.1 %copy-start.43 = (bf16[1,16,16,128]{3,2,1,0:T(8,128)(2,1)S(1)}, bf16[1,16,16,128]{3,2,1,0:T(8,128)(2,1)}, u32[]{:S(2)}) copy-start(bf16[1,16,16,128]{3,2,1,0:T(8,128)(2,1)} %slice.398) | copy-start | bytes 196612
  162.1 6.2 %copy-start.41 = (bf16[1,16,16,128]{3,2,1,0:T(8,128)(2,1)S(1)}, bf16[1,16,16,128]{3,2,1,0:T(8,128)(2,1)}, u32[]{:S(2)}) copy-start(bf16[1,16,16,128]{3,2,1,0:T(8,128)(2,1)} %slice.400) | copy-start | bytes 196612
  163.2 5.3 %copy-start.39 = (bf16[1,16,16,128]{3,2,1,0:T(8,128)(2,1)S(1)}, bf16[1,16,16,128]{3,2,1,0:T(8,128)(2,1)}, u32[]{:S(2)}) copy-start(bf16[1,16,16,128]{3,2,1,0:T(8,128)(2,1)} %slice.402) | copy-start | bytes 196612
  164.3 4.4 %copy-start.37 = (bf16[1,16,16,128]{3,2,1,0:T(8,128)(2,1)S(1)}, bf16[1,16,16,128]{3,2,1,0:T(8,128)(2,1)}, u32[]{:S(2)}) copy-start(bf16[1,16,16,128]{3,2,1,0:T(8,128)(2,1)} %slice.404) | copy-start | bytes 196612
  165.4 3.5 %copy-start.35 = (bf16[1,16,16,128]{3,2,1,0:T(8,128)(2,1)S(1)}, bf16[1,16,16,128]{3,2,1,0:T(8,128)(2,1)}, u32[]{:S(2)}) copy-start(bf16[1,16,16,128]{3,2,1,0:T(8,128)(2,1)} %slice.406) | copy-start | bytes 196612
  166.5 2.6 copy-start.33
  167.6 1.7 copy-start.31
  167.9 1.7 copy-start.29
  168.1 1.7 copy-start.27
  168.3 1.7 copy-start.25
  168.5 1.7 copy-start.23
  168.7 1.7 copy-start.21
  168.9 1.7 copy-start.19
  169.1 1.7 copy-start.17
  173.8 5.4 %copy-start.49 = (bf16[1,16,16,128]{3,2,1,0:T(8,128)(2,1)S(1)}, bf16[1,16,16,128]{3,2,1,0:T(8,128)(2,1)}, u32[]{:S(2)}) copy-start(bf16[1,16,16,128]{3,2,1,0:T(8,128)(2,1)} %slice.392) | copy-start | bytes 196612
  173.8 5.6 %copy-start.48 = (bf16[1,16,16,128]{3,2,1,0:T(8,128)(2,1)S(1)}, bf16[1,16,16,128]{3,2,1,0:T(8,128)(2,1)}, u32[]{:S(2)}) copy-start(bf16[1,16,16,128]{3,2,1,0:T(8,128)(2,1)} %slice.394) | copy-start | bytes 196612
  173.8 5.8 %copy-start.46 = (bf16[1,16,16,128]{3,2,1,0:T(8,128)(2,1)S(1)}, bf16[1,16,16,128]{3,2,1,0:T(8,128)(2,1)}, u32[]{:S(2)}) copy-start(bf16[1,16,16,128]{3,2,1,0:T(8,128)(2,1)} %slice.396) | copy-start | bytes 196612
  173.8 5.9 %copy-start.44 = (bf16[1,16,16,128]{3,2,1,0:T(8,128)(2,1)S(1)}, bf16[1,16,16,128]{3,2,1,0:T(8,128)(2,1)}, u32[]{:S(2)}) copy-start(bf16[1,16,16,128]{3,2,1,0:T(8,128)(2,1)} %slice.398) | copy-start | bytes 196612
  173.8 6.1 %copy-start.42 = (bf16[1,16,16,128]{3,2,1,0:T(8,128)(2,1)S(1)}, bf16[1,16,16,128]{3,2,1,0:T(8,128)(2,1)}, u32[]{:S(2)}) copy-start(bf16[1,16,16,128]{3,2,1,0:T(8,128)(2,1)} %slice.400) | copy-start | bytes 196612
  173.8 6.3 %copy-start.40 = (bf16[1,16,16,128]{3,2,1,0:T(8,128)(2,1)S(1)}, bf16[1,16,16,128]{3,2,1,0:T(8,128)(2,1)}, u32[]{:S(2)}) copy-start(bf16[1,16,16,128]{3,2,1,0:T(8,128)(2,1)} %slice.402) | copy-start | bytes 196612
  175.0 5.3 %copy-start.38 = (bf16[1,16,16,128]{3,2,1,0:T(8,128)(2,1)S(1)}, bf16[1,16,16,128]{3,2,1,0:T(8,128)(2,1)}, u32[]{:S(2)}) copy-start(bf16[1,16,16,128]{3,2,1,0:T(8,128)(2,1)} %slice.404) | copy-start | bytes 196612
  176.1 4.5 %copy-start.36 = (bf16[1,16,16,128]{3,2,1,0:T(8,128)(2,1)S(1)}, bf16[1,16,16,128]{3,2,1,0:T(8,128)(2,1)}, u32[]{:S(2)}) copy-start(bf16[1,16,16,128]{3,2,1,0:T(8,128)(2,1)} %slice.406) | copy-start | bytes 196612
  177.1 3.6 %copy-start.34 = (bf16[1,16,16,128]{3,2,1,0:T(8,128)(2,1)S(1)}, bf16[1,16,16,128]{3,2,1,0:T(8,128)(2,1)}, u32[]{:S(2)}) copy-start(bf16[1,16,16,128]{3,2,1,0:T(8,128)(2,1)} %slice.408) | copy-start | bytes 196612
  178.2 2.7 copy-start.32
  179.2 1.9 copy-start.30
  179.4 1.9 copy-start.28
  179.6 1.9 copy-start.26
  179.8 1.9 copy-start.24
  180.0 1.8 copy-start.22
  180.2 1.8 copy-start.20
  180.3 1.8 copy-start.18
  180.5 1.8 copy-start.16
  180.7 1.8 copy-start.14
  180.9 1.8 copy-start.12
  181.1 1.8 copy-start.10
  182.9 3.1 %copy-start.8 = (bf16[1,9,16,256]{3,2,1,0:T(8,128)(2,1)S(1)}, bf16[1,9,16,256]{3,2,1,0:T(8,128)(2,1)}, u32[]{:S(2)}) copy-start(bf16[1,9,16,256]{3,2,1,0:T(8,128)(2,1)} %copy-done.7) | copy-start | bytes 221188
  183.8 3.6 %copy-start.1 = (bf16[3,3,3,256,128]{4,3,2,1,0:T(8,128)(2,1)S(1)}, bf16[3,3,3,256,128]{4,3,2,1,0:T(8,128)(2,1)}, u32[]{:S(2)}) copy-start(bf16[3,3,3,256,128]{4,3,2,1,0:T(8,128)(2,1)} %all-gather.2.cloned.1.call-done) | copy-start | bytes 5308420
  187.1 2.9 copy-start.3
  193.5 2.7 copy-start.2
  205.3 80.4 %collective-permute-start.1 = (f32[1,16,32,128]{3,0,2,1:T(1,128)S(1)}, f32[1,16,32,128]{3,0,2,1:T(1,128)S(1)}, u32[]{:S(2)}, u32[]{:S(2)}) collective-permute-start(f32[1,16,32,128]{3,0,2,1:T(1,128)S(1)} %slice.502), channel_id=1, source_target_pairs={{2,0},{4,2},{6,4},{8,6},{10,8},{12,10},{14,12},{16,14},{18,16},{20... | collective-permute-start | bytes 786440 | tf_op jit(solution)/shard_map/ppermute | solution.py:10
  (8 other events, 11.5 us)
Sparse Core Ops, SparseCore 0:
  19.7 31.7 all-gather.1
Sparse Core Ops, SparseCore 1:
  183.8 98.6 all-reduce.4
where the time goes:
time: 301 us; the launch traced here: 300 us
  local copies, waits for them, and re-layouts  149 us (50%)
  waiting for transfers between devices  75.9 us (25%)
  matrix products  32.1 us (11%)
  between operations  16.8 us (6%)
  blocking collectives  15.2 us (5%)
  other arithmetic  8.03 us (3%)
    slice x27, local copies, waits for them, and re-layouts, take_patch(): lax.slice(padded, (a, b, c, 0), (a + 2 * ox - 1, b + 2 * oy - 1, c + 2 *...  130 us
    psum x1, waiting for transfers between devices, on_device(): kernel_grad = lax.psum(kgrad, 'space') * factor  75.9 us
    dot_general x27, matrix products, weight_terms(): lax.dot_general(grad_rows, patch, (((0,), (0,)), ((), ())), preferred_ele...  11.5 us
    dot_general x27, matrix products, conv_out(): lax.dot_general(patch, weights[a, b, c], (((1,), (1,)), ((), ())), prefer...  11.1 us
    all_gather x1, blocking collectives, on_device(): whole = lax.all_gather(volume, 'filt', axis=1, tiled=True)  10.2 us
    dot_general x27, matrix products, parity_transpose(): jnp.dot(window_piece, weights[a, b, c], preferred_element_type=jnp.float32)  9.56 us
    another operation x11, local copies, waits for them, and re-layouts, parity_transpose(): jnp.stack(depth_list, axis=3)  6.23 us
  transfers between devices with their start and end apart: 4, of which 1 were waited for; matrix products, arithmetic and copies ran while one was open for 61% of the time, Pallas kernels for 0%

commit v1 on v0

v1 whole, which is shorter than its diff:
```python
import functools

import jax
import jax.numpy as jnp
from jax import lax
from jax.experimental import pallas as pl
from jax.experimental.pallas import tpu as pltpu
from jax.sharding import PartitionSpec as P

F32, BF16, F16 = jnp.float32, jnp.bfloat16, jnp.float16
TOP = 15.0
TAPS = 27


def tap(a, b, c):
    return (a * 3 + b) * 3 + c


def uses(parity):
    return ((1, 0),) if parity == 0 else ((2, 0), (0, 1))


def shift_index(dx, dy, dz):
    return (dx * 2 + dy) * 2 + dz


def dot(x, y, dims):
    return lax.dot_general(x, y, (dims, ((), ())), preferred_element_type=F32)


def wide_weights(w_ref, a, b):
    return jnp.concatenate([w_ref[tap(a, b, 1)], w_ref[tap(a, b, 2)]], axis=1)


def grad_kernel(blocks, half, place, g_ref, above_ref, w_ref, gt_ref, part_ref, shifted, cells_of):
    rows, oz, cout = g_ref.shape
    last = lax.broadcasted_iota(jnp.int32, (rows, oz, cout), 1) == oz - 1
    for dx, ref in ((0, g_ref), (1, above_ref)):
        grad = ref[...].astype(F32)
        moved = jnp.where(last, 0.0, pltpu.roll(grad, oz - 1, 1))
        for dz, value in ((0, grad), (1, moved)):
            shifted[dx * 2 + dz, :rows] = value
            shifted[dx * 2 + dz, rows:] = jnp.zeros((1, oz, cout), F32)
    cells = half * oz
    for dx in range(2):
        for dy in range(2):
            for dz in range(2):
                for block in range(blocks):
                    first = place[block] * half + dy
                    piece = shifted[dx * 2 + dz, pl.ds(first, half)].reshape(cells, cout)
                    index = shift_index(dx, dy, dz)
                    span = pl.ds(block * cells, cells)
                    cells_of[index, span] = piece.astype(BF16)
                    gt_ref[index, :, span] = piece.T.astype(BF16)
    cin = w_ref.shape[2]
    for p in range(2):
        for r in range(2):
            total, odd = None, None
            for a, dx in uses(p):
                for b, dy in uses(r):
                    both = dot(cells_of[shift_index(dx, dy, 0)], wide_weights(w_ref, a, b), ((1,), (0,)))
                    late = dot(cells_of[shift_index(dx, dy, 1)], w_ref[tap(a, b, 0)], ((1,), (0,)))
                    total = both if total is None else total + both
                    odd = late if odd is None else odd + late
            parts = (total[:, :cin], total[:, cin:] + odd)
            for block in range(blocks):
                for j in range(half):
                    at = (block * half + j) * oz
                    for q in range(2):
                        part_ref[block, p, 2 * j + r, pl.ds(q, oz, stride=2), :] = parts[q][at : at + oz]


def weight_kernel(blocks, *refs):
    volumes = refs[:blocks]
    gt_ref, sum_ref, class_ref, wide = refs[blocks:]
    planes, rows, depth, cin = volumes[0].shape
    half, oz = rows // 2, depth // 2
    for block in range(blocks):
        wide[...] = volumes[block][...].astype(F32)
        for p in range(2):
            for row in range(rows):
                at = (block * half + row // 2) * oz
                for q in range(2):
                    piece = wide[p, row, pl.ds(q, oz, stride=2), :]
                    class_ref[p * 2 + row % 2, at : at + oz, q * cin : (q + 1) * cin] = piece.astype(BF16)
    largest = None
    for p in range(2):
        for r in range(2):
            patch = class_ref[p * 2 + r]
            for a, dx in uses(p):
                for b, dy in uses(r):
                    both = dot(gt_ref[shift_index(dx, dy, 0)], patch, ((1,), (0,)))
                    late = dot(gt_ref[shift_index(dx, dy, 1)], patch[:, cin:], ((1,), (0,)))
                    for c, term in ((0, late), (1, both[:, :cin]), (2, both[:, cin:])):
                        sum_ref[tap(a, b, c)] = term
                        size = jnp.abs(term)
                        largest = size if largest is None else jnp.maximum(largest, size)
    sum_ref[TAPS] = jnp.maximum(jnp.floor(jnp.log2(largest)) + 1.0, -100.0)


def feature_kernel(blocks, half, place, class_ref, w_ref, own_ref, send_ref, total):
    rows, oz, cout = own_ref.shape
    cin = w_ref.shape[2]
    first_cell = lax.broadcasted_iota(jnp.int32, (rows, oz, cout), 1) == 0
    total[...] = jnp.zeros_like(total)
    for dx in range(2):
        for dy in range(2):
            level, late = None, None
            for p in range(2):
                for a, shift_x in uses(p):
                    for r in range(2):
                        for b, shift_y in uses(r):
                            if (shift_x, shift_y) != (dx, dy):
                                continue
                            patch = class_ref[p * 2 + r]
                            both = dot(patch, wide_weights(w_ref, a, b), ((1,), (1,)))
                            odd = dot(patch[:, cin:], w_ref[tap(a, b, 0)], ((1,), (1,)))
                            level = both if level is None else level + both
                            late = odd if late is None else late + odd
            late = late.reshape(rows, oz, cout)
            level = level.reshape(rows, oz, cout) + jnp.where(first_cell, 0.0, pltpu.roll(late, 1, 1))
            for block in range(blocks):
                where = pl.ds(place[block] * half + dy, half)
                total[dx, where] = total[dx, where] + level[block * half : (block + 1) * half]
    own_ref[...] = total[0, :rows]
    send_ref[...] = total[1, :rows]


def call(kernel, out_shape, arguments, scratch=(), placed=False, flops=0):
    vmem = pl.BlockSpec(memory_space=pltpu.VMEM)
    smem = pl.BlockSpec(memory_space=pltpu.SMEM)
    size = sum(x.size * x.dtype.itemsize for x in list(arguments) + list(out_shape))
    return pl.pallas_call(
        kernel,
        out_shape=out_shape,
        in_specs=[smem if placed and i == 0 else vmem for i in range(len(arguments))],
        out_specs=[vmem] * len(out_shape),
        scratch_shapes=list(scratch),
        compiler_params=pltpu.CompilerParams(vmem_limit_bytes=32 * 1024 * 1024),
        cost_estimate=pl.CostEstimate(flops=flops, bytes_accessed=size, transcendentals=0),
    )(*arguments)


def swap(x, axis, bits):
    peers = lax.axis_size(axis)
    return lax.ppermute(x, axis, [(i, i ^ bits) for i in range(peers)])


def move(x, axis, by):
    peers = lax.axis_size(axis)
    return lax.ppermute(x, axis, [(i, i + by) for i in range(peers) if 0 <= i + by < peers])


def is_level(x):
    return lax.broadcasted_iota(jnp.int32, x.shape, 0) == TAPS


def encode(x):
    return jnp.where(is_level(x), x, x * jnp.exp2(TOP - x[TAPS:])).astype(F16)


def decode(x):
    wide = x.astype(F32)
    return jnp.where(is_level(x), wide, wide * jnp.exp2(wide[TAPS:] - TOP))


def add(x, y):
    return jnp.where(is_level(x), jnp.maximum(x, y) + 1.0, x + y)


def pick(x, index):
    return lax.dynamic_index_in_dim(x, index, 1, keepdims=False)


def arrange(pieces, mine):
    shape = pieces[0].shape[:1] + (len(pieces),) + pieces[0].shape[1:]
    source = lax.broadcasted_iota(jnp.int32, shape, 1) ^ mine
    out = jnp.broadcast_to(pieces[-1][:, None], shape)
    for q in range(len(pieces) - 1):
        out = jnp.where(source == q, jnp.broadcast_to(pieces[q][:, None], shape), out)
    return out


def sum_over_space(terms, factor):
    _, cout, cin = terms.shape
    peers = lax.axis_size("space")
    nz = peers // 4
    index = lax.axis_index("space")
    core, x, z = index & 1, (index >> 1) & 1, index >> 2
    part = terms.reshape(TAPS + 1, 2, 2, nz, cout // peers, cin)
    part = add(pick(part, core), decode(swap(encode(pick(part, 1 - core)), "space", 1)))
    part = add(pick(part, x), decode(swap(encode(pick(part, 1 - x)), "space", 2)))
    got = [swap(encode(pick(part, z ^ q)), "space", 4 * q) for q in range(1, nz)]
    total = pick(part, z)
    for piece in got:
        total = add(total, decode(piece))
    total = encode(jnp.where(is_level(total), total, total * factor))
    total = arrange([total] + [swap(total, "space", 4 * q) for q in range(1, nz)], z)
    total = arrange([total, swap(total, "space", 2)], x)
    total = arrange([total, swap(total, "space", 1)], core)
    return decode(total)[:TAPS].reshape(3, 3, 3, cout, cin)


def on_device(volume, kernel, out_grad):
    planes, rows, depth, cin = volume.shape
    cout = kernel.shape[3]
    filt = lax.axis_size("filt")
    half, oz = rows // 2, depth // 2
    oy = half * filt
    cells = oy * oz
    mine = lax.axis_index("filt")
    if filt == 2:
        volumes = [volume, swap(volume, "filt", 1)]
        place = jnp.stack([mine, 1 - mine]).astype(jnp.int32)
    else:
        gathered = lax.all_gather(volume, "filt", axis=0, tiled=False)
        volumes = [gathered[i] for i in range(filt)]
        place = jnp.arange(filt, dtype=jnp.int32)
    above = move(out_grad, "space", -1)
    weights = kernel.reshape(TAPS, cout, cin)
    flops = 2 * TAPS * cells * cin * cout
    grads, part = call(
        functools.partial(grad_kernel, filt, half),
        [
            jax.ShapeDtypeStruct((8, cout, cells), BF16),
            jax.ShapeDtypeStruct((filt, planes, rows, depth, cin), F32),
        ],
        (place, out_grad[0], above[0], weights),
        [pltpu.VMEM((4, oy + 1, oz, cout), F32), pltpu.VMEM((8, cells, cout), BF16)],
        placed=True,
        flops=flops,
    )
    terms, classes = call(
        functools.partial(weight_kernel, filt),
        [
            jax.ShapeDtypeStruct((TAPS + 1, cout, cin), F32),
            jax.ShapeDtypeStruct((4, cells, 2 * cin), BF16),
        ],
        (*volumes, grads),
        [pltpu.VMEM(volume.shape, F32)],
        flops=flops,
    )
    own, send = call(
        functools.partial(feature_kernel, filt, half),
        [jax.ShapeDtypeStruct((oy, oz, cout), F32)] * 2,
        (place, classes, weights),
        [pltpu.VMEM((2, oy + 1, oz, cout), F32)],
        placed=True,
        flops=flops,
    )
    features = (own + move(send, "space", 1)).astype(BF16)[None]
    if filt == 2:
        gradient = (part[0] + swap(part[1], "filt", 1)).astype(BF16)
    else:
        gradient = lax.psum_scatter(part, "filt", scatter_dimension=0).astype(BF16)
    factor = float(lax.axis_size("space") * cells) ** (-0.5)
    return features, gradient, sum_over_space(terms, factor)


def solution(mesh):
    return jax.shard_map(
        on_device,
        mesh=mesh,
        in_specs=(
            P("space", "filt", None, None),
            P(None, None, None, "filt", None),
            P("space", None, None, "filt"),
        ),
        out_specs=(
            P("space", None, None, "filt"),
            P("space", "filt", None, None),
            P(None, None, None, "filt", None),
        ),
        check_vma=False,
    )
```

time: 301 us -> 64.9 us (0.22)
  local copies, waits for them, and re-layouts: 149 us -> 5.53 us
  waiting for transfers between devices: 75.9 us -> 25.3 us
  matrix products: 32.1 us -> 0 us
  starting transfers between devices: 2.68 us -> 20.7 us
  between operations: 16.8 us -> 0.91 us
  blocking collectives: 15.2 us -> 0 us
    slice x31 -> x0, local copies, waits for them, and re-layouts: 131 us -> none  [the longest x27 130 us: take_patch(): lax.slice(padded, (a, b, c, 0), (a + 2 * ox - 1, b + 2 * oy - 1, c + 2 *...]
    psum x1 -> x0, waiting for transfers between devices: 75.9 us -> none  [on_device(): kernel_grad = lax.psum(kgrad, 'space') * factor]
    dot_general x81 -> x0, matrix products: 32.1 us -> none  [the longest x27 11.5 us: weight_terms(): lax.dot_general(grad_rows, patch, (((0,), (0,)), ((), ())), preferred_ele...]
    ppermute x2 -> x14, waiting for transfers between devices: 0.01 us -> 25.3 us  [the longest x12 23.4 us: swap(): return lax.ppermute(x, axis, [(i, i ^ bits) for i in range(peers)])]
    ppermute x2 -> x14, starting transfers between devices: 2.6 us -> 20.7 us  [the longest x12 18.1 us: swap(): return lax.ppermute(x, axis, [(i, i ^ bits) for i in range(peers)])]
    all_gather x2 -> x0, blocking collectives: 15.2 us -> none  [the longest x1 10.2 us: on_device(): whole = lax.all_gather(volume, 'filt', axis=1, tiled=True)]
    another operation x14 -> x0, local copies, waits for them, and re-layouts: 7.05 us -> none  [the longest x11 6.23 us: parity_transpose(): jnp.stack(depth_list, axis=3)]
    scatter-add x1 -> x0, local copies, waits for them, and re-layouts: 5.8 us -> none  [on_device(): gradient = gradient.at[planes - 1:].add(above)]
  transfers between devices with their start and end apart: 4 -> 14, of which waited for: 1 -> 9; matrix products, arithmetic and copies ran while one was open for 61% -> 3% of each run, Pallas kernels for 0% -> 4%
where the time goes in v1:
time: 64.9 us; the launch traced here: 64.5 us
  waiting for transfers between devices  25.3 us (39%)
  starting transfers between devices  20.7 us (32%)
  other arithmetic  9.12 us (14%)
  local copies, waits for them, and re-layouts  5.53 us (9%)
  Pallas kernels  2.93 us (5%)
  between operations  0.91 us (1%)
    ppermute x12, waiting for transfers between devices, swap(): return lax.ppermute(x, axis, [(i, i ^ bits) for i in range(peers)])  23.4 us
    ppermute x12, starting transfers between devices, swap(): return lax.ppermute(x, axis, [(i, i ^ bits) for i in range(peers)])  18.1 us
    unnamed x14, local copies, waits for them, and re-layouts  5.5 us
    pallas_call x3, Pallas kernels, call(): pl.pallas_call(kernel, out_shape=out_shape, in_specs=[smem if placed and...  2.93 us
    ppermute x2, starting transfers between devices, move(): lax.ppermute(x, axis, [(i, i + by) for i in range(peers) if 0 <= i + by <...  2.58 us
    select_n x2, other arithmetic, add(): return jnp.where(is_level(x), jnp.maximum(x, y) + 1.0, x + y)  2.5 us
    ppermute x2, waiting for transfers between devices, move(): lax.ppermute(x, axis, [(i, i + by) for i in range(peers) if 0 <= i + by <...  1.97 us
    convert_element_type x6, other arithmetic, decode(): wide = x.astype(F32)  1.6 us
  transfers between devices with their start and end apart: 14, of which 9 were waited for; matrix products, arithmetic and copies ran while one was open for 3% of the time, Pallas kernels for 4%

profile of v1, /device:TPU:0, one launch (start us, length us, event | category | flops | bytes accessed | tf_op | source)
XLA Modules:
  0.0 64.5 jit_solution(9535624424489589115)
XLA Ops:
  0.6 3.0 %collective-permute-start = (bf16[2,16,32,128]{3,2,1,0:T(8,128)(2,1)}, bf16[2,16,32,128]{3,2,1,0:T(8,128)(2,1)S(1)}, u32[]{:S(2)}, u32[]{:S(2)}) collective-permute-start(bf16[2,16,32,128]{3,2,1,0:T(8,128)(2,1)} %refs_0_.1), channel_id=1, source_target_pairs={{0,1},{1,0},{2,3},{3,2},{4,5},{5,4},{6,7},{7,6},{8,9},{9,8},{10,11... | collective-permute-start | bytes 786440 | tf_op jit(solution)/shard_map/ppermute | solution.py:146
  3.7 1.3 %collective-permute-start.1 = (bf16[1,16,16,128]{3,2,1,0:T(8,128)(2,1)}, bf16[1,16,16,128]{3,2,1,0:T(8,128)(2,1)S(1)}, u32[]{:S(2)}, u32[]{:S(2)}) collective-permute-start(bf16[1,16,16,128]{3,2,1,0:T(8,128)(2,1)} %param.5), channel_id=1, source_target_pairs={{2,0},{4,2},{6,4},{8,6},{10,8},{12,10},{14,12},{16,14},{18,16},{20... | collective-permute-start | bytes 196616 | tf_op jit(solution)/shard_map/ppermute | solution.py:151
  5.0 0.1 pad_add_fusion.place
  5.0 2.0 %collective-permute-done.1 = bf16[1,16,16,128]{3,2,1,0:T(8,128)(2,1)S(1)} collective-permute-done((bf16[1,16,16,128]{3,2,1,0:T(8,128)(2,1)}, bf16[1,16,16,128]{3,2,1,0:T(8,128)(2,1)S(1)}, u32[]{:S(2)}, u32[]{:S(2)}) %collective-permute-start.1) | collective-permute-done | bytes 65568 | tf_op jit(solution)/shard_map/ppermute | solution.py:151
  7.0 1.2 %copy-done = bf16[3,3,3,128,128]{4,3,2,1,0:T(8,128)(2,1)S(1)} copy-done((bf16[3,3,3,128,128]{4,3,2,1,0:T(8,128)(2,1)S(1)}, bf16[3,3,3,128,128]{4,3,2,1,0:T(8,128)(2,1)}, u32[]{:S(2)}) %copy-start) | copy-done | bytes 884760
  8.2 0.8 %copy-done.5 = bf16[1,16,16,128]{3,2,1,0:T(8,128)(2,1)S(1)} copy-done((bf16[1,16,16,128]{3,2,1,0:T(8,128)(2,1)S(1)}, bf16[1,16,16,128]{3,2,1,0:T(8,128)(2,1)}, u32[]{:S(2)}) %copy-start.5) | copy-done | bytes 65560
  9.0 1.2 %shard_map.58 = (bf16[8,128,256]{2,1,0:T(8,128)(2,1)S(1)}, f32[2,2,16,32,128]{4,3,2,1,0:T(8,128)S(1)}) custom-call(s32[2]{0:T(128)S(1)} %pad_add_fusion.place, bf16[16,16,128]{2,1,0:T(8,128)(2,1)S(1)} %bitcast.84, bf16[16,16,128]{2,1,0:T(8,128)(2,1)S(1)} %bitcast.85, bf16[27,128,128]{2,1,0:T(8,128)(2,1)S(1)} %bitcast.79), custom_call_target="tpu_custom_call" | custom-call | flops 226492416 | bytes 2588680 | tf_op jit(solution)/shard_map/pallas_call | solution.py:133
  10.2 0.0 copy-start.3
  10.2 0.7 %copy-done.3 = bf16[2,16,32,128]{3,2,1,0:T(8,128)(2,1)} copy-done((bf16[2,16,32,128]{3,2,1,0:T(8,128)(2,1)}, bf16[2,16,32,128]{3,2,1,0:T(8,128)(2,1)S(1)}, u32[]{:S(2)}) %copy-start.3) | copy-done | bytes 262168
  10.9 0.9 %copy-done.2 = bf16[2,16,32,128]{3,2,1,0:T(8,128)(2,1)S(1)} copy-done((bf16[2,16,32,128]{3,2,1,0:T(8,128)(2,1)S(1)}, bf16[2,16,32,128]{3,2,1,0:T(8,128)(2,1)}, u32[]{:S(2)}) %copy-start.2) | copy-done | bytes 262168
  11.9 0.9 %copy-done.4 = bf16[2,16,32,128]{3,2,1,0:T(8,128)(2,1)S(1)} copy-done((bf16[2,16,32,128]{3,2,1,0:T(8,128)(2,1)S(1)}, bf16[2,16,32,128]{3,2,1,0:T(8,128)(2,1)}, u32[]{:S(2)}) %copy-start.4) | copy-done | bytes 262168
  12.8 0.5 shard_map.59
  13.4 1.0 %fusion = f16[28,2,4,8,128]{4,3,2,1,0:T(8,128)(2,1)} fusion(f32[28,2,2,4,8,128]{5,4,3,2,1,0:T(8,128)S(1)} %bitcast.82, s32[]{:T(128)S(6)} %select_n.120, f32[2,4,8,128]{3,2,1,0:T(8,128)S(1)} %fusion.22, pred[28]{0:T(512)(128)(4,1)S(1)} %iota_compare_fusion), kind=kLoop, calls=%fused_computation.3 | loop fusion | flops 688128 | bytes 1409056 | tf_op jit(solution)/shard_map/convert_element_type | solution.py:159
  14.4 2.6 %collective-permute-start.4 = (f16[28,2,4,8,128]{4,3,2,1,0:T(8,128)(2,1)}, f16[28,2,4,8,128]{4,3,2,1,0:T(8,128)(2,1)}, u32[]{:S(2)}, u32[]{:S(2)}) collective-permute-start(f16[28,2,4,8,128]{4,3,2,1,0:T(8,128)(2,1)} %fusion), channel_id=1, source_target_pairs={{0,2},{2,0},{4,6},{6,4},{8,10},{10,8},{12,14},{14,12},{16,18},{18,... | collective-permute-start | bytes 1376264 | tf_op jit(solution)/shard_map/ppermute | solution.py:146
  17.0 1.8 %collective-permute-done.4 = f16[28,2,4,8,128]{4,3,2,1,0:T(8,128)(2,1)} collective-permute-done((f16[28,2,4,8,128]{4,3,2,1,0:T(8,128)(2,1)}, f16[28,2,4,8,128]{4,3,2,1,0:T(8,128)(2,1)}, u32[]{:S(2)}, u32[]{:S(2)}) %collective-permute-start.4) | collective-permute-done | bytes 458784 | tf_op jit(solution)/shard_map/ppermute | solution.py:146
  18.8 1.1 %convert_element_type.45 = f32[28,2,4,8,128]{4,3,2,1,0:T(8,128)S(1)} convert(f16[28,2,4,8,128]{4,3,2,1,0:T(8,128)(2,1)} %collective-permute-done.4) | non-fusion elementwise | flops 229376 | bytes 1376256 | tf_op jit(solution)/shard_map/convert_element_type | solution.py:163
  19.9 1.3 %fusion.2 = f32[28,2,4,8,128]{4,3,2,1,0:T(8,128)S(1)} fusion(f32[28,2,2,4,8,128]{5,4,3,2,1,0:T(8,128)S(1)} %bitcast.83, s32[]{:T(128)S(6)} %select_n.119, f32[2,4,8,128]{3,2,1,0:T(8,128)S(1)} %fusion.19, pred[28]{0:T(512)(128)(4,1)S(1)} %iota_compare_fusion, f16[28,2,4,8,128]{4,3,2,1,0:T(8,128)(2,1)} %collective-permute-done.4), kind=kLoop, calls=%fused_computation.7 | loop fusion | flops 1605632 | bytes 2326560 | tf_op jit(solution)/shard_map/jit(_where)/select_n | solution.py:168
  21.3 0.9 %copy-done.6 = f32[28,2,4,8,128]{4,3,2,1,0:T(8,128)} copy-done((f32[28,2,4,8,128]{4,3,2,1,0:T(8,128)}, f32[28,2,4,8,128]{4,3,2,1,0:T(8,128)S(1)}, u32[]{:S(2)}) %copy-start.6) | copy-done | bytes 917528
  22.2 0.1 fusion.4
  22.3 1.9 %collective-permute-start.5 = (f16[28,4,8,128]{3,2,1,0:T(8,128)(2,1)S(1)}, f16[28,4,8,128]{3,2,1,0:T(8,128)(2,1)S(1)}, u32[]{:S(2)}, u32[]{:S(2)}) collective-permute-start(f16[28,4,8,128]{3,2,1,0:T(8,128)(2,1)S(1)} %fusion.4), channel_id=1, source_target_pairs={{0,4},{2,6},{4,0},{6,2},{8,12},{10,14},{12,8},{14,10},{16,20},{18,... | collective-permute-start | bytes 688136 | tf_op jit(solution)/shard_map/ppermute | solution.py:146
  24.1 6.1 %collective-permute-done.5 = f16[28,4,8,128]{3,2,1,0:T(8,128)(2,1)S(1)} collective-permute-done((f16[28,4,8,128]{3,2,1,0:T(8,128)(2,1)S(1)}, f16[28,4,8,128]{3,2,1,0:T(8,128)(2,1)S(1)}, u32[]{:S(2)}, u32[]{:S(2)}) %collective-permute-start.5) | collective-permute-done | bytes 229408 | tf_op jit(solution)/shard_map/ppermute | solution.py:146
  30.3 1.2 %fusion.6 = f32[28,4,8,128]{3,2,1,0:T(8,128)S(1)} fusion(f32[28,2,4,8,128]{4,3,2,1,0:T(8,128)} %copy-done.6, s32[]{:T(128)S(6)} %select_n.124, f32[4,8,128]{2,1,0:T(8,128)S(1)} %fusion.25, pred[28]{0:T(512)(128)(4,1)S(1)} %iota_compare_fusion, f16[28,4,8,128]{3,2,1,0:T(8,128)(2,1)S(1)} %collective-permute-done.5), kind=kLoop, calls=%fused_computation.18 | loop fusion | flops 802816 | bytes 1163296 | tf_op jit(solution)/shard_map/jit(_where)/select_n | solution.py:168
  31.6 0.1 fusion.7
  31.7 2.7 %collective-permute-start.7 = (f16[28,8,128]{2,1,0:T(8,128)(2,1)S(1)}, f16[28,8,128]{2,1,0:T(8,128)(2,1)S(1)}, u32[]{:S(2)}, u32[]{:S(2)}) collective-permute-start(f16[28,8,128]{2,1,0:T(8,128)(2,1)S(1)} %get-tuple-element.17), channel_id=1, source_target_pairs={{0,16},{2,18},{4,20},{6,22},{8,24},{10,26},{12,28},{14,30},{16,0},... | collective-permute-start | bytes 172040 | tf_op jit(solution)/shard_map/ppermute | solution.py:146
  34.4 1.5 %collective-permute-start.6 = (f16[28,8,128]{2,1,0:T(8,128)(2,1)S(1)}, f16[28,8,128]{2,1,0:T(8,128)(2,1)S(1)}, u32[]{:S(2)}, u32[]{:S(2)}) collective-permute-start(f16[28,8,128]{2,1,0:T(8,128)(2,1)S(1)} %get-tuple-element.15), channel_id=1, source_target_pairs={{0,8},{2,10},{4,12},{6,14},{8,0},{10,2},{12,4},{14,6},{16,24},{18,... | collective-permute-start | bytes 172040 | tf_op jit(solution)/shard_map/ppermute | solution.py:146
  35.9 0.3 collective-permute-start.8
  36.2 1.0 %collective-permute-done.7 = f16[28,8,128]{2,1,0:T(8,128)(2,1)S(1)} collective-permute-done((f16[28,8,128]{2,1,0:T(8,128)(2,1)S(1)}, f16[28,8,128]{2,1,0:T(8,128)(2,1)S(1)}, u32[]{:S(2)}, u32[]{:S(2)}) %collective-permute-start.7) | collective-permute-done | bytes 57376 | tf_op jit(solution)/shard_map/ppermute | solution.py:146
  37.2 4.6 %collective-permute-done.8 = f16[28,8,128]{2,1,0:T(8,128)(2,1)S(1)} collective-permute-done((f16[28,8,128]{2,1,0:T(8,128)(2,1)S(1)}, f16[28,8,128]{2,1,0:T(8,128)(2,1)S(1)}, u32[]{:S(2)}, u32[]{:S(2)}) %collective-permute-start.8) | collective-permute-done | bytes 57376 | tf_op jit(solution)/shard_map/ppermute | solution.py:146
  41.9 0.2 multiply_select_fusion.6
  42.1 0.1 fusion.10
  42.2 0.9 %collective-permute-start.11 = (f16[28,8,128]{2,1,0:T(8,128)(2,1)S(1)}, f16[28,8,128]{2,1,0:T(8,128)(2,1)S(1)}, u32[]{:S(2)}, u32[]{:S(2)}) collective-permute-start(f16[28,8,128]{2,1,0:T(8,128)(2,1)S(1)} %fusion.10), channel_id=1, source_target_pairs={{0,24},{2,26},{4,28},{6,30},{8,16},{10,18},{12,20},{14,22},{16,8},... | collective-permute-start | bytes 172040 | tf_op jit(solution)/shard_map/ppermute | solution.py:146
  43.2 0.2 collective-permute-start.10
  43.3 3.3 %collective-permute-start.9 = (f16[28,8,128]{2,1,0:T(8,128)(2,1)S(1)}, f16[28,8,128]{2,1,0:T(8,128)(2,1)S(1)}, u32[]{:S(2)}, u32[]{:S(2)}) collective-permute-start(f16[28,8,128]{2,1,0:T(8,128)(2,1)S(1)} %fusion.10), channel_id=1, source_target_pairs={{0,16},{2,18},{4,20},{6,22},{8,24},{10,26},{12,28},{14,30},{16,0},... | collective-permute-start | bytes 172040 | tf_op jit(solution)/shard_map/ppermute | solution.py:146
  46.7 1.6 %collective-permute-done.11 = f16[28,8,128]{2,1,0:T(8,128)(2,1)S(1)} collective-permute-done((f16[28,8,128]{2,1,0:T(8,128)(2,1)S(1)}, f16[28,8,128]{2,1,0:T(8,128)(2,1)S(1)}, u32[]{:S(2)}, u32[]{:S(2)}) %collective-permute-start.11) | collective-permute-done | bytes 57376 | tf_op jit(solution)/shard_map/ppermute | solution.py:146
  48.3 0.6 collective-permute-done.9
  48.9 0.2 select_select_fusion
  49.0 1.0 %collective-permute-start.12 = (f16[28,4,8,128]{3,2,1,0:T(8,128)(2,1)S(1)}, f16[28,4,8,128]{3,2,1,0:T(8,128)(2,1)S(1)}, u32[]{:S(2)}, u32[]{:S(2)}) collective-permute-start(f16[28,4,8,128]{3,2,1,0:T(8,128)(2,1)S(1)} %select_select_fusion), channel_id=1, source_target_pairs={{0,4},{2,6},{4,0},{6,2},{8,12},{10,14},{12,8},{14,10},{16,20},{18,... | collective-permute-start | bytes 688136 | tf_op jit(solution)/shard_map/ppermute | solution.py:146
  50.1 0.6 collective-permute-start.3
  50.7 1.2 %shard_map.60 = (f32[16,16,128]{2,1,0:T(8,128)S(1)}, f32[16,16,128]{2,1,0:T(8,128)S(1)}) custom-call(s32[2]{0:T(128)S(1)} %pad_add_fusion.place, bf16[4,256,256]{2,1,0:T(8,128)(2,1)S(1)} %get-tuple-element.10.class_ref, bf16[27,128,128]{2,1,0:T(8,128)(2,1)S(1)} %bitcast.80), custom_call_target="tpu_custom_call" | custom-call | flops 226492416 | bytes 1671176 | tf_op jit(solution)/shard_map/pallas_call | solution.py:133
  51.9 1.3 %collective-permute-start.2 = (f32[16,16,128]{2,1,0:T(8,128)S(1)}, f32[16,16,128]{2,1,0:T(8,128)S(1)}, u32[]{:S(2)}, u32[]{:S(2)}) collective-permute-start(f32[16,16,128]{2,1,0:T(8,128)S(1)} %get-tuple-element.12), channel_id=1, source_target_pairs={{0,2},{2,4},{4,6},{6,8},{8,10},{10,12},{12,14},{14,16},{16,18},{18... | collective-permute-start | bytes 393224 | tf_op jit(solution)/shard_map/ppermute | solution.py:151
  53.2 1.9 %collective-permute-done.12 = f16[28,4,8,128]{3,2,1,0:T(8,128)(2,1)S(1)} collective-permute-done((f16[28,4,8,128]{3,2,1,0:T(8,128)(2,1)S(1)}, f16[28,4,8,128]{3,2,1,0:T(8,128)(2,1)S(1)}, u32[]{:S(2)}, u32[]{:S(2)}) %collective-permute-start.12) | collective-permute-done | bytes 229408 | tf_op jit(solution)/shard_map/ppermute | solution.py:146
  55.1 0.2 broadcast_select_fusion
  55.4 0.1 collective-permute-start.13
  55.5 0.6 %fusion.13 = bf16[1,16,16,128]{3,2,1,0:T(8,128)(2,1)} fusion(f32[16,16,128]{2,1,0:T(8,128)S(1)} %get-tuple-element.11, f32[16,16,128]{2,1,0:T(8,128)S(1)} %collective-permute-done.2), kind=kLoop, calls=%fused_computation.38 | loop fusion | flops 65536 | bytes 327680 | tf_op jit(solution)/shard_map/broadcast_in_dim | solution.py:251
  56.1 5.6 %collective-permute-done.3 = f32[2,16,32,128]{3,2,1,0:T(8,128)S(1)} collective-permute-done((f32[2,16,32,128]{3,2,1,0:T(8,128)S(1)}, f32[2,16,32,128]{3,2,1,0:T(8,128)S(1)}, u32[]{:S(2)}, u32[]{:S(2)}) %collective-permute-start.3) | collective-permute-done | bytes 524320 | tf_op jit(solution)/shard_map/ppermute | solution.py:146
  61.8 0.8 %fusion.3 = bf16[2,16,32,128]{3,2,1,0:T(8,128)(2,1)} fusion(f32[2,16,32,128]{3,2,1,0:T(8,128)S(1)} %collective-permute-done.3, f32[2,2,16,32,128]{4,3,2,1,0:T(8,128)S(1)} %get-tuple-element.13), kind=kLoop, calls=%fused_computation.12 | loop fusion | flops 262144 | bytes 1310720 | tf_op jit(solution)/shard_map/convert_element_type | solution.py:253
  62.6 0.4 select_convert_fusion
  63.0 1.5 %multiply_select_fusion = f32[27,2,2,4,8,128]{5,4,3,2,1,0:T(8,128)} fusion(f32[28,2,2,4,8,128]{5,4,3,2,1,0:T(8,128)S(1)} %select_convert_fusion, f32[2,2,4,8,128]{4,3,2,1,0:T(8,128)S(1)} %fusion.16, pred[27]{0:T(512)(128)(4,1)S(1)} %bitcast.87), kind=kLoop, calls=%fused_computation | loop fusion | flops 884736 | bytes 3604507 | tf_op jit(solution)/shard_map/jit(_where)/select_n | solution.py:164
  (32 shorter events, 0.3 us)
Async XLA Ops:
  0.6 9.6 %collective-permute-start = (bf16[2,16,32,128]{3,2,1,0:T(8,128)(2,1)}, bf16[2,16,32,128]{3,2,1,0:T(8,128)(2,1)S(1)}, u32[]{:S(2)}, u32[]{:S(2)}) collective-permute-start(bf16[2,16,32,128]{3,2,1,0:T(8,128)(2,1)} %refs_0_.1), channel_id=1, source_target_pairs={{0,1},{1,0},{2,3},{3,2},{4,5},{5,4},{6,7},{7,6},{8,9},{9,8},{10,11... | collective-permute-start | bytes 786440 | tf_op jit(solution)/shard_map/ppermute | solution.py:146
  3.7 3.3 %collective-permute-start.1 = (bf16[1,16,16,128]{3,2,1,0:T(8,128)(2,1)}, bf16[1,16,16,128]{3,2,1,0:T(8,128)(2,1)S(1)}, u32[]{:S(2)}, u32[]{:S(2)}) collective-permute-start(bf16[1,16,16,128]{3,2,1,0:T(8,128)(2,1)} %param.5), channel_id=1, source_target_pairs={{2,0},{4,2},{6,4},{8,6},{10,8},{12,10},{14,12},{16,14},{18,16},{20... | collective-permute-start | bytes 196616 | tf_op jit(solution)/shard_map/ppermute | solution.py:151
  7.0 1.2 %copy-start = (bf16[3,3,3,128,128]{4,3,2,1,0:T(8,128)(2,1)S(1)}, bf16[3,3,3,128,128]{4,3,2,1,0:T(8,128)(2,1)}, u32[]{:S(2)}) copy-start(bf16[3,3,3,128,128]{4,3,2,1,0:T(8,128)(2,1)} %param.4) | copy-start | bytes 2654212
  8.2 0.8 %copy-start.5 = (bf16[1,16,16,128]{3,2,1,0:T(8,128)(2,1)S(1)}, bf16[1,16,16,128]{3,2,1,0:T(8,128)(2,1)}, u32[]{:S(2)}) copy-start(bf16[1,16,16,128]{3,2,1,0:T(8,128)(2,1)} %param.5) | copy-start | bytes 196612
  10.2 0.7 %copy-start.3 = (bf16[2,16,32,128]{3,2,1,0:T(8,128)(2,1)}, bf16[2,16,32,128]{3,2,1,0:T(8,128)(2,1)S(1)}, u32[]{:S(2)}) copy-start(bf16[2,16,32,128]{3,2,1,0:T(8,128)(2,1)S(1)} %collective-permute-done.refs_1_) | copy-start | bytes 786436
  10.9 0.9 %copy-start.2 = (bf16[2,16,32,128]{3,2,1,0:T(8,128)(2,1)S(1)}, bf16[2,16,32,128]{3,2,1,0:T(8,128)(2,1)}, u32[]{:S(2)}) copy-start(bf16[2,16,32,128]{3,2,1,0:T(8,128)(2,1)} %refs_0_.1) | copy-start | bytes 786436
  11.9 0.9 %copy-start.4 = (bf16[2,16,32,128]{3,2,1,0:T(8,128)(2,1)S(1)}, bf16[2,16,32,128]{3,2,1,0:T(8,128)(2,1)}, u32[]{:S(2)}) copy-start(bf16[2,16,32,128]{3,2,1,0:T(8,128)(2,1)} %copy-done.3) | copy-start | bytes 786436
  14.4 4.4 %collective-permute-start.4 = (f16[28,2,4,8,128]{4,3,2,1,0:T(8,128)(2,1)}, f16[28,2,4,8,128]{4,3,2,1,0:T(8,128)(2,1)}, u32[]{:S(2)}, u32[]{:S(2)}) collective-permute-start(f16[28,2,4,8,128]{4,3,2,1,0:T(8,128)(2,1)} %fusion), channel_id=1, source_target_pairs={{0,2},{2,0},{4,6},{6,4},{8,10},{10,8},{12,14},{14,12},{16,18},{18,... | collective-permute-start | bytes 1376264 | tf_op jit(solution)/shard_map/ppermute | solution.py:146
  21.2 0.9 %copy-start.6 = (f32[28,2,4,8,128]{4,3,2,1,0:T(8,128)}, f32[28,2,4,8,128]{4,3,2,1,0:T(8,128)S(1)}, u32[]{:S(2)}) copy-start(f32[28,2,4,8,128]{4,3,2,1,0:T(8,128)S(1)} %fusion.2) | copy-start | bytes 2752516
  22.3 8.0 %collective-permute-start.5 = (f16[28,4,8,128]{3,2,1,0:T(8,128)(2,1)S(1)}, f16[28,4,8,128]{3,2,1,0:T(8,128)(2,1)S(1)}, u32[]{:S(2)}, u32[]{:S(2)}) collective-permute-start(f16[28,4,8,128]{3,2,1,0:T(8,128)(2,1)S(1)} %fusion.4), channel_id=1, source_target_pairs={{0,4},{2,6},{4,0},{6,2},{8,12},{10,14},{12,8},{14,10},{16,20},{18,... | collective-permute-start | bytes 688136 | tf_op jit(solution)/shard_map/ppermute | solution.py:146
  31.5 19.2 %copy-start.1 = (bf16[3,3,3,128,128]{4,3,2,1,0:T(8,128)(2,1)S(1)}, bf16[3,3,3,128,128]{4,3,2,1,0:T(8,128)(2,1)}, u32[]{:S(2)}) copy-start(bf16[3,3,3,128,128]{4,3,2,1,0:T(8,128)(2,1)} %param.4) | copy-start | bytes 2654212
  31.7 5.5 %collective-permute-start.7 = (f16[28,8,128]{2,1,0:T(8,128)(2,1)S(1)}, f16[28,8,128]{2,1,0:T(8,128)(2,1)S(1)}, u32[]{:S(2)}, u32[]{:S(2)}) collective-permute-start(f16[28,8,128]{2,1,0:T(8,128)(2,1)S(1)} %get-tuple-element.17), channel_id=1, source_target_pairs={{0,16},{2,18},{4,20},{6,22},{8,24},{10,26},{12,28},{14,30},{16,0},... | collective-permute-start | bytes 172040 | tf_op jit(solution)/shard_map/ppermute | solution.py:146
  34.4 7.5 %collective-permute-start.6 = (f16[28,8,128]{2,1,0:T(8,128)(2,1)S(1)}, f16[28,8,128]{2,1,0:T(8,128)(2,1)S(1)}, u32[]{:S(2)}, u32[]{:S(2)}) collective-permute-start(f16[28,8,128]{2,1,0:T(8,128)(2,1)S(1)} %get-tuple-element.15), channel_id=1, source_target_pairs={{0,8},{2,10},{4,12},{6,14},{8,0},{10,2},{12,4},{14,6},{16,24},{18,... | collective-permute-start | bytes 172040 | tf_op jit(solution)/shard_map/ppermute | solution.py:146
  35.9 6.0 %collective-permute-start.8 = (f16[28,8,128]{2,1,0:T(8,128)(2,1)S(1)}, f16[28,8,128]{2,1,0:T(8,128)(2,1)S(1)}, u32[]{:S(2)}, u32[]{:S(2)}) collective-permute-start(f16[28,8,128]{2,1,0:T(8,128)(2,1)S(1)} %get-tuple-element.16), channel_id=1, source_target_pairs={{0,24},{2,26},{4,28},{6,30},{8,16},{10,18},{12,20},{14,22},{16,8},... | collective-permute-start | bytes 172040 | tf_op jit(solution)/shard_map/ppermute | solution.py:146
  42.2 6.0 %collective-permute-start.11 = (f16[28,8,128]{2,1,0:T(8,128)(2,1)S(1)}, f16[28,8,128]{2,1,0:T(8,128)(2,1)S(1)}, u32[]{:S(2)}, u32[]{:S(2)}) collective-permute-start(f16[28,8,128]{2,1,0:T(8,128)(2,1)S(1)} %fusion.10), channel_id=1, source_target_pairs={{0,24},{2,26},{4,28},{6,30},{8,16},{10,18},{12,20},{14,22},{16,8},... | collective-permute-start | bytes 172040 | tf_op jit(solution)/shard_map/ppermute | solution.py:146
  43.2 5.1 %collective-permute-start.10 = (f16[28,8,128]{2,1,0:T(8,128)(2,1)S(1)}, f16[28,8,128]{2,1,0:T(8,128)(2,1)S(1)}, u32[]{:S(2)}, u32[]{:S(2)}) collective-permute-start(f16[28,8,128]{2,1,0:T(8,128)(2,1)S(1)} %fusion.10), channel_id=1, source_target_pairs={{0,8},{2,10},{4,12},{6,14},{8,0},{10,2},{12,4},{14,6},{16,24},{18,... | collective-permute-start | bytes 172040 | tf_op jit(solution)/shard_map/ppermute | solution.py:146
  43.3 5.5 %collective-permute-start.9 = (f16[28,8,128]{2,1,0:T(8,128)(2,1)S(1)}, f16[28,8,128]{2,1,0:T(8,128)(2,1)S(1)}, u32[]{:S(2)}, u32[]{:S(2)}) collective-permute-start(f16[28,8,128]{2,1,0:T(8,128)(2,1)S(1)} %fusion.10), channel_id=1, source_target_pairs={{0,16},{2,18},{4,20},{6,22},{8,24},{10,26},{12,28},{14,30},{16,0},... | collective-permute-start | bytes 172040 | tf_op jit(solution)/shard_map/ppermute | solution.py:146
  49.0 6.1 %collective-permute-start.12 = (f16[28,4,8,128]{3,2,1,0:T(8,128)(2,1)S(1)}, f16[28,4,8,128]{3,2,1,0:T(8,128)(2,1)S(1)}, u32[]{:S(2)}, u32[]{:S(2)}) collective-permute-start(f16[28,4,8,128]{3,2,1,0:T(8,128)(2,1)S(1)} %select_select_fusion), channel_id=1, source_target_pairs={{0,4},{2,6},{4,0},{6,2},{8,12},{10,14},{12,8},{14,10},{16,20},{18,... | collective-permute-start | bytes 688136 | tf_op jit(solution)/shard_map/ppermute | solution.py:146
  50.1 11.6 %collective-permute-start.3 = (f32[2,16,32,128]{3,2,1,0:T(8,128)S(1)}, f32[2,16,32,128]{3,2,1,0:T(8,128)S(1)}, u32[]{:S(2)}, u32[]{:S(2)}) collective-permute-start(f32[2,16,32,128]{3,2,1,0:T(8,128)S(1)} %slice_bitcast_fusion), channel_id=1, source_target_pairs={{0,1},{1,0},{2,3},{3,2},{4,5},{5,4},{6,7},{7,6},{8,9},{9,8},{10,11... | collective-permute-start | bytes 1572872 | tf_op jit(solution)/shard_map/ppermute | solution.py:146
  51.9 3.5 %collective-permute-start.2 = (f32[16,16,128]{2,1,0:T(8,128)S(1)}, f32[16,16,128]{2,1,0:T(8,128)S(1)}, u32[]{:S(2)}, u32[]{:S(2)}) collective-permute-start(f32[16,16,128]{2,1,0:T(8,128)S(1)} %get-tuple-element.12), channel_id=1, source_target_pairs={{0,2},{2,4},{4,6},{6,8},{8,10},{10,12},{12,14},{14,16},{16,18},{18... | collective-permute-start | bytes 393224 | tf_op jit(solution)/shard_map/ppermute | solution.py:151
  55.4 7.2 %collective-permute-start.13 = (f16[28,2,4,8,128]{4,3,2,1,0:T(8,128)(2,1)S(1)}, f16[28,2,4,8,128]{4,3,2,1,0:T(8,128)(2,1)S(1)}, u32[]{:S(2)}, u32[]{:S(2)}) collective-permute-start(f16[28,2,4,8,128]{4,3,2,1,0:T(8,128)(2,1)S(1)} %broadcast_select_fusion), channel_id=1, source_target_pairs={{0,2},{2,0},{4,6},{6,4},{8,10},{10,8},{12,14},{14,12},{16,18},{18,... | collective-permute-start | bytes 1376264 | tf_op jit(solution)/shard_map/ppermute | solution.py:146

commit v2 on v1

v2 whole, which is shorter than its diff:
```python
import functools

import jax
import jax.numpy as jnp
from jax import lax
from jax.experimental import pallas as pl
from jax.experimental.pallas import tpu as pltpu
from jax.sharding import PartitionSpec as P

F32, BF16, F16 = jnp.float32, jnp.bfloat16, jnp.float16
TOP = 15.0
TAPS = 27


def tap(a, b, c):
    return (a * 3 + b) * 3 + c


def uses(parity):
    return ((1, 0),) if parity == 0 else ((2, 0), (0, 1))


def shift_index(dx, dy, dz):
    return (dx * 2 + dy) * 2 + dz


def dot(x, y, dims):
    return lax.dot_general(x, y, (dims, ((), ())), preferred_element_type=F32)


def wide_weights(w_ref, a, b):
    return jnp.concatenate([w_ref[tap(a, b, 1)], w_ref[tap(a, b, 2)]], axis=1)


def shift_grads(place, half, blocks, levels, shifted, store):
    for level, (dx, ref) in enumerate(levels):
        rows, oz, cout = ref.shape
        last = lax.broadcasted_iota(jnp.int32, (rows, oz, cout), 1) == oz - 1
        grad = ref[...].astype(F32)
        moved = jnp.where(last, 0.0, pltpu.roll(grad, oz - 1, 1))
        for dz, value in ((0, grad), (1, moved)):
            shifted[level * 2 + dz, :rows] = value
            shifted[level * 2 + dz, rows:] = jnp.zeros((1, oz, cout), F32)
    cells = half * oz
    for level, (dx, ref) in enumerate(levels):
        for dy in range(2):
            for dz in range(2):
                for block in range(blocks):
                    first = place[block] * half + dy
                    piece = shifted[level * 2 + dz, pl.ds(first, half)].reshape(cells, cout)
                    store(shift_index(dx, dy, dz), pl.ds(block * cells, cells), piece)


def turn(place, half, blocks, size, g_ref, gt_ref, shifted, turned):
    cout = g_ref.shape[2]
    own = place[blocks]

    def store(index, span, piece):
        turned[...] = piece.T
        order = [turned[pl.ds((own ^ i) * size, size)] for i in range(cout // size)]
        gt_ref[index, :, span] = jnp.concatenate(order, axis=0).astype(BF16)

    shift_grads(place, half, blocks, ((0, g_ref),), shifted, store)


def split_classes(volume_ref, class_ref, wide):
    _, rows, depth, cin = volume_ref.shape
    oz = depth // 2
    wide[...] = volume_ref[...].astype(F32)
    for p in range(2):
        for row in range(rows):
            at = (row // 2) * oz
            for q in range(2):
                piece = wide[p, row, pl.ds(q, oz, stride=2), :]
                class_ref[p * 2 + row % 2, at : at + oz, q * cin : (q + 1) * cin] = piece.astype(BF16)


def own_kernel(blocks, half, size, place, g_ref, volume_ref, gt_ref, class_ref, shifted, turned, wide):
    split_classes(volume_ref, class_ref, wide)
    turn(place, half, blocks, size, g_ref, gt_ref, shifted, turned)


def above_kernel(blocks, half, size, place, g_ref, gt_ref, shifted, turned):
    turn(place, half, blocks, size, g_ref, gt_ref, shifted, turned)


def input_kernel(blocks, half, place, g_ref, above_ref, w_ref, *refs):
    part_refs, (shifted, cells_of) = refs[:blocks], refs[blocks:]
    oz = g_ref.shape[1]

    def store(index, span, piece):
        cells_of[index, span] = piece.astype(BF16)

    shift_grads(place, half, blocks, ((0, g_ref), (1, above_ref)), shifted, store)
    cin = w_ref.shape[2]
    for p in range(2):
        for r in range(2):
            total, odd = None, None
            for a, dx in uses(p):
                for b, dy in uses(r):
                    both = dot(cells_of[shift_index(dx, dy, 0)], wide_weights(w_ref, a, b), ((1,), (0,)))
                    late = dot(cells_of[shift_index(dx, dy, 1)], w_ref[tap(a, b, 0)], ((1,), (0,)))
                    total = both if total is None else total + both
                    odd = late if odd is None else odd + late
            parts = (total[:, :cin], total[:, cin:] + odd)
            for block in range(blocks):
                for j in range(half):
                    at = (block * half + j) * oz
                    for q in range(2):
                        part_refs[block][p, 2 * j + r, pl.ds(q, oz, stride=2), :] = parts[q][at : at + oz]


def weight_kernel(blocks, *refs):
    own_ref, others = refs[0], refs[1:blocks]
    gt0_ref, gt1_ref, near_ref, mid_ref, far_ref, class_ref, wide = refs[blocks:]
    quarter, cin = near_ref.shape[1:]
    cells = own_ref.shape[1]

    def store(index, term):
        near_ref[index] = term[:quarter]
        mid_ref[index] = term[quarter : 2 * quarter]
        far_ref[index] = term[2 * quarter :]

    class_ref[:, :cells] = own_ref[...]
    for block, ref in enumerate(others):
        split_classes(ref, class_ref.at[:, pl.ds((block + 1) * cells, cells)], wide)
    largest = None
    for p in range(2):
        for r in range(2):
            patch = class_ref[p * 2 + r]
            for a, dx in uses(p):
                gt_ref = (gt0_ref, gt1_ref)[dx]
                for b, dy in uses(r):
                    both = dot(gt_ref[shift_index(0, dy, 0)], patch, ((1,), (0,)))
                    late = dot(gt_ref[shift_index(0, dy, 1)], patch[:, cin:], ((1,), (0,)))
                    for c, term in ((0, late), (1, both[:, :cin]), (2, both[:, cin:])):
                        store(tap(a, b, c), term)
                        size = jnp.abs(term)
                        largest = size if largest is None else jnp.maximum(largest, size)
    store(TAPS, jnp.maximum(jnp.floor(jnp.log2(largest)) + 1.0, -100.0))


def feature_kernel(blocks, half, place, class_ref, w_ref, own_ref, send_ref, total):
    rows, oz, cout = own_ref.shape
    cin = w_ref.shape[2]
    first_cell = lax.broadcasted_iota(jnp.int32, (rows, oz, cout), 1) == 0
    total[...] = jnp.zeros_like(total)
    for dx in range(2):
        for dy in range(2):
            level, late = None, None
            for p in range(2):
                for a, shift_x in uses(p):
                    for r in range(2):
                        for b, shift_y in uses(r):
                            if (shift_x, shift_y) != (dx, dy):
                                continue
                            patch = class_ref[p * 2 + r]
                            both = dot(patch, wide_weights(w_ref, a, b), ((1,), (1,)))
                            odd = dot(patch[:, cin:], w_ref[tap(a, b, 0)], ((1,), (1,)))
                            level = both if level is None else level + both
                            late = odd if late is None else late + odd
            late = late.reshape(rows, oz, cout)
            level = level.reshape(rows, oz, cout) + jnp.where(first_cell, 0.0, pltpu.roll(late, 1, 1))
            for block in range(blocks):
                where = pl.ds(place[block] * half + dy, half)
                total[dx, where] = total[dx, where] + level[block * half : (block + 1) * half]
    own_ref[...] = total[0, :rows]
    send_ref[...] = total[1, :rows]


def call(kernel, out_shape, arguments, scratch=(), placed=False, flops=0):
    vmem = pl.BlockSpec(memory_space=pltpu.VMEM)
    smem = pl.BlockSpec(memory_space=pltpu.SMEM)
    size = sum(x.size * x.dtype.itemsize for x in list(arguments) + list(out_shape))
    return pl.pallas_call(
        kernel,
        out_shape=out_shape,
        in_specs=[smem if placed and i == 0 else vmem for i in range(len(arguments))],
        out_specs=[vmem] * len(out_shape),
        scratch_shapes=list(scratch),
        compiler_params=pltpu.CompilerParams(vmem_limit_bytes=8 * 1024 * 1024),
        cost_estimate=pl.CostEstimate(flops=flops, bytes_accessed=size, transcendentals=0),
    )(*arguments)


def swap(x, axis, bits):
    peers = lax.axis_size(axis)
    return lax.ppermute(x, axis, [(i, i ^ bits) for i in range(peers)])


def move(x, axis, by):
    peers = lax.axis_size(axis)
    return lax.ppermute(x, axis, [(i, i + by) for i in range(peers) if 0 <= i + by < peers])


def is_level(x):
    return lax.broadcasted_iota(jnp.int32, x.shape, 0) == TAPS


def encode(x):
    return jnp.where(is_level(x), x, x * jnp.exp2(TOP - x[TAPS:])).astype(F16)


def decode(x):
    return jnp.where(is_level(x), x.astype(F32), x.astype(F32) * jnp.exp2(x[TAPS:].astype(F32) - TOP))


def add(x, y):
    return jnp.where(is_level(x), jnp.maximum(x, y) + 1.0, x + y)


def arrange(pieces, mine):
    shape = pieces[0].shape[:1] + (len(pieces),) + pieces[0].shape[1:]
    source = lax.broadcasted_iota(jnp.int32, shape, 1) ^ mine
    out = jnp.broadcast_to(pieces[-1][:, None], shape)
    for q in range(len(pieces) - 1):
        out = jnp.where(source == q, jnp.broadcast_to(pieces[q][:, None], shape), out)
    return out


def sum_over_space(near, mid, far, where, factor, beside):
    core, x, z, nz = where
    quarter = near.shape[1]
    got = beside("core", swap(encode(far), "space", 1))
    sent = encode(add(mid, decode(got[:, quarter:])))
    near = add(near, decode(got[:, :quarter]))
    got = beside("x", swap(sent, "space", 2))
    total = add(near, decode(got)).reshape(TAPS + 1, nz, quarter // nz, near.shape[2])
    got = [swap(encode(total[:, q]), "space", 4 * q) for q in range(1, nz)]
    total = total[:, 0]
    for piece in got:
        total = add(total, decode(piece))
    total = beside("z", encode(jnp.where(is_level(total), total, total * factor)))
    total = arrange([total] + [swap(total, "space", 4 * q) for q in range(1, nz)], z)
    total = beside("back", total)
    across = beside("end", swap(total, "space", 2))
    cin = near.shape[2]
    out = jnp.zeros((TAPS, 2, 2, nz, quarter // nz, cin), F32)
    pieces = ((core, x, total), (core, 1 - x, across))
    pieces += tuple((1 - core, at, swap(piece, "space", 1)) for _, at, piece in pieces)
    for half, at, piece in pieces:
        out = lax.dynamic_update_slice(out, decode(piece)[:TAPS][:, None, None], (0, half, at, 0, 0, 0))
    return out.reshape(3, 3, 3, 4 * quarter, cin)


def on_device(volume, kernel, out_grad):
    planes, rows, depth, cin = volume.shape
    cout = kernel.shape[3]
    filt = lax.axis_size("filt")
    half, oz = rows // 2, depth // 2
    oy = half * filt
    cells = oy * oz
    mine = lax.axis_index("filt")
    if filt == 2:
        volumes = [volume, swap(volume, "filt", 1)]
        place = [mine, 1 - mine]
    else:
        gathered = lax.all_gather(volume, "filt", axis=0, tiled=False)
        volumes = [gathered[i] for i in range(filt)]
        place = list(range(filt))
    peers = lax.axis_size("space")
    index, nz = lax.axis_index("space"), peers // 4
    core, x, z = index & 1, (index >> 1) & 1, index >> 2
    place = jnp.stack([jnp.asarray(i, jnp.int32) for i in place + [(core * 2 + x) * nz + z]])
    above = move(out_grad, "space", -1)
    weights = kernel.reshape(TAPS, cout, cin)
    flops = 2 * TAPS * cells * cin * cout
    turn_scratch = [pltpu.VMEM((2, oy + 1, oz, cout), F32), pltpu.VMEM((cout, half * oz), F32)]
    own_grads, own_classes = call(
        functools.partial(own_kernel, filt, half, cout // peers),
        [
            jax.ShapeDtypeStruct((4, cout, cells), BF16),
            jax.ShapeDtypeStruct((4, half * oz, 2 * cin), BF16),
        ],
        (place, out_grad[0], volumes[0]),
        turn_scratch + [pltpu.VMEM(volume.shape, F32)],
        placed=True,
    )
    (above_grads,) = call(
        functools.partial(above_kernel, filt, half, cout // peers),
        [jax.ShapeDtypeStruct((4, cout, cells), BF16)],
        (place, above[0]),
        turn_scratch,
        placed=True,
    )
    near, mid, far, classes = call(
        functools.partial(weight_kernel, filt),
        [
            jax.ShapeDtypeStruct((TAPS + 1, cout // 4, cin), F32),
            jax.ShapeDtypeStruct((TAPS + 1, cout // 4, cin), F32),
            jax.ShapeDtypeStruct((TAPS + 1, cout // 2, cin), F32),
            jax.ShapeDtypeStruct((4, cells, 2 * cin), BF16),
        ],
        (own_classes, *volumes[1:], own_grads, above_grads),
        [pltpu.VMEM(volume.shape, F32)],
        flops=flops,
    )
    held = {}

    def beside(stage, value):
        if stage == "core":
            value, gradient, upper = lax.optimization_barrier((value, out_grad, above))
            held["part"] = call(
                functools.partial(input_kernel, filt, half),
                [jax.ShapeDtypeStruct(volume.shape, F32)] * filt,
                (place, gradient[0], upper[0], weights),
                [pltpu.VMEM((4, oy + 1, oz, cout), F32), pltpu.VMEM((8, cells, cout), BF16)],
                placed=True,
                flops=flops,
            )
            held["own"], held["send"] = call(
                functools.partial(feature_kernel, filt, half),
                [jax.ShapeDtypeStruct((oy, oz, cout), F32)] * 2,
                (place, classes, weights),
                [pltpu.VMEM((2, oy + 1, oz, cout), F32)],
                placed=True,
                flops=flops,
            )
            if filt == 2:
                held["in"] = swap(held["part"][1], "filt", 1)
            held["below"] = move(held["send"], "space", 1)
        if stage == "x":
            value, *held["part"], held["own"], held["send"] = lax.optimization_barrier(
                (value, *held["part"], held["own"], held["send"])
            )
        if stage == "end":
            value, held["below"] = lax.optimization_barrier((value, held["below"]))
        if stage == "back" and filt == 2:
            value, held["in"] = lax.optimization_barrier((value, held["in"]))
        return value

    factor = float(peers * cells) ** (-0.5)
    kernel_grad = sum_over_space(near, mid, far, (core, x, z, nz), factor, beside)
    features = (held["own"] + held["below"]).astype(BF16)[None]
    if filt == 2:
        gradient = (held["part"][0] + held["in"]).astype(BF16)
    else:
        gradient = lax.psum_scatter(jnp.stack(held["part"]), "filt", scatter_dimension=0).astype(BF16)
    return features, gradient, kernel_grad


def solution(mesh):
    return jax.shard_map(
        on_device,
        mesh=mesh,
        in_specs=(
            P("space", "filt", None, None),
            P(None, None, None, "filt", None),
            P("space", None, None, "filt"),
        ),
        out_specs=(
            P("space", None, None, "filt"),
            P("space", "filt", None, None),
            P(None, None, None, "filt", None),
        ),
        check_vma=False,
    )
```

time: 64.9 us -> 51.1 us (0.79)
  waiting for transfers between devices: 25.3 us -> 18.8 us
  other arithmetic: 9.12 us -> 3.46 us
  local copies, waits for them, and re-layouts: 5.53 us -> 3.21 us
  Pallas kernels: 2.93 us -> 4.59 us
  starting transfers between devices: 20.7 us -> 19.9 us
    ppermute x12 -> x13, waiting for transfers between devices: 23.4 us -> 18.8 us  [swap(): return lax.ppermute(x, axis, [(i, i ^ bits) for i in range(peers)])]
    unnamed x14 -> x10, local copies, waits for them, and re-layouts: 5.5 us -> 3.01 us
    select_n x2 -> x1, other arithmetic: 2.5 us -> 0.17 us  [add(): return jnp.where(is_level(x), jnp.maximum(x, y) + 1.0, x + y)]
    ppermute x2, waiting for transfers between devices: 1.97 us -> 0.01 us  [move(): lax.ppermute(x, axis, [(i, i + by) for i in range(peers) if 0 <= i + by <...]
    pallas_call x3 -> x5, Pallas kernels: 2.93 us -> 4.59 us  [call(): pl.pallas_call(kernel, out_shape=out_shape, in_specs=[smem if placed and...]
    convert_element_type x7 -> x1, other arithmetic: 2.41 us -> 0.79 us  [on_device(): gradient = (held['part'][0] + held['in']).astype(BF16)]
    select_n x2 -> x1, other arithmetic: 1.63 us -> 0.16 us  [sum_over_space(): jnp.where(is_level(total), total, total * factor)]
    convert_element_type x4, other arithmetic: 1.29 us -> 0.51 us  [encode(): return jnp.where(is_level(x), x, x * jnp.exp2(TOP - x[TAPS:])).astype(F16)]
  transfers between devices with their start and end apart: 14 -> 15, of which waited for: 9 -> 9; matrix products, arithmetic and copies ran while one was open for 3% -> 5% of each run, Pallas kernels for 4% -> 8%
where the time goes in v2:
time: 51.1 us; the launch traced here: 50.9 us
  starting transfers between devices  19.9 us (39%)
  waiting for transfers between devices  18.8 us (37%)
  Pallas kernels  4.59 us (9%)
  other arithmetic  3.46 us (7%)
  local copies, waits for them, and re-layouts  3.21 us (6%)
  between operations  0.92 us (2%)
    ppermute x13, waiting for transfers between devices, swap(): return lax.ppermute(x, axis, [(i, i ^ bits) for i in range(peers)])  18.8 us
    ppermute x13, starting transfers between devices, swap(): return lax.ppermute(x, axis, [(i, i ^ bits) for i in range(peers)])  17.3 us
    pallas_call x5, Pallas kernels, call(): pl.pallas_call(kernel, out_shape=out_shape, in_specs=[smem if placed and...  4.59 us
    unnamed x10, local copies, waits for them, and re-layouts  3.01 us
    ppermute x2, starting transfers between devices, move(): lax.ppermute(x, axis, [(i, i + by) for i in range(peers) if 0 <= i + by <...  2.57 us
  transfers between devices with their start and end apart: 15, of which 9 were waited for; matrix products, arithmetic and copies ran while one was open for 5% of the time, Pallas kernels for 8%

profile of v2, /device:TPU:0, one launch (start us, length us, event | category | flops | bytes accessed | tf_op | source)
XLA Modules:
  0.0 50.9 jit_solution(3257532606378602281)
XLA Ops:
  0.6 3.0 %collective-permute-start = (bf16[2,16,32,128]{3,2,1,0:T(8,128)(2,1)}, bf16[2,16,32,128]{3,2,1,0:T(8,128)(2,1)S(1)}, u32[]{:S(2)}, u32[]{:S(2)}) collective-permute-start(bf16[2,16,32,128]{3,2,1,0:T(8,128)(2,1)} %volume_ref.1), channel_id=1, source_target_pairs={{0,1},{1,0},{2,3},{3,2},{4,5},{5,4},{6,7},{7,6},{8,9},{9,8},{10,11... | collective-permute-start | bytes 786440 | tf_op jit(solution)/shard_map/ppermute | solution.py:188
  3.7 1.3 %collective-permute-start.1 = (bf16[1,16,16,128]{3,2,1,0:T(8,128)(2,1)}, bf16[1,16,16,128]{3,2,1,0:T(8,128)(2,1)S(1)}, u32[]{:S(2)}, u32[]{:S(2)}) collective-permute-start(bf16[1,16,16,128]{3,2,1,0:T(8,128)(2,1)} %param.5), channel_id=1, source_target_pairs={{2,0},{4,2},{6,4},{8,6},{10,8},{12,10},{14,12},{16,14},{18,16},{20... | collective-permute-start | bytes 196616 | tf_op jit(solution)/shard_map/ppermute | solution.py:193
  5.0 0.1 pad_add_fusion.place
  5.0 0.8 %copy-done.1 = bf16[1,16,16,128]{3,2,1,0:T(8,128)(2,1)S(1)} copy-done((bf16[1,16,16,128]{3,2,1,0:T(8,128)(2,1)S(1)}, bf16[1,16,16,128]{3,2,1,0:T(8,128)(2,1)}, u32[]{:S(2)}) %copy-start.1) | copy-done | bytes 65560
  5.9 0.9 %copy-done.3 = bf16[2,16,32,128]{3,2,1,0:T(8,128)(2,1)S(1)} copy-done((bf16[2,16,32,128]{3,2,1,0:T(8,128)(2,1)S(1)}, bf16[2,16,32,128]{3,2,1,0:T(8,128)(2,1)}, u32[]{:S(2)}) %copy-start.3) | copy-done | bytes 262168
  6.8 0.9 %shard_map.58 = (bf16[4,128,256]{2,1,0:T(8,128)(2,1)S(1)}, bf16[4,128,256]{2,1,0:T(8,128)(2,1)S(1)}) custom-call(s32[3]{0:T(128)S(1)} %pad_add_fusion.place, bf16[16,16,128]{2,1,0:T(8,128)(2,1)S(1)} %bitcast.92, bf16[2,16,32,128]{3,2,1,0:T(8,128)(2,1)S(1)} %copy-done.3), custom_call_target="tpu_custom_call" | custom-call | bytes 851980 | tf_op jit(solution)/shard_map/pallas_call | solution.py:175
  7.7 0.8 %shard_map.59.refs_3_ = bf16[4,128,256]{2,1,0:T(8,128)(2,1)S(1)} custom-call(s32[3]{0:T(128)S(1)} %pad_add_fusion.place, bf16[16,16,128]{2,1,0:T(8,128)(2,1)S(1)} %bitcast.94), custom_call_target="tpu_custom_call" | custom-call | bytes 327692 | tf_op jit(solution)/shard_map/pallas_call | solution.py:175
  8.6 1.6 %collective-permute-done.refs_1_ = bf16[2,16,32,128]{3,2,1,0:T(8,128)(2,1)S(1)} collective-permute-done((bf16[2,16,32,128]{3,2,1,0:T(8,128)(2,1)}, bf16[2,16,32,128]{3,2,1,0:T(8,128)(2,1)S(1)}, u32[]{:S(2)}, u32[]{:S(2)}) %collective-permute-start) | collective-permute-done | bytes 262176 | tf_op jit(solution)/shard_map/ppermute | solution.py:188
  10.2 0.5 %shard_map.60 = (f32[28,32,128]{2,1,0:T(8,128)S(1)}, f32[28,32,128]{2,1,0:T(8,128)S(1)}, f32[28,64,128]{2,1,0:T(8,128)S(1)}, bf16[4,256,256]{2,1,0:T(8,128)(2,1)S(1)}) custom-call(bf16[4,128,256]{2,1,0:T(8,128)(2,1)S(1)} %get-tuple-element.23.refs_0_, bf16[2,16,32,128]{3,2,1,0:T(8,128)(2,1)S(1)} %collective-permute-done.refs_1_, ...), custom_call_target="tpu_custom_call" | custom-call | flops 226492416 | bytes 3407872 | tf_op jit(solution)/shard_map/pallas_call | solution.py:175
  10.7 0.2 fusion
  10.9 0.3 collective-permute-start.2
  11.3 1.5 %collective-permute-done.2 = f16[28,64,128]{2,1,0:T(8,128)(2,1)S(1)} collective-permute-done((f16[28,64,128]{2,1,0:T(8,128)(2,1)S(1)}, f16[28,64,128]{2,1,0:T(8,128)(2,1)S(1)}, u32[]{:S(2)}, u32[]{:S(2)}) %collective-permute-start.2) | collective-permute-done | bytes 458784 | tf_op jit(solution)/shard_map/ppermute | solution.py:188
  12.8 0.2 add_select_fusion
  13.0 0.1 fusion.1
  13.1 1.8 %collective-permute-start.3 = (f16[28,32,128]{2,1,0:T(8,128)(2,1)S(1)}, f16[28,32,128]{2,1,0:T(8,128)(2,1)S(1)}, u32[]{:S(2)}, u32[]{:S(2)}) collective-permute-start(f16[28,32,128]{2,1,0:T(8,128)(2,1)S(1)} %fusion.1), channel_id=1, source_target_pairs={{0,4},{2,6},{4,0},{6,2},{8,12},{10,14},{12,8},{14,10},{16,20},{18,... | collective-permute-start | bytes 688136 | tf_op jit(solution)/shard_map/ppermute | solution.py:188
  14.9 1.2 %shard_map.62 = (f32[16,16,128]{2,1,0:T(8,128)S(1)}, f32[16,16,128]{2,1,0:T(8,128)S(1)}) custom-call(s32[3]{0:T(128)S(1)} %pad_add_fusion.place, bf16[4,256,256]{2,1,0:T(8,128)(2,1)S(1)} %get-tuple-element.32.class_ref, bf16[27,128,128]{2,1,0:T(8,128)(2,1)S(1)} %bitcast.90), custom_call_target="tpu_custom_call" | custom-call | flops 226492416 | bytes 1671180 | tf_op jit(solution)/shard_map/pallas_call | solution.py:175
  16.1 1.2 %shard_map.61 = (f32[2,16,32,128]{3,2,1,0:T(8,128)S(1)}, f32[2,16,32,128]{3,2,1,0:T(8,128)S(1)}) custom-call(s32[3]{0:T(128)S(1)} %pad_add_fusion.place, bf16[16,16,128]{2,1,0:T(8,128)(2,1)S(1)} %bitcast.93, bf16[16,16,128]{2,1,0:T(8,128)(2,1)S(1)} %bitcast.95, bf16[27,128,128]{2,1,0:T(8,128)(2,1)S(1)} %bitcast.91), custom_call_target="tpu_custom_call" | custom-call | flops 226492416 | bytes 2064396 | tf_op jit(solution)/shard_map/pallas_call | solution.py:175
  17.3 3.7 %collective-permute-done.3 = f16[28,32,128]{2,1,0:T(8,128)(2,1)S(1)} collective-permute-done((f16[28,32,128]{2,1,0:T(8,128)(2,1)S(1)}, f16[28,32,128]{2,1,0:T(8,128)(2,1)S(1)}, u32[]{:S(2)}, u32[]{:S(2)}) %collective-permute-start.3) | collective-permute-done | bytes 229408 | tf_op jit(solution)/shard_map/ppermute | solution.py:188
  21.1 0.3 select_bitcast_fusion
  21.4 0.1 fusion.10
  21.5 3.7 %collective-permute-start.6 = (f16[28,8,128]{2,1,0:T(8,128)(2,1)S(1)}, f16[28,8,128]{2,1,0:T(8,128)(2,1)S(1)}, u32[]{:S(2)}, u32[]{:S(2)}) collective-permute-start(f16[28,8,128]{2,1,0:T(8,128)(2,1)S(1)} %get-tuple-element.44), channel_id=1, source_target_pairs={{0,24},{2,26},{4,28},{6,30},{8,16},{10,18},{12,20},{14,22},{16,8},... | collective-permute-start | bytes 172040 | tf_op jit(solution)/shard_map/ppermute | solution.py:188
  25.2 1.5 %collective-permute-start.10 = (f32[2,16,32,128]{3,2,1,0:T(8,128)S(1)}, f32[2,16,32,128]{3,2,1,0:T(8,128)S(1)}, u32[]{:S(2)}, u32[]{:S(2)}) collective-permute-start(f32[2,16,32,128]{3,2,1,0:T(8,128)S(1)} %get-tuple-element.31), channel_id=1, source_target_pairs={{0,1},{1,0},{2,3},{3,2},{4,5},{5,4},{6,7},{7,6},{8,9},{9,8},{10,11... | collective-permute-start | bytes 1572872 | tf_op jit(solution)/shard_map/ppermute | solution.py:188
  26.7 0.8 %collective-permute-start.4 = (f16[28,8,128]{2,1,0:T(8,128)(2,1)S(1)}, f16[28,8,128]{2,1,0:T(8,128)(2,1)S(1)}, u32[]{:S(2)}, u32[]{:S(2)}) collective-permute-start(f16[28,8,128]{2,1,0:T(8,128)(2,1)S(1)} %get-tuple-element.43), channel_id=1, source_target_pairs={{0,8},{2,10},{4,12},{6,14},{8,0},{10,2},{12,4},{14,6},{16,24},{18,... | collective-permute-start | bytes 172040 | tf_op jit(solution)/shard_map/ppermute | solution.py:188
  27.5 0.0 collective-permute-done.6
  27.5 4.4 %collective-permute-done.5 = f16[28,8,128]{2,1,0:T(8,128)(2,1)S(1)} collective-permute-done((f16[28,8,128]{2,1,0:T(8,128)(2,1)S(1)}, f16[28,8,128]{2,1,0:T(8,128)(2,1)S(1)}, u32[]{:S(2)}, u32[]{:S(2)}) %collective-permute-start.5) | collective-permute-done | bytes 57376 | tf_op jit(solution)/shard_map/ppermute | solution.py:188
  31.9 0.2 multiply_select_fusion.10
  32.1 0.1 fusion.13
  32.2 1.6 %collective-permute-start.9 = (f16[28,8,128]{2,1,0:T(8,128)(2,1)S(1)}, f16[28,8,128]{2,1,0:T(8,128)(2,1)S(1)}, u32[]{:S(2)}, u32[]{:S(2)}) collective-permute-start(f16[28,8,128]{2,1,0:T(8,128)(2,1)S(1)} %fusion.13), channel_id=1, source_target_pairs={{0,24},{2,26},{4,28},{6,30},{8,16},{10,18},{12,20},{14,22},{16,8},... | collective-permute-start | bytes 172040 | tf_op jit(solution)/shard_map/ppermute | solution.py:188
  33.8 0.9 %collective-permute-start.8 = (f16[28,8,128]{2,1,0:T(8,128)(2,1)S(1)}, f16[28,8,128]{2,1,0:T(8,128)(2,1)S(1)}, u32[]{:S(2)}, u32[]{:S(2)}) collective-permute-start(f16[28,8,128]{2,1,0:T(8,128)(2,1)S(1)} %fusion.13), channel_id=1, source_target_pairs={{0,8},{2,10},{4,12},{6,14},{8,0},{10,2},{12,4},{14,6},{16,24},{18,... | collective-permute-start | bytes 172040 | tf_op jit(solution)/shard_map/ppermute | solution.py:188
  34.7 1.9 %collective-permute-start.7 = (f16[28,8,128]{2,1,0:T(8,128)(2,1)S(1)}, f16[28,8,128]{2,1,0:T(8,128)(2,1)S(1)}, u32[]{:S(2)}, u32[]{:S(2)}) collective-permute-start(f16[28,8,128]{2,1,0:T(8,128)(2,1)S(1)} %fusion.13), channel_id=1, source_target_pairs={{0,16},{2,18},{4,20},{6,22},{8,24},{10,26},{12,28},{14,30},{16,0},... | collective-permute-start | bytes 172040 | tf_op jit(solution)/shard_map/ppermute | solution.py:188
  36.6 1.3 %collective-permute-start.12 = (f32[16,16,128]{2,1,0:T(8,128)S(1)}, f32[16,16,128]{2,1,0:T(8,128)S(1)}, u32[]{:S(2)}, u32[]{:S(2)}) collective-permute-start(f32[16,16,128]{2,1,0:T(8,128)S(1)} %get-tuple-element.34), channel_id=1, source_target_pairs={{0,2},{2,4},{4,6},{6,8},{8,10},{10,12},{12,14},{14,16},{16,18},{18... | collective-permute-start | bytes 393224 | tf_op jit(solution)/shard_map/ppermute | solution.py:193
  37.9 0.4 collective-permute-done.9
  38.4 0.2 collective-permute-done.8
  38.6 1.2 %collective-permute-done.7 = f16[28,8,128]{2,1,0:T(8,128)(2,1)S(1)} collective-permute-done((f16[28,8,128]{2,1,0:T(8,128)(2,1)S(1)}, f16[28,8,128]{2,1,0:T(8,128)(2,1)S(1)}, u32[]{:S(2)}, u32[]{:S(2)}) %collective-permute-start.7) | collective-permute-done | bytes 57376 | tf_op jit(solution)/shard_map/ppermute | solution.py:188
  39.8 0.2 select_select_fusion
  40.0 1.5 %collective-permute-start.11 = (f16[28,4,8,128]{3,2,1,0:T(8,128)(2,1)S(1)}, f16[28,4,8,128]{3,2,1,0:T(8,128)(2,1)S(1)}, u32[]{:S(2)}, u32[]{:S(2)}) collective-permute-start(f16[28,4,8,128]{3,2,1,0:T(8,128)(2,1)S(1)} %select_select_fusion), channel_id=1, source_target_pairs={{0,4},{2,6},{4,0},{6,2},{8,12},{10,14},{12,8},{14,10},{16,20},{18,... | collective-permute-start | bytes 688136 | tf_op jit(solution)/shard_map/ppermute | solution.py:188
  41.5 0.1 collective-permute-start.13
  41.6 0.8 %add_convert_fusion = bf16[2,16,32,128]{3,2,1,0:T(8,128)(2,1)} fusion(f32[2,16,32,128]{3,2,1,0:T(8,128)S(1)} %get-tuple-element.40, f32[2,16,32,128]{3,2,1,0:T(8,128)S(1)} %collective-permute-done.10), kind=kLoop, calls=%fused_computation.10 | loop fusion | flops 262144 | bytes 1310720 | tf_op jit(solution)/shard_map/convert_element_type | solution.py:336
  42.4 0.2 broadcast_in_dim.47
  42.6 0.1 fusion.3
  42.8 5.2 %collective-permute-done.11 = f16[28,4,8,128]{3,2,1,0:T(8,128)(2,1)S(1)} collective-permute-done((f16[28,4,8,128]{3,2,1,0:T(8,128)(2,1)S(1)}, f16[28,4,8,128]{3,2,1,0:T(8,128)(2,1)S(1)}, u32[]{:S(2)}, u32[]{:S(2)}) %collective-permute-start.11) | collective-permute-done | bytes 229408 | tf_op jit(solution)/shard_map/ppermute | solution.py:188
  48.0 0.1 collective-permute-start.14
  48.0 0.1 fusion.5
  48.2 0.1 fusion.7
  48.3 0.6 %fusion.14 = bf16[1,16,16,128]{3,2,1,0:T(8,128)(2,1)} fusion(f32[16,16,128]{2,1,0:T(8,128)S(1)} %get-tuple-element.35, f32[16,16,128]{2,1,0:T(8,128)S(1)} %collective-permute-done.12), kind=kLoop, calls=%fused_computation.40 | loop fusion | flops 65536 | bytes 327680 | tf_op jit(solution)/shard_map/broadcast_in_dim | solution.py:334
  49.0 0.5 %collective-permute-done.14 = f16[28,4,8,128]{3,2,1,0:T(8,128)(2,1)S(1)} collective-permute-done((f16[28,4,8,128]{3,2,1,0:T(8,128)(2,1)S(1)}, f16[28,4,8,128]{3,2,1,0:T(8,128)(2,1)S(1)}, u32[]{:S(2)}, u32[]{:S(2)}) %collective-permute-start.14) | collective-permute-done | bytes 229408 | tf_op jit(solution)/shard_map/ppermute | solution.py:188
  49.5 0.1 fusion.9
  49.7 1.2 %copy-done.4 = f32[27,2,2,4,8,128]{5,4,3,2,1,0:T(8,128)} copy-done((f32[27,2,2,4,8,128]{5,4,3,2,1,0:T(8,128)}, f32[27,2,2,4,8,128]{5,4,3,2,1,0:T(8,128)S(1)}, u32[]{:S(2)}) %copy-start.4) | copy-done | bytes 1769496
  (29 shorter events, 0.2 us)
Async XLA Ops:
  0.6 9.6 %collective-permute-start = (bf16[2,16,32,128]{3,2,1,0:T(8,128)(2,1)}, bf16[2,16,32,128]{3,2,1,0:T(8,128)(2,1)S(1)}, u32[]{:S(2)}, u32[]{:S(2)}) collective-permute-start(bf16[2,16,32,128]{3,2,1,0:T(8,128)(2,1)} %volume_ref.1), channel_id=1, source_target_pairs={{0,1},{1,0},{2,3},{3,2},{4,5},{5,4},{6,7},{7,6},{8,9},{9,8},{10,11... | collective-permute-start | bytes 786440 | tf_op jit(solution)/shard_map/ppermute | solution.py:188
  3.7 4.0 %collective-permute-start.1 = (bf16[1,16,16,128]{3,2,1,0:T(8,128)(2,1)}, bf16[1,16,16,128]{3,2,1,0:T(8,128)(2,1)S(1)}, u32[]{:S(2)}, u32[]{:S(2)}) collective-permute-start(bf16[1,16,16,128]{3,2,1,0:T(8,128)(2,1)} %param.5), channel_id=1, source_target_pairs={{2,0},{4,2},{6,4},{8,6},{10,8},{12,10},{14,12},{16,14},{18,16},{20... | collective-permute-start | bytes 196616 | tf_op jit(solution)/shard_map/ppermute | solution.py:193
  5.0 0.8 %copy-start.1 = (bf16[1,16,16,128]{3,2,1,0:T(8,128)(2,1)S(1)}, bf16[1,16,16,128]{3,2,1,0:T(8,128)(2,1)}, u32[]{:S(2)}) copy-start(bf16[1,16,16,128]{3,2,1,0:T(8,128)(2,1)} %param.5) | copy-start | bytes 196612
  5.9 0.9 %copy-start.3 = (bf16[2,16,32,128]{3,2,1,0:T(8,128)(2,1)S(1)}, bf16[2,16,32,128]{3,2,1,0:T(8,128)(2,1)}, u32[]{:S(2)}) copy-start(bf16[2,16,32,128]{3,2,1,0:T(8,128)(2,1)} %volume_ref.1) | copy-start | bytes 786436
  10.7 4.2 %copy-start = (bf16[3,3,3,128,128]{4,3,2,1,0:T(8,128)(2,1)S(1)}, bf16[3,3,3,128,128]{4,3,2,1,0:T(8,128)(2,1)}, u32[]{:S(2)}) copy-start(bf16[3,3,3,128,128]{4,3,2,1,0:T(8,128)(2,1)} %param.4) | copy-start | bytes 2654212
  10.9 5.2 %copy-start.2 = (bf16[1,16,16,128]{3,2,1,0:T(8,128)(2,1)S(1)}, bf16[1,16,16,128]{3,2,1,0:T(8,128)(2,1)}, u32[]{:S(2)}) copy-start(bf16[1,16,16,128]{3,2,1,0:T(8,128)(2,1)} %param.5) | copy-start | bytes 196612
  10.9 1.9 %collective-permute-start.2 = (f16[28,64,128]{2,1,0:T(8,128)(2,1)S(1)}, f16[28,64,128]{2,1,0:T(8,128)(2,1)S(1)}, u32[]{:S(2)}, u32[]{:S(2)}) collective-permute-start(f16[28,64,128]{2,1,0:T(8,128)(2,1)S(1)} %fusion), channel_id=1, source_target_pairs={{0,2},{2,0},{4,6},{6,4},{8,10},{10,8},{12,14},{14,12},{16,18},{18,... | collective-permute-start | bytes 1376264 | tf_op jit(solution)/shard_map/ppermute | solution.py:188
  13.1 7.9 %collective-permute-start.3 = (f16[28,32,128]{2,1,0:T(8,128)(2,1)S(1)}, f16[28,32,128]{2,1,0:T(8,128)(2,1)S(1)}, u32[]{:S(2)}, u32[]{:S(2)}) collective-permute-start(f16[28,32,128]{2,1,0:T(8,128)(2,1)S(1)} %fusion.1), channel_id=1, source_target_pairs={{0,4},{2,6},{4,0},{6,2},{8,12},{10,14},{12,8},{14,10},{16,20},{18,... | collective-permute-start | bytes 688136 | tf_op jit(solution)/shard_map/ppermute | solution.py:188
  21.5 6.0 %collective-permute-start.6 = (f16[28,8,128]{2,1,0:T(8,128)(2,1)S(1)}, f16[28,8,128]{2,1,0:T(8,128)(2,1)S(1)}, u32[]{:S(2)}, u32[]{:S(2)}) collective-permute-start(f16[28,8,128]{2,1,0:T(8,128)(2,1)S(1)} %get-tuple-element.44), channel_id=1, source_target_pairs={{0,24},{2,26},{4,28},{6,30},{8,16},{10,18},{12,20},{14,22},{16,8},... | collective-permute-start | bytes 172040 | tf_op jit(solution)/shard_map/ppermute | solution.py:188
  25.2 14.8 %collective-permute-start.10 = (f32[2,16,32,128]{3,2,1,0:T(8,128)S(1)}, f32[2,16,32,128]{3,2,1,0:T(8,128)S(1)}, u32[]{:S(2)}, u32[]{:S(2)}) collective-permute-start(f32[2,16,32,128]{3,2,1,0:T(8,128)S(1)} %get-tuple-element.31), channel_id=1, source_target_pairs={{0,1},{1,0},{2,3},{3,2},{4,5},{5,4},{6,7},{7,6},{8,9},{9,8},{10,11... | collective-permute-start | bytes 1572872 | tf_op jit(solution)/shard_map/ppermute | solution.py:188
  26.7 5.2 %collective-permute-start.5 = (f16[28,8,128]{2,1,0:T(8,128)(2,1)S(1)}, f16[28,8,128]{2,1,0:T(8,128)(2,1)S(1)}, u32[]{:S(2)}, u32[]{:S(2)}) collective-permute-start(f16[28,8,128]{2,1,0:T(8,128)(2,1)S(1)} %get-tuple-element.45), channel_id=1, source_target_pairs={{0,16},{2,18},{4,20},{6,22},{8,24},{10,26},{12,28},{14,30},{16,0},... | collective-permute-start | bytes 172040 | tf_op jit(solution)/shard_map/ppermute | solution.py:188
  26.7 5.2 %collective-permute-start.4 = (f16[28,8,128]{2,1,0:T(8,128)(2,1)S(1)}, f16[28,8,128]{2,1,0:T(8,128)(2,1)S(1)}, u32[]{:S(2)}, u32[]{:S(2)}) collective-permute-start(f16[28,8,128]{2,1,0:T(8,128)(2,1)S(1)} %get-tuple-element.43), channel_id=1, source_target_pairs={{0,8},{2,10},{4,12},{6,14},{8,0},{10,2},{12,4},{14,6},{16,24},{18,... | collective-permute-start | bytes 172040 | tf_op jit(solution)/shard_map/ppermute | solution.py:188
  32.2 6.2 %collective-permute-start.9 = (f16[28,8,128]{2,1,0:T(8,128)(2,1)S(1)}, f16[28,8,128]{2,1,0:T(8,128)(2,1)S(1)}, u32[]{:S(2)}, u32[]{:S(2)}) collective-permute-start(f16[28,8,128]{2,1,0:T(8,128)(2,1)S(1)} %fusion.13), channel_id=1, source_target_pairs={{0,24},{2,26},{4,28},{6,30},{8,16},{10,18},{12,20},{14,22},{16,8},... | collective-permute-start | bytes 172040 | tf_op jit(solution)/shard_map/ppermute | solution.py:188
  33.8 4.8 %collective-permute-start.8 = (f16[28,8,128]{2,1,0:T(8,128)(2,1)S(1)}, f16[28,8,128]{2,1,0:T(8,128)(2,1)S(1)}, u32[]{:S(2)}, u32[]{:S(2)}) collective-permute-start(f16[28,8,128]{2,1,0:T(8,128)(2,1)S(1)} %fusion.13), channel_id=1, source_target_pairs={{0,8},{2,10},{4,12},{6,14},{8,0},{10,2},{12,4},{14,6},{16,24},{18,... | collective-permute-start | bytes 172040 | tf_op jit(solution)/shard_map/ppermute | solution.py:188
  34.7 5.1 %collective-permute-start.7 = (f16[28,8,128]{2,1,0:T(8,128)(2,1)S(1)}, f16[28,8,128]{2,1,0:T(8,128)(2,1)S(1)}, u32[]{:S(2)}, u32[]{:S(2)}) collective-permute-start(f16[28,8,128]{2,1,0:T(8,128)(2,1)S(1)} %fusion.13), channel_id=1, source_target_pairs={{0,16},{2,18},{4,20},{6,22},{8,24},{10,26},{12,28},{14,30},{16,0},... | collective-permute-start | bytes 172040 | tf_op jit(solution)/shard_map/ppermute | solution.py:188
  36.6 6.1 %collective-permute-start.12 = (f32[16,16,128]{2,1,0:T(8,128)S(1)}, f32[16,16,128]{2,1,0:T(8,128)S(1)}, u32[]{:S(2)}, u32[]{:S(2)}) collective-permute-start(f32[16,16,128]{2,1,0:T(8,128)S(1)} %get-tuple-element.34), channel_id=1, source_target_pairs={{0,2},{2,4},{4,6},{6,8},{8,10},{10,12},{12,14},{14,16},{16,18},{18... | collective-permute-start | bytes 393224 | tf_op jit(solution)/shard_map/ppermute | solution.py:193
  40.0 8.0 %collective-permute-start.11 = (f16[28,4,8,128]{3,2,1,0:T(8,128)(2,1)S(1)}, f16[28,4,8,128]{3,2,1,0:T(8,128)(2,1)S(1)}, u32[]{:S(2)}, u32[]{:S(2)}) collective-permute-start(f16[28,4,8,128]{3,2,1,0:T(8,128)(2,1)S(1)} %select_select_fusion), channel_id=1, source_target_pairs={{0,4},{2,6},{4,0},{6,2},{8,12},{10,14},{12,8},{14,10},{16,20},{18,... | collective-permute-start | bytes 688136 | tf_op jit(solution)/shard_map/ppermute | solution.py:188
  41.5 6.6 %collective-permute-start.13 = (f16[28,4,8,128]{3,2,1,0:T(8,128)(2,1)S(1)}, f16[28,4,8,128]{3,2,1,0:T(8,128)(2,1)S(1)}, u32[]{:S(2)}, u32[]{:S(2)}) collective-permute-start(f16[28,4,8,128]{3,2,1,0:T(8,128)(2,1)S(1)} %select_select_fusion), channel_id=1, source_target_pairs={{0,2},{2,0},{4,6},{6,4},{8,10},{10,8},{12,14},{14,12},{16,18},{18,... | collective-permute-start | bytes 688136 | tf_op jit(solution)/shard_map/ppermute | solution.py:188
  48.0 1.6 %collective-permute-start.14 = (f16[28,4,8,128]{3,2,1,0:T(8,128)(2,1)S(1)}, f16[28,4,8,128]{3,2,1,0:T(8,128)(2,1)S(1)}, u32[]{:S(2)}, u32[]{:S(2)}) collective-permute-start(f16[28,4,8,128]{3,2,1,0:T(8,128)(2,1)S(1)} %collective-permute-done.11), channel_id=1, source_target_pairs={{0,2},{2,0},{4,6},{6,4},{8,10},{10,8},{12,14},{14,12},{16,18},{18,... | collective-permute-start | bytes 688136 | tf_op jit(solution)/shard_map/ppermute | solution.py:188
  49.7 1.2 %copy-start.4 = (f32[27,2,2,4,8,128]{5,4,3,2,1,0:T(8,128)}, f32[27,2,2,4,8,128]{5,4,3,2,1,0:T(8,128)S(1)}, u32[]{:S(2)}) copy-start(f32[27,2,2,4,8,128]{5,4,3,2,1,0:T(8,128)S(1)} %fusion.9) | copy-start | bytes 5308420

commit v3 on v2

--- a/solution.py
+++ b/solution.py
@@ -226,18 +226,18 @@
     near = add(near, decode(got[:, :quarter]))
     got = beside("x", swap(sent, "space", 2))
     total = add(near, decode(got)).reshape(TAPS + 1, nz, quarter // nz, near.shape[2])
-    got = [swap(encode(total[:, q]), "space", 4 * q) for q in range(1, nz)]
+    got = [beside(f"z{q}", swap(encode(total[:, q]), "space", 4 * q)) for q in range(1, nz)]
     total = total[:, 0]
     for piece in got:
         total = add(total, decode(piece))
     total = beside("z", encode(jnp.where(is_level(total), total, total * factor)))
-    total = arrange([total] + [swap(total, "space", 4 * q) for q in range(1, nz)], z)
+    total = arrange([total] + [beside(f"a{q}", swap(total, "space", 4 * q)) for q in range(1, nz)], z)
     total = beside("back", total)
-    across = beside("end", swap(total, "space", 2))
+    across = swap(total, "space", 2)
     cin = near.shape[2]
     out = jnp.zeros((TAPS, 2, 2, nz, quarter // nz, cin), F32)
     pieces = ((core, x, total), (core, 1 - x, across))
-    pieces += tuple((1 - core, at, swap(piece, "space", 1)) for _, at, piece in pieces)
+    pieces += tuple((1 - core, at, beside(f"c{i}", swap(piece, "space", 1))) for i, (_, at, piece) in enumerate(pieces))
     for half, at, piece in pieces:
         out = lax.dynamic_update_slice(out, decode(piece)[:TAPS][:, None, None], (0, half, at, 0, 0, 0))
     return out.reshape(3, 3, 3, 4 * quarter, cin)
@@ -316,27 +316,29 @@
                 placed=True,
                 flops=flops,
             )
-            if filt == 2:
-                held["in"] = swap(held["part"][1], "filt", 1)
-            held["below"] = move(held["send"], "space", 1)
         if stage == "x":
             value, *held["part"], held["own"], held["send"] = lax.optimization_barrier(
                 (value, *held["part"], held["own"], held["send"])
             )
-        if stage == "end":
-            value, held["below"] = lax.optimization_barrier((value, held["below"]))
-        if stage == "back" and filt == 2:
-            value, held["in"] = lax.optimization_barrier((value, held["in"]))
+        if stage == "a2":
+            value, held["send"] = lax.optimization_barrier((value, held["send"]))
+            held["below"] = move(held["send"], "space", 1)
+        if stage == "z3" and filt == 2:
+            value, held["part"][1] = lax.optimization_barrier((value, held["part"][1]))
+            held["in"] = swap(held["part"][1], "filt", 1)
+        if stage == "c1":
+            features = (held["own"] + held["below"]).astype(BF16)[None]
+            if filt == 2:
+                gradient = (held["part"][0] + held["in"]).astype(BF16)
+            else:
+                gradient = lax.psum_scatter(jnp.stack(held["part"]), "filt", scatter_dimension=0).astype(BF16)
+            held["features"], held["gradient"] = features, gradient
+            value, held["gradient"] = lax.optimization_barrier((value, gradient))
         return value
 
     factor = float(peers * cells) ** (-0.5)
     kernel_grad = sum_over_space(near, mid, far, (core, x, z, nz), factor, beside)
-    features = (held["own"] + held["below"]).astype(BF16)[None]
-    if filt == 2:
-        gradient = (held["part"][0] + held["in"]).astype(BF16)
-    else:
-        gradient = lax.psum_scatter(jnp.stack(held["part"]), "filt", scatter_dimension=0).astype(BF16)
-    return features, gradient, kernel_grad
+    return held["features"], held["gradient"], kernel_grad
 
 
 def solution(mesh):

time: 51.1 us -> 48.9 us (0.957)
  waiting for transfers between devices: 18.8 us -> 15.2 us
  starting transfers between devices: 19.9 us -> 21.2 us
    ppermute x13, waiting for transfers between devices: 18.8 us -> 14.6 us  [swap(): return lax.ppermute(x, axis, [(i, i ^ bits) for i in range(peers)])]
    ppermute x2, starting transfers between devices: 2.57 us -> 3.68 us  [move(): lax.ppermute(x, axis, [(i, i + by) for i in range(peers) if 0 <= i + by <...]
    ppermute x2, waiting for transfers between devices: 0.01 us -> 0.61 us  [move(): lax.ppermute(x, axis, [(i, i + by) for i in range(peers) if 0 <= i + by <...]
where the time goes in v3:
time: 48.9 us; the launch traced here: 48.5 us
  starting transfers between devices  21.2 us (43%)
  waiting for transfers between devices  15.2 us (31%)
  Pallas kernels  4.59 us (9%)
  other arithmetic  3.45 us (7%)
  local copies, waits for them, and re-layouts  3.21 us (7%)
  between operations  0.91 us (2%)
    ppermute x13, starting transfers between devices, swap(): return lax.ppermute(x, axis, [(i, i ^ bits) for i in range(peers)])  17.5 us
    ppermute x13, waiting for transfers between devices, swap(): return lax.ppermute(x, axis, [(i, i ^ bits) for i in range(peers)])  14.6 us
    pallas_call x5, Pallas kernels, call(): pl.pallas_call(kernel, out_shape=out_shape, in_specs=[smem if placed and...  4.59 us
    ppermute x2, starting transfers between devices, move(): lax.ppermute(x, axis, [(i, i + by) for i in range(peers) if 0 <= i + by <...  3.68 us
    unnamed x10, local copies, waits for them, and re-layouts  3.01 us
  transfers between devices with their start and end apart: 15, of which 9 were waited for; matrix products, arithmetic and copies ran while one was open for 5% of the time, Pallas kernels for 8%

profile of v3, /device:TPU:0, one launch (start us, length us, event | category | flops | bytes accessed | tf_op | source)
XLA Modules:
  0.0 48.5 jit_solution(11448684951120601632)
XLA Ops:
  0.6 3.0 %collective-permute-start = (bf16[2,16,32,128]{3,2,1,0:T(8,128)(2,1)}, bf16[2,16,32,128]{3,2,1,0:T(8,128)(2,1)S(1)}, u32[]{:S(2)}, u32[]{:S(2)}) collective-permute-start(bf16[2,16,32,128]{3,2,1,0:T(8,128)(2,1)} %volume_ref.1), channel_id=1, source_target_pairs={{0,1},{1,0},{2,3},{3,2},{4,5},{5,4},{6,7},{7,6},{8,9},{9,8},{10,11... | collective-permute-start | bytes 786440 | tf_op jit(solution)/shard_map/ppermute | solution.py:188
  3.7 1.3 %collective-permute-start.1 = (bf16[1,16,16,128]{3,2,1,0:T(8,128)(2,1)}, bf16[1,16,16,128]{3,2,1,0:T(8,128)(2,1)S(1)}, u32[]{:S(2)}, u32[]{:S(2)}) collective-permute-start(bf16[1,16,16,128]{3,2,1,0:T(8,128)(2,1)} %param.5), channel_id=1, source_target_pairs={{2,0},{4,2},{6,4},{8,6},{10,8},{12,10},{14,12},{16,14},{18,16},{20... | collective-permute-start | bytes 196616 | tf_op jit(solution)/shard_map/ppermute | solution.py:193
  5.0 0.1 pad_add_fusion.place
  5.0 0.8 %copy-done.1 = bf16[1,16,16,128]{3,2,1,0:T(8,128)(2,1)S(1)} copy-done((bf16[1,16,16,128]{3,2,1,0:T(8,128)(2,1)S(1)}, bf16[1,16,16,128]{3,2,1,0:T(8,128)(2,1)}, u32[]{:S(2)}) %copy-start.1) | copy-done | bytes 65560
  5.9 0.9 %copy-done.3 = bf16[2,16,32,128]{3,2,1,0:T(8,128)(2,1)S(1)} copy-done((bf16[2,16,32,128]{3,2,1,0:T(8,128)(2,1)S(1)}, bf16[2,16,32,128]{3,2,1,0:T(8,128)(2,1)}, u32[]{:S(2)}) %copy-start.3) | copy-done | bytes 262168
  6.8 0.9 %shard_map.58 = (bf16[4,128,256]{2,1,0:T(8,128)(2,1)S(1)}, bf16[4,128,256]{2,1,0:T(8,128)(2,1)S(1)}) custom-call(s32[3]{0:T(128)S(1)} %pad_add_fusion.place, bf16[16,16,128]{2,1,0:T(8,128)(2,1)S(1)} %bitcast.92, bf16[2,16,32,128]{3,2,1,0:T(8,128)(2,1)S(1)} %copy-done.3), custom_call_target="tpu_custom_call" | custom-call | bytes 851980 | tf_op jit(solution)/shard_map/pallas_call | solution.py:175
  7.7 0.8 %shard_map.59.refs_3_ = bf16[4,128,256]{2,1,0:T(8,128)(2,1)S(1)} custom-call(s32[3]{0:T(128)S(1)} %pad_add_fusion.place, bf16[16,16,128]{2,1,0:T(8,128)(2,1)S(1)} %bitcast.94), custom_call_target="tpu_custom_call" | custom-call | bytes 327692 | tf_op jit(solution)/shard_map/pallas_call | solution.py:175
  8.6 1.6 %collective-permute-done.refs_1_ = bf16[2,16,32,128]{3,2,1,0:T(8,128)(2,1)S(1)} collective-permute-done((bf16[2,16,32,128]{3,2,1,0:T(8,128)(2,1)}, bf16[2,16,32,128]{3,2,1,0:T(8,128)(2,1)S(1)}, u32[]{:S(2)}, u32[]{:S(2)}) %collective-permute-start) | collective-permute-done | bytes 262176 | tf_op jit(solution)/shard_map/ppermute | solution.py:188
  10.2 0.5 %shard_map.60 = (f32[28,32,128]{2,1,0:T(8,128)S(1)}, f32[28,32,128]{2,1,0:T(8,128)S(1)}, f32[28,64,128]{2,1,0:T(8,128)S(1)}, bf16[4,256,256]{2,1,0:T(8,128)(2,1)S(1)}) custom-call(bf16[4,128,256]{2,1,0:T(8,128)(2,1)S(1)} %get-tuple-element.27.refs_0_, bf16[2,16,32,128]{3,2,1,0:T(8,128)(2,1)S(1)} %collective-permute-done.refs_1_, ...), custom_call_target="tpu_custom_call" | custom-call | flops 226492416 | bytes 3407872 | tf_op jit(solution)/shard_map/pallas_call | solution.py:175
  10.7 0.2 fusion
  10.9 0.3 collective-permute-start.2
  11.3 1.5 %collective-permute-done.2 = f16[28,64,128]{2,1,0:T(8,128)(2,1)S(1)} collective-permute-done((f16[28,64,128]{2,1,0:T(8,128)(2,1)S(1)}, f16[28,64,128]{2,1,0:T(8,128)(2,1)S(1)}, u32[]{:S(2)}, u32[]{:S(2)}) %collective-permute-start.2) | collective-permute-done | bytes 458784 | tf_op jit(solution)/shard_map/ppermute | solution.py:188
  12.8 0.2 add_select_fusion
  13.0 0.1 fusion.1
  13.1 1.8 %collective-permute-start.3 = (f16[28,32,128]{2,1,0:T(8,128)(2,1)S(1)}, f16[28,32,128]{2,1,0:T(8,128)(2,1)S(1)}, u32[]{:S(2)}, u32[]{:S(2)}) collective-permute-start(f16[28,32,128]{2,1,0:T(8,128)(2,1)S(1)} %fusion.1), channel_id=1, source_target_pairs={{0,4},{2,6},{4,0},{6,2},{8,12},{10,14},{12,8},{14,10},{16,20},{18,... | collective-permute-start | bytes 688136 | tf_op jit(solution)/shard_map/ppermute | solution.py:188
  14.9 1.2 %shard_map.62 = (f32[16,16,128]{2,1,0:T(8,128)S(1)}, f32[16,16,128]{2,1,0:T(8,128)S(1)}) custom-call(s32[3]{0:T(128)S(1)} %pad_add_fusion.place, bf16[4,256,256]{2,1,0:T(8,128)(2,1)S(1)} %get-tuple-element.36.class_ref, bf16[27,128,128]{2,1,0:T(8,128)(2,1)S(1)} %bitcast.90), custom_call_target="tpu_custom_call" | custom-call | flops 226492416 | bytes 1671180 | tf_op jit(solution)/shard_map/pallas_call | solution.py:175
  16.1 1.2 %shard_map.61 = (f32[2,16,32,128]{3,2,1,0:T(8,128)S(1)}, f32[2,16,32,128]{3,2,1,0:T(8,128)S(1)}) custom-call(s32[3]{0:T(128)S(1)} %pad_add_fusion.place, bf16[16,16,128]{2,1,0:T(8,128)(2,1)S(1)} %bitcast.93, bf16[16,16,128]{2,1,0:T(8,128)(2,1)S(1)} %bitcast.95, bf16[27,128,128]{2,1,0:T(8,128)(2,1)S(1)} %bitcast.91), custom_call_target="tpu_custom_call" | custom-call | flops 226492416 | bytes 2064396 | tf_op jit(solution)/shard_map/pallas_call | solution.py:175
  17.3 3.7 %collective-permute-done.3 = f16[28,32,128]{2,1,0:T(8,128)(2,1)S(1)} collective-permute-done((f16[28,32,128]{2,1,0:T(8,128)(2,1)S(1)}, f16[28,32,128]{2,1,0:T(8,128)(2,1)S(1)}, u32[]{:S(2)}, u32[]{:S(2)}) %collective-permute-start.3) | collective-permute-done | bytes 229408 | tf_op jit(solution)/shard_map/ppermute | solution.py:188
  21.1 0.3 select_bitcast_fusion
  21.4 0.1 fusion.10
  21.5 3.7 %collective-permute-start.6 = (f16[28,8,128]{2,1,0:T(8,128)(2,1)S(1)}, f16[28,8,128]{2,1,0:T(8,128)(2,1)S(1)}, u32[]{:S(2)}, u32[]{:S(2)}) collective-permute-start(f16[28,8,128]{2,1,0:T(8,128)(2,1)S(1)} %get-tuple-element.52), channel_id=1, source_target_pairs={{0,24},{2,26},{4,28},{6,30},{8,16},{10,18},{12,20},{14,22},{16,8},... | collective-permute-start | bytes 172040 | tf_op jit(solution)/shard_map/ppermute | solution.py:188
  25.2 0.8 %collective-permute-start.4 = (f16[28,8,128]{2,1,0:T(8,128)(2,1)S(1)}, f16[28,8,128]{2,1,0:T(8,128)(2,1)S(1)}, u32[]{:S(2)}, u32[]{:S(2)}) collective-permute-start(f16[28,8,128]{2,1,0:T(8,128)(2,1)S(1)} %get-tuple-element.51), channel_id=1, source_target_pairs={{0,8},{2,10},{4,12},{6,14},{8,0},{10,2},{12,4},{14,6},{16,24},{18,... | collective-permute-start | bytes 172040 | tf_op jit(solution)/shard_map/ppermute | solution.py:188
  25.9 2.2 %collective-permute-done.6 = f16[28,8,128]{2,1,0:T(8,128)(2,1)S(1)} collective-permute-done((f16[28,8,128]{2,1,0:T(8,128)(2,1)S(1)}, f16[28,8,128]{2,1,0:T(8,128)(2,1)S(1)}, u32[]{:S(2)}, u32[]{:S(2)}) %collective-permute-start.6) | collective-permute-done | bytes 57376 | tf_op jit(solution)/shard_map/ppermute | solution.py:188
  28.1 2.1 %collective-permute-done.5 = f16[28,8,128]{2,1,0:T(8,128)(2,1)S(1)} collective-permute-done((f16[28,8,128]{2,1,0:T(8,128)(2,1)S(1)}, f16[28,8,128]{2,1,0:T(8,128)(2,1)S(1)}, u32[]{:S(2)}, u32[]{:S(2)}) %collective-permute-start.5) | collective-permute-done | bytes 57376 | tf_op jit(solution)/shard_map/ppermute | solution.py:188
  30.3 0.2 multiply_select_fusion.10
  30.4 0.1 fusion.13
  30.6 2.1 %collective-permute-start.7 = (f16[28,8,128]{2,1,0:T(8,128)(2,1)S(1)}, f16[28,8,128]{2,1,0:T(8,128)(2,1)S(1)}, u32[]{:S(2)}, u32[]{:S(2)}) collective-permute-start(f16[28,8,128]{2,1,0:T(8,128)(2,1)S(1)} %fusion.13), channel_id=1, source_target_pairs={{0,16},{2,18},{4,20},{6,22},{8,24},{10,26},{12,28},{14,30},{16,0},... | collective-permute-start | bytes 172040 | tf_op jit(solution)/shard_map/ppermute | solution.py:188
  32.6 0.9 %collective-permute-start.10 = (f16[28,8,128]{2,1,0:T(8,128)(2,1)S(1)}, f16[28,8,128]{2,1,0:T(8,128)(2,1)S(1)}, u32[]{:S(2)}, u32[]{:S(2)}) collective-permute-start(f16[28,8,128]{2,1,0:T(8,128)(2,1)S(1)} %fusion.13), channel_id=1, source_target_pairs={{0,24},{2,26},{4,28},{6,30},{8,16},{10,18},{12,20},{14,22},{16,8},... | collective-permute-start | bytes 172040 | tf_op jit(solution)/shard_map/ppermute | solution.py:188
  33.5 0.6 %collective-permute-start.9 = (f16[28,8,128]{2,1,0:T(8,128)(2,1)S(1)}, f16[28,8,128]{2,1,0:T(8,128)(2,1)S(1)}, u32[]{:S(2)}, u32[]{:S(2)}) collective-permute-start(f16[28,8,128]{2,1,0:T(8,128)(2,1)S(1)} %fusion.13), channel_id=1, source_target_pairs={{0,8},{2,10},{4,12},{6,14},{8,0},{10,2},{12,4},{14,6},{16,24},{18,... | collective-permute-start | bytes 172040 | tf_op jit(solution)/shard_map/ppermute | solution.py:188
  34.1 1.5 %collective-permute-start.13 = (f32[2,16,32,128]{3,2,1,0:T(8,128)S(1)}, f32[2,16,32,128]{3,2,1,0:T(8,128)S(1)}, u32[]{:S(2)}, u32[]{:S(2)}) collective-permute-start(f32[2,16,32,128]{3,2,1,0:T(8,128)S(1)} %get-tuple-element.48), channel_id=1, source_target_pairs={{0,1},{1,0},{2,3},{3,2},{4,5},{5,4},{6,7},{7,6},{8,9},{9,8},{10,11... | collective-permute-start | bytes 1572872 | tf_op jit(solution)/shard_map/ppermute | solution.py:188
  35.6 0.9 %collective-permute-done.7 = f16[28,8,128]{2,1,0:T(8,128)(2,1)S(1)} collective-permute-done((f16[28,8,128]{2,1,0:T(8,128)(2,1)S(1)}, f16[28,8,128]{2,1,0:T(8,128)(2,1)S(1)}, u32[]{:S(2)}, u32[]{:S(2)}) %collective-permute-start.7) | collective-permute-done | bytes 57376 | tf_op jit(solution)/shard_map/ppermute | solution.py:188
  36.5 2.1 %collective-permute-done.10 = f16[28,8,128]{2,1,0:T(8,128)(2,1)S(1)} collective-permute-done((f16[28,8,128]{2,1,0:T(8,128)(2,1)S(1)}, f16[28,8,128]{2,1,0:T(8,128)(2,1)S(1)}, u32[]{:S(2)}, u32[]{:S(2)}) %collective-permute-start.10) | collective-permute-done | bytes 57376 | tf_op jit(solution)/shard_map/ppermute | solution.py:188
  38.6 0.2 select_select_fusion
  38.8 1.6 %collective-permute-start.11 = (f16[28,4,8,128]{3,2,1,0:T(8,128)(2,1)S(1)}, f16[28,4,8,128]{3,2,1,0:T(8,128)(2,1)S(1)}, u32[]{:S(2)}, u32[]{:S(2)}) collective-permute-start(f16[28,4,8,128]{3,2,1,0:T(8,128)(2,1)S(1)} %select_select_fusion), channel_id=1, source_target_pairs={{0,4},{2,6},{4,0},{6,2},{8,12},{10,14},{12,8},{14,10},{16,20},{18,... | collective-permute-start | bytes 688136 | tf_op jit(solution)/shard_map/ppermute | solution.py:188
  40.3 0.1 collective-permute-start.14
  40.4 2.4 %collective-permute-start.8 = (f32[16,16,128]{2,1,0:T(8,128)S(1)}, f32[16,16,128]{2,1,0:T(8,128)S(1)}, u32[]{:S(2)}, u32[]{:S(2)}) collective-permute-start(f32[16,16,128]{2,1,0:T(8,128)S(1)} %get-tuple-element.45), channel_id=1, source_target_pairs={{0,2},{2,4},{4,6},{6,8},{8,10},{10,12},{12,14},{14,16},{16,18},{18... | collective-permute-start | bytes 393224 | tf_op jit(solution)/shard_map/ppermute | solution.py:193
  42.8 0.2 broadcast_in_dim.47
  43.0 0.1 fusion.3
  43.2 0.6 %collective-permute-done.8 = f32[16,16,128]{2,1,0:T(8,128)S(1)} collective-permute-done((f32[16,16,128]{2,1,0:T(8,128)S(1)}, f32[16,16,128]{2,1,0:T(8,128)S(1)}, u32[]{:S(2)}, u32[]{:S(2)}) %collective-permute-start.8) | collective-permute-done | bytes 131104 | tf_op jit(solution)/shard_map/ppermute | solution.py:193
  43.8 0.6 %fusion.14 = bf16[1,16,16,128]{3,2,1,0:T(8,128)(2,1)} fusion(f32[16,16,128]{2,1,0:T(8,128)S(1)} %get-tuple-element.39, f32[16,16,128]{2,1,0:T(8,128)S(1)} %collective-permute-done.8), kind=kLoop, calls=%fused_computation.40 | loop fusion | flops 65536 | bytes 327680 | tf_op jit(solution)/shard_map/broadcast_in_dim | solution.py:330
  44.4 0.4 collective-permute-done.11
  44.9 1.2 %collective-permute-start.12 = (f16[28,4,8,128]{3,2,1,0:T(8,128)(2,1)S(1)}, f16[28,4,8,128]{3,2,1,0:T(8,128)(2,1)S(1)}, u32[]{:S(2)}, u32[]{:S(2)}) collective-permute-start(f16[28,4,8,128]{3,2,1,0:T(8,128)(2,1)S(1)} %collective-permute-done.11), channel_id=1, source_target_pairs={{0,2},{2,0},{4,6},{6,4},{8,10},{10,8},{12,14},{14,12},{16,18},{18,... | collective-permute-start | bytes 688136 | tf_op jit(solution)/shard_map/ppermute | solution.py:188
  46.1 0.1 fusion.5
  46.2 0.1 fusion.7
  46.4 0.8 %add_convert_fusion = bf16[2,16,32,128]{3,2,1,0:T(8,128)(2,1)} fusion(f32[2,16,32,128]{3,2,1,0:T(8,128)S(1)} %get-tuple-element.47, f32[2,16,32,128]{3,2,1,0:T(8,128)S(1)} %collective-permute-done.13), kind=kLoop, calls=%fused_computation.10 | loop fusion | flops 262144 | bytes 1310720 | tf_op jit(solution)/shard_map/convert_element_type | solution.py:332
  47.2 0.1 fusion.9
  47.3 0.0 copy-start.4
  47.3 1.2 %copy-done.4 = f32[27,2,2,4,8,128]{5,4,3,2,1,0:T(8,128)} copy-done((f32[27,2,2,4,8,128]{5,4,3,2,1,0:T(8,128)}, f32[27,2,2,4,8,128]{5,4,3,2,1,0:T(8,128)S(1)}, u32[]{:S(2)}) %copy-start.4) | copy-done | bytes 1769496
  (29 shorter events, 0.2 us)
Async XLA Ops:
  0.6 9.6 %collective-permute-start = (bf16[2,16,32,128]{3,2,1,0:T(8,128)(2,1)}, bf16[2,16,32,128]{3,2,1,0:T(8,128)(2,1)S(1)}, u32[]{:S(2)}, u32[]{:S(2)}) collective-permute-start(bf16[2,16,32,128]{3,2,1,0:T(8,128)(2,1)} %volume_ref.1), channel_id=1, source_target_pairs={{0,1},{1,0},{2,3},{3,2},{4,5},{5,4},{6,7},{7,6},{8,9},{9,8},{10,11... | collective-permute-start | bytes 786440 | tf_op jit(solution)/shard_map/ppermute | solution.py:188
  3.7 4.0 %collective-permute-start.1 = (bf16[1,16,16,128]{3,2,1,0:T(8,128)(2,1)}, bf16[1,16,16,128]{3,2,1,0:T(8,128)(2,1)S(1)}, u32[]{:S(2)}, u32[]{:S(2)}) collective-permute-start(bf16[1,16,16,128]{3,2,1,0:T(8,128)(2,1)} %param.5), channel_id=1, source_target_pairs={{2,0},{4,2},{6,4},{8,6},{10,8},{12,10},{14,12},{16,14},{18,16},{20... | collective-permute-start | bytes 196616 | tf_op jit(solution)/shard_map/ppermute | solution.py:193
  5.0 0.8 %copy-start.1 = (bf16[1,16,16,128]{3,2,1,0:T(8,128)(2,1)S(1)}, bf16[1,16,16,128]{3,2,1,0:T(8,128)(2,1)}, u32[]{:S(2)}) copy-start(bf16[1,16,16,128]{3,2,1,0:T(8,128)(2,1)} %param.5) | copy-start | bytes 196612
  5.9 0.9 %copy-start.3 = (bf16[2,16,32,128]{3,2,1,0:T(8,128)(2,1)S(1)}, bf16[2,16,32,128]{3,2,1,0:T(8,128)(2,1)}, u32[]{:S(2)}) copy-start(bf16[2,16,32,128]{3,2,1,0:T(8,128)(2,1)} %volume_ref.1) | copy-start | bytes 786436
  10.7 4.2 %copy-start = (bf16[3,3,3,128,128]{4,3,2,1,0:T(8,128)(2,1)S(1)}, bf16[3,3,3,128,128]{4,3,2,1,0:T(8,128)(2,1)}, u32[]{:S(2)}) copy-start(bf16[3,3,3,128,128]{4,3,2,1,0:T(8,128)(2,1)} %param.4) | copy-start | bytes 2654212
  10.9 5.2 %copy-start.2 = (bf16[1,16,16,128]{3,2,1,0:T(8,128)(2,1)S(1)}, bf16[1,16,16,128]{3,2,1,0:T(8,128)(2,1)}, u32[]{:S(2)}) copy-start(bf16[1,16,16,128]{3,2,1,0:T(8,128)(2,1)} %param.5) | copy-start | bytes 196612
  10.9 1.9 %collective-permute-start.2 = (f16[28,64,128]{2,1,0:T(8,128)(2,1)S(1)}, f16[28,64,128]{2,1,0:T(8,128)(2,1)S(1)}, u32[]{:S(2)}, u32[]{:S(2)}) collective-permute-start(f16[28,64,128]{2,1,0:T(8,128)(2,1)S(1)} %fusion), channel_id=1, source_target_pairs={{0,2},{2,0},{4,6},{6,4},{8,10},{10,8},{12,14},{14,12},{16,18},{18,... | collective-permute-start | bytes 1376264 | tf_op jit(solution)/shard_map/ppermute | solution.py:188
  13.1 7.9 %collective-permute-start.3 = (f16[28,32,128]{2,1,0:T(8,128)(2,1)S(1)}, f16[28,32,128]{2,1,0:T(8,128)(2,1)S(1)}, u32[]{:S(2)}, u32[]{:S(2)}) collective-permute-start(f16[28,32,128]{2,1,0:T(8,128)(2,1)S(1)} %fusion.1), channel_id=1, source_target_pairs={{0,4},{2,6},{4,0},{6,2},{8,12},{10,14},{12,8},{14,10},{16,20},{18,... | collective-permute-start | bytes 688136 | tf_op jit(solution)/shard_map/ppermute | solution.py:188
  21.5 6.6 %collective-permute-start.6 = (f16[28,8,128]{2,1,0:T(8,128)(2,1)S(1)}, f16[28,8,128]{2,1,0:T(8,128)(2,1)S(1)}, u32[]{:S(2)}, u32[]{:S(2)}) collective-permute-start(f16[28,8,128]{2,1,0:T(8,128)(2,1)S(1)} %get-tuple-element.52), channel_id=1, source_target_pairs={{0,24},{2,26},{4,28},{6,30},{8,16},{10,18},{12,20},{14,22},{16,8},... | collective-permute-start | bytes 172040 | tf_op jit(solution)/shard_map/ppermute | solution.py:188
  25.2 5.1 %collective-permute-start.5 = (f16[28,8,128]{2,1,0:T(8,128)(2,1)S(1)}, f16[28,8,128]{2,1,0:T(8,128)(2,1)S(1)}, u32[]{:S(2)}, u32[]{:S(2)}) collective-permute-start(f16[28,8,128]{2,1,0:T(8,128)(2,1)S(1)} %get-tuple-element.53), channel_id=1, source_target_pairs={{0,16},{2,18},{4,20},{6,22},{8,24},{10,26},{12,28},{14,30},{16,0},... | collective-permute-start | bytes 172040 | tf_op jit(solution)/shard_map/ppermute | solution.py:188
  25.2 5.1 %collective-permute-start.4 = (f16[28,8,128]{2,1,0:T(8,128)(2,1)S(1)}, f16[28,8,128]{2,1,0:T(8,128)(2,1)S(1)}, u32[]{:S(2)}, u32[]{:S(2)}) collective-permute-start(f16[28,8,128]{2,1,0:T(8,128)(2,1)S(1)} %get-tuple-element.51), channel_id=1, source_target_pairs={{0,8},{2,10},{4,12},{6,14},{8,0},{10,2},{12,4},{14,6},{16,24},{18,... | collective-permute-start | bytes 172040 | tf_op jit(solution)/shard_map/ppermute | solution.py:188
  30.6 6.0 %collective-permute-start.7 = (f16[28,8,128]{2,1,0:T(8,128)(2,1)S(1)}, f16[28,8,128]{2,1,0:T(8,128)(2,1)S(1)}, u32[]{:S(2)}, u32[]{:S(2)}) collective-permute-start(f16[28,8,128]{2,1,0:T(8,128)(2,1)S(1)} %fusion.13), channel_id=1, source_target_pairs={{0,16},{2,18},{4,20},{6,22},{8,24},{10,26},{12,28},{14,30},{16,0},... | collective-permute-start | bytes 172040 | tf_op jit(solution)/shard_map/ppermute | solution.py:188
  32.6 6.0 %collective-permute-start.10 = (f16[28,8,128]{2,1,0:T(8,128)(2,1)S(1)}, f16[28,8,128]{2,1,0:T(8,128)(2,1)S(1)}, u32[]{:S(2)}, u32[]{:S(2)}) collective-permute-start(f16[28,8,128]{2,1,0:T(8,128)(2,1)S(1)} %fusion.13), channel_id=1, source_target_pairs={{0,24},{2,26},{4,28},{6,30},{8,16},{10,18},{12,20},{14,22},{16,8},... | collective-permute-start | bytes 172040 | tf_op jit(solution)/shard_map/ppermute | solution.py:188
  33.5 5.1 %collective-permute-start.9 = (f16[28,8,128]{2,1,0:T(8,128)(2,1)S(1)}, f16[28,8,128]{2,1,0:T(8,128)(2,1)S(1)}, u32[]{:S(2)}, u32[]{:S(2)}) collective-permute-start(f16[28,8,128]{2,1,0:T(8,128)(2,1)S(1)} %fusion.13), channel_id=1, source_target_pairs={{0,8},{2,10},{4,12},{6,14},{8,0},{10,2},{12,4},{14,6},{16,24},{18,... | collective-permute-start | bytes 172040 | tf_op jit(solution)/shard_map/ppermute | solution.py:188
  34.1 12.2 %collective-permute-start.13 = (f32[2,16,32,128]{3,2,1,0:T(8,128)S(1)}, f32[2,16,32,128]{3,2,1,0:T(8,128)S(1)}, u32[]{:S(2)}, u32[]{:S(2)}) collective-permute-start(f32[2,16,32,128]{3,2,1,0:T(8,128)S(1)} %get-tuple-element.48), channel_id=1, source_target_pairs={{0,1},{1,0},{2,3},{3,2},{4,5},{5,4},{6,7},{7,6},{8,9},{9,8},{10,11... | collective-permute-start | bytes 1572872 | tf_op jit(solution)/shard_map/ppermute | solution.py:188
  38.8 6.1 %collective-permute-start.11 = (f16[28,4,8,128]{3,2,1,0:T(8,128)(2,1)S(1)}, f16[28,4,8,128]{3,2,1,0:T(8,128)(2,1)S(1)}, u32[]{:S(2)}, u32[]{:S(2)}) collective-permute-start(f16[28,4,8,128]{3,2,1,0:T(8,128)(2,1)S(1)} %select_select_fusion), channel_id=1, source_target_pairs={{0,4},{2,6},{4,0},{6,2},{8,12},{10,14},{12,8},{14,10},{16,20},{18,... | collective-permute-start | bytes 688136 | tf_op jit(solution)/shard_map/ppermute | solution.py:188
  40.3 5.7 %collective-permute-start.14 = (f16[28,4,8,128]{3,2,1,0:T(8,128)(2,1)S(1)}, f16[28,4,8,128]{3,2,1,0:T(8,128)(2,1)S(1)}, u32[]{:S(2)}, u32[]{:S(2)}) collective-permute-start(f16[28,4,8,128]{3,2,1,0:T(8,128)(2,1)S(1)} %select_select_fusion), channel_id=1, source_target_pairs={{0,2},{2,0},{4,6},{6,4},{8,10},{10,8},{12,14},{14,12},{16,18},{18,... | collective-permute-start | bytes 688136 | tf_op jit(solution)/shard_map/ppermute | solution.py:188
  40.4 3.4 %collective-permute-start.8 = (f32[16,16,128]{2,1,0:T(8,128)S(1)}, f32[16,16,128]{2,1,0:T(8,128)S(1)}, u32[]{:S(2)}, u32[]{:S(2)}) collective-permute-start(f32[16,16,128]{2,1,0:T(8,128)S(1)} %get-tuple-element.45), channel_id=1, source_target_pairs={{0,2},{2,4},{4,6},{6,8},{8,10},{10,12},{12,14},{14,16},{16,18},{18... | collective-permute-start | bytes 393224 | tf_op jit(solution)/shard_map/ppermute | solution.py:193
  44.9 2.3 %collective-permute-start.12 = (f16[28,4,8,128]{3,2,1,0:T(8,128)(2,1)S(1)}, f16[28,4,8,128]{3,2,1,0:T(8,128)(2,1)S(1)}, u32[]{:S(2)}, u32[]{:S(2)}) collective-permute-start(f16[28,4,8,128]{3,2,1,0:T(8,128)(2,1)S(1)} %collective-permute-done.11), channel_id=1, source_target_pairs={{0,2},{2,0},{4,6},{6,4},{8,10},{10,8},{12,14},{14,12},{16,18},{18,... | collective-permute-start | bytes 688136 | tf_op jit(solution)/shard_map/ppermute | solution.py:188
  47.3 1.2 %copy-start.4 = (f32[27,2,2,4,8,128]{5,4,3,2,1,0:T(8,128)}, f32[27,2,2,4,8,128]{5,4,3,2,1,0:T(8,128)S(1)}, u32[]{:S(2)}) copy-start(f32[27,2,2,4,8,128]{5,4,3,2,1,0:T(8,128)S(1)} %fusion.9) | copy-start | bytes 5308420

commit v4 on v3

--- a/solution.py
+++ b/solution.py
@@ -168,6 +168,11 @@
     send_ref[...] = total[1, :rows]
 
 
+def round_kernel(own_ref, below_ref, part_ref, other_ref, features_ref, gradient_ref):
+    features_ref[...] = (own_ref[...] + below_ref[...]).astype(BF16)
+    gradient_ref[...] = (part_ref[...] + other_ref[...]).astype(BF16)
+
+
 def call(kernel, out_shape, arguments, scratch=(), placed=False, flops=0):
     vmem = pl.BlockSpec(memory_space=pltpu.VMEM)
     smem = pl.BlockSpec(memory_space=pltpu.SMEM)
@@ -233,7 +238,7 @@
     total = beside("z", encode(jnp.where(is_level(total), total, total * factor)))
     total = arrange([total] + [beside(f"a{q}", swap(total, "space", 4 * q)) for q in range(1, nz)], z)
     total = beside("back", total)
-    across = swap(total, "space", 2)
+    across = beside("end", swap(total, "space", 2))
     cin = near.shape[2]
     out = jnp.zeros((TAPS, 2, 2, nz, quarter // nz, cin), F32)
     pieces = ((core, x, total), (core, 1 - x, across))
@@ -327,18 +332,21 @@
             value, held["part"][1] = lax.optimization_barrier((value, held["part"][1]))
             held["in"] = swap(held["part"][1], "filt", 1)
         if stage == "c1":
-            features = (held["own"] + held["below"]).astype(BF16)[None]
             if filt == 2:
-                gradient = (held["part"][0] + held["in"]).astype(BF16)
+                _, below, other = lax.optimization_barrier((value, held["below"], held["in"]))
+                held["features"], held["gradient"] = call(
+                    round_kernel,
+                    [jax.ShapeDtypeStruct(held["own"].shape, BF16), jax.ShapeDtypeStruct(volume.shape, BF16)],
+                    (held["own"], below, held["part"][0], other),
+                )
             else:
-                gradient = lax.psum_scatter(jnp.stack(held["part"]), "filt", scatter_dimension=0).astype(BF16)
-            held["features"], held["gradient"] = features, gradient
-            value, held["gradient"] = lax.optimization_barrier((value, gradient))
+                gradient = lax.psum_scatter(jnp.stack(held["part"]), "filt", scatter_dimension=0)
+                held["features"], held["gradient"] = (held["own"] + held["below"]).astype(BF16), gradient.astype(BF16)
         return value
 
     factor = float(peers * cells) ** (-0.5)
     kernel_grad = sum_over_space(near, mid, far, (core, x, z, nz), factor, beside)
-    return held["features"], held["gradient"], kernel_grad
+    return held["features"][None], held["gradient"], kernel_grad
 
 
 def solution(mesh):

time: 48.9 us -> 47.7 us (0.975)
  other arithmetic: 3.45 us -> 2.01 us
  Pallas kernels: 4.59 us -> 5.52 us
  local copies, waits for them, and re-layouts: 3.21 us -> 2.3 us
  waiting for transfers between devices: 15.2 us -> 15.8 us
    ppermute x13, waiting for transfers between devices: 14.6 us -> 15.8 us  [swap(): return lax.ppermute(x, axis, [(i, i ^ bits) for i in range(peers)])]
    pallas_call x5 -> x6, Pallas kernels: 4.59 us -> 5.52 us  [call(): pl.pallas_call(kernel, out_shape=out_shape, in_specs=[smem if placed and...]
    unnamed x10, local copies, waits for them, and re-layouts: 3.01 us -> 2.09 us
    convert_element_type x1 -> x0, other arithmetic: 0.79 us -> none  [beside(): gradient = (held['part'][0] + held['in']).astype(BF16)]
    broadcast_in_dim x1 -> x0, other arithmetic: 0.65 us -> none  [beside(): features = (held['own'] + held['below']).astype(BF16)[None]]
    ppermute x2, waiting for transfers between devices: 0.61 us -> 0.01 us  [move(): lax.ppermute(x, axis, [(i, i + by) for i in range(peers) if 0 <= i + by <...]
  transfers between devices with their start and end apart: 15 -> 15, of which waited for: 9 -> 9; matrix products, arithmetic and copies ran while one was open for 5% -> 2% of each run, Pallas kernels for 8% -> 9%
where the time goes in v4:
time: 47.7 us; the launch traced here: 47.5 us
  starting transfers between devices  20.9 us (44%)
  waiting for transfers between devices  15.8 us (33%)
  Pallas kernels  5.52 us (12%)
  local copies, waits for them, and re-layouts  2.3 us (5%)
  other arithmetic  2.01 us (4%)
  between operations  0.91 us (2%)
    ppermute x13, starting transfers between devices, swap(): return lax.ppermute(x, axis, [(i, i ^ bits) for i in range(peers)])  17.2 us
    ppermute x13, waiting for transfers between devices, swap(): return lax.ppermute(x, axis, [(i, i ^ bits) for i in range(peers)])  15.8 us
    pallas_call x6, Pallas kernels, call(): pl.pallas_call(kernel, out_shape=out_shape, in_specs=[smem if placed and...  5.52 us
    ppermute x2, starting transfers between devices, move(): lax.ppermute(x, axis, [(i, i + by) for i in range(peers) if 0 <= i + by <...  3.68 us
    unnamed x10, local copies, waits for them, and re-layouts  2.09 us
  transfers between devices with their start and end apart: 15, of which 9 were waited for; matrix products, arithmetic and copies ran while one was open for 2% of the time, Pallas kernels for 9%

profile of v4, /device:TPU:0, one launch (start us, length us, event | category | flops | bytes accessed | tf_op | source)
XLA Modules:
  0.0 47.5 jit_solution(2792461489048557432)
XLA Ops:
  0.6 3.0 %collective-permute-start = (bf16[2,16,32,128]{3,2,1,0:T(8,128)(2,1)}, bf16[2,16,32,128]{3,2,1,0:T(8,128)(2,1)S(1)}, u32[]{:S(2)}, u32[]{:S(2)}) collective-permute-start(bf16[2,16,32,128]{3,2,1,0:T(8,128)(2,1)} %volume_ref.1), channel_id=1, source_target_pairs={{0,1},{1,0},{2,3},{3,2},{4,5},{5,4},{6,7},{7,6},{8,9},{9,8},{10,11... | collective-permute-start | bytes 786440 | tf_op jit(solution)/shard_map/ppermute | solution.py:193
  3.7 1.3 %collective-permute-start.1 = (bf16[1,16,16,128]{3,2,1,0:T(8,128)(2,1)}, bf16[1,16,16,128]{3,2,1,0:T(8,128)(2,1)S(1)}, u32[]{:S(2)}, u32[]{:S(2)}) collective-permute-start(bf16[1,16,16,128]{3,2,1,0:T(8,128)(2,1)} %param.5), channel_id=1, source_target_pairs={{2,0},{4,2},{6,4},{8,6},{10,8},{12,10},{14,12},{16,14},{18,16},{20... | collective-permute-start | bytes 196616 | tf_op jit(solution)/shard_map/ppermute | solution.py:198
  5.0 0.1 pad_add_fusion.place
  5.0 0.8 %copy-done.1 = bf16[1,16,16,128]{3,2,1,0:T(8,128)(2,1)S(1)} copy-done((bf16[1,16,16,128]{3,2,1,0:T(8,128)(2,1)S(1)}, bf16[1,16,16,128]{3,2,1,0:T(8,128)(2,1)}, u32[]{:S(2)}) %copy-start.1) | copy-done | bytes 65560
  5.9 0.9 %copy-done.3 = bf16[2,16,32,128]{3,2,1,0:T(8,128)(2,1)S(1)} copy-done((bf16[2,16,32,128]{3,2,1,0:T(8,128)(2,1)S(1)}, bf16[2,16,32,128]{3,2,1,0:T(8,128)(2,1)}, u32[]{:S(2)}) %copy-start.3) | copy-done | bytes 262168
  6.8 0.9 %shard_map.58 = (bf16[4,128,256]{2,1,0:T(8,128)(2,1)S(1)}, bf16[4,128,256]{2,1,0:T(8,128)(2,1)S(1)}) custom-call(s32[3]{0:T(128)S(1)} %pad_add_fusion.place, bf16[16,16,128]{2,1,0:T(8,128)(2,1)S(1)} %bitcast.91, bf16[2,16,32,128]{3,2,1,0:T(8,128)(2,1)S(1)} %copy-done.3), custom_call_target="tpu_custom_call" | custom-call | bytes 851980 | tf_op jit(solution)/shard_map/pallas_call | solution.py:180
  7.7 0.8 %shard_map.59.refs_3_ = bf16[4,128,256]{2,1,0:T(8,128)(2,1)S(1)} custom-call(s32[3]{0:T(128)S(1)} %pad_add_fusion.place, bf16[16,16,128]{2,1,0:T(8,128)(2,1)S(1)} %bitcast.93), custom_call_target="tpu_custom_call" | custom-call | bytes 327692 | tf_op jit(solution)/shard_map/pallas_call | solution.py:180
  8.6 1.6 %collective-permute-done.refs_1_ = bf16[2,16,32,128]{3,2,1,0:T(8,128)(2,1)S(1)} collective-permute-done((bf16[2,16,32,128]{3,2,1,0:T(8,128)(2,1)}, bf16[2,16,32,128]{3,2,1,0:T(8,128)(2,1)S(1)}, u32[]{:S(2)}, u32[]{:S(2)}) %collective-permute-start) | collective-permute-done | bytes 262176 | tf_op jit(solution)/shard_map/ppermute | solution.py:193
  10.2 0.5 %shard_map.60 = (f32[28,32,128]{2,1,0:T(8,128)S(1)}, f32[28,32,128]{2,1,0:T(8,128)S(1)}, f32[28,64,128]{2,1,0:T(8,128)S(1)}, bf16[4,256,256]{2,1,0:T(8,128)(2,1)S(1)}) custom-call(bf16[4,128,256]{2,1,0:T(8,128)(2,1)S(1)} %get-tuple-element.29.refs_0_, bf16[2,16,32,128]{3,2,1,0:T(8,128)(2,1)S(1)} %collective-permute-done.refs_1_, ...), custom_call_target="tpu_custom_call" | custom-call | flops 226492416 | bytes 3407872 | tf_op jit(solution)/shard_map/pallas_call | solution.py:180
  10.7 0.0 copy-start
  10.7 0.2 fusion
  10.9 0.0 copy-start.2
  10.9 0.3 collective-permute-start.2
  11.3 1.5 %collective-permute-done.2 = f16[28,64,128]{2,1,0:T(8,128)(2,1)S(1)} collective-permute-done((f16[28,64,128]{2,1,0:T(8,128)(2,1)S(1)}, f16[28,64,128]{2,1,0:T(8,128)(2,1)S(1)}, u32[]{:S(2)}, u32[]{:S(2)}) %collective-permute-start.2) | collective-permute-done | bytes 458784 | tf_op jit(solution)/shard_map/ppermute | solution.py:193
  12.8 0.2 add_select_fusion
  13.0 0.1 fusion.1
  13.1 1.8 %collective-permute-start.3 = (f16[28,32,128]{2,1,0:T(8,128)(2,1)S(1)}, f16[28,32,128]{2,1,0:T(8,128)(2,1)S(1)}, u32[]{:S(2)}, u32[]{:S(2)}) collective-permute-start(f16[28,32,128]{2,1,0:T(8,128)(2,1)S(1)} %fusion.1), channel_id=1, source_target_pairs={{0,4},{2,6},{4,0},{6,2},{8,12},{10,14},{12,8},{14,10},{16,20},{18,... | collective-permute-start | bytes 688136 | tf_op jit(solution)/shard_map/ppermute | solution.py:193
  14.9 1.2 %shard_map.62 = (f32[16,16,128]{2,1,0:T(8,128)S(1)}, f32[16,16,128]{2,1,0:T(8,128)S(1)}) custom-call(s32[3]{0:T(128)S(1)} %pad_add_fusion.place, bf16[4,256,256]{2,1,0:T(8,128)(2,1)S(1)} %get-tuple-element.38.class_ref, bf16[27,128,128]{2,1,0:T(8,128)(2,1)S(1)} %bitcast.89), custom_call_target="tpu_custom_call" | custom-call | flops 226492416 | bytes 1671180 | tf_op jit(solution)/shard_map/pallas_call | solution.py:180
  16.1 1.2 %shard_map.61 = (f32[2,16,32,128]{3,2,1,0:T(8,128)S(1)}, f32[2,16,32,128]{3,2,1,0:T(8,128)S(1)}) custom-call(s32[3]{0:T(128)S(1)} %pad_add_fusion.place, bf16[16,16,128]{2,1,0:T(8,128)(2,1)S(1)} %bitcast.92, bf16[16,16,128]{2,1,0:T(8,128)(2,1)S(1)} %bitcast.94, bf16[27,128,128]{2,1,0:T(8,128)(2,1)S(1)} %bitcast.90), custom_call_target="tpu_custom_call" | custom-call | flops 226492416 | bytes 2064396 | tf_op jit(solution)/shard_map/pallas_call | solution.py:180
  17.3 3.7 %collective-permute-done.3 = f16[28,32,128]{2,1,0:T(8,128)(2,1)S(1)} collective-permute-done((f16[28,32,128]{2,1,0:T(8,128)(2,1)S(1)}, f16[28,32,128]{2,1,0:T(8,128)(2,1)S(1)}, u32[]{:S(2)}, u32[]{:S(2)}) %collective-permute-start.3) | collective-permute-done | bytes 229408 | tf_op jit(solution)/shard_map/ppermute | solution.py:193
  21.1 0.3 select_bitcast_fusion
  21.4 0.1 fusion.10
  21.5 3.7 %collective-permute-start.6 = (f16[28,8,128]{2,1,0:T(8,128)(2,1)S(1)}, f16[28,8,128]{2,1,0:T(8,128)(2,1)S(1)}, u32[]{:S(2)}, u32[]{:S(2)}) collective-permute-start(f16[28,8,128]{2,1,0:T(8,128)(2,1)S(1)} %get-tuple-element.56), channel_id=1, source_target_pairs={{0,24},{2,26},{4,28},{6,30},{8,16},{10,18},{12,20},{14,22},{16,8},... | collective-permute-start | bytes 172040 | tf_op jit(solution)/shard_map/ppermute | solution.py:193
  25.2 0.8 %collective-permute-start.4 = (f16[28,8,128]{2,1,0:T(8,128)(2,1)S(1)}, f16[28,8,128]{2,1,0:T(8,128)(2,1)S(1)}, u32[]{:S(2)}, u32[]{:S(2)}) collective-permute-start(f16[28,8,128]{2,1,0:T(8,128)(2,1)S(1)} %get-tuple-element.55), channel_id=1, source_target_pairs={{0,8},{2,10},{4,12},{6,14},{8,0},{10,2},{12,4},{14,6},{16,24},{18,... | collective-permute-start | bytes 172040 | tf_op jit(solution)/shard_map/ppermute | solution.py:193
  25.9 2.2 %collective-permute-done.6 = f16[28,8,128]{2,1,0:T(8,128)(2,1)S(1)} collective-permute-done((f16[28,8,128]{2,1,0:T(8,128)(2,1)S(1)}, f16[28,8,128]{2,1,0:T(8,128)(2,1)S(1)}, u32[]{:S(2)}, u32[]{:S(2)}) %collective-permute-start.6) | collective-permute-done | bytes 57376 | tf_op jit(solution)/shard_map/ppermute | solution.py:193
  28.1 2.1 %collective-permute-done.5 = f16[28,8,128]{2,1,0:T(8,128)(2,1)S(1)} collective-permute-done((f16[28,8,128]{2,1,0:T(8,128)(2,1)S(1)}, f16[28,8,128]{2,1,0:T(8,128)(2,1)S(1)}, u32[]{:S(2)}, u32[]{:S(2)}) %collective-permute-start.5) | collective-permute-done | bytes 57376 | tf_op jit(solution)/shard_map/ppermute | solution.py:193
  30.3 0.2 multiply_select_fusion.10
  30.4 0.1 fusion.13
  30.6 2.2 %collective-permute-start.9 = (f16[28,8,128]{2,1,0:T(8,128)(2,1)S(1)}, f16[28,8,128]{2,1,0:T(8,128)(2,1)S(1)}, u32[]{:S(2)}, u32[]{:S(2)}) collective-permute-start(f16[28,8,128]{2,1,0:T(8,128)(2,1)S(1)} %fusion.13), channel_id=1, source_target_pairs={{0,24},{2,26},{4,28},{6,30},{8,16},{10,18},{12,20},{14,22},{16,8},... | collective-permute-start | bytes 172040 | tf_op jit(solution)/shard_map/ppermute | solution.py:193
  32.8 0.4 collective-permute-start.8
  33.2 1.8 %collective-permute-start.7 = (f16[28,8,128]{2,1,0:T(8,128)(2,1)S(1)}, f16[28,8,128]{2,1,0:T(8,128)(2,1)S(1)}, u32[]{:S(2)}, u32[]{:S(2)}) collective-permute-start(f16[28,8,128]{2,1,0:T(8,128)(2,1)S(1)} %fusion.13), channel_id=1, source_target_pairs={{0,16},{2,18},{4,20},{6,22},{8,24},{10,26},{12,28},{14,30},{16,0},... | collective-permute-start | bytes 172040 | tf_op jit(solution)/shard_map/ppermute | solution.py:193
  35.0 1.5 %collective-permute-start.13 = (f32[2,16,32,128]{3,2,1,0:T(8,128)S(1)}, f32[2,16,32,128]{3,2,1,0:T(8,128)S(1)}, u32[]{:S(2)}, u32[]{:S(2)}) collective-permute-start(f32[2,16,32,128]{3,2,1,0:T(8,128)S(1)} %get-tuple-element.49), channel_id=1, source_target_pairs={{0,1},{1,0},{2,3},{3,2},{4,5},{5,4},{6,7},{7,6},{8,9},{9,8},{10,11... | collective-permute-start | bytes 1572872 | tf_op jit(solution)/shard_map/ppermute | solution.py:193
  36.5 1.7 %collective-permute-done.7 = f16[28,8,128]{2,1,0:T(8,128)(2,1)S(1)} collective-permute-done((f16[28,8,128]{2,1,0:T(8,128)(2,1)S(1)}, f16[28,8,128]{2,1,0:T(8,128)(2,1)S(1)}, u32[]{:S(2)}, u32[]{:S(2)}) %collective-permute-start.7) | collective-permute-done | bytes 57376 | tf_op jit(solution)/shard_map/ppermute | solution.py:193
  38.3 0.2 select_select_fusion
  38.4 1.6 %collective-permute-start.10 = (f16[28,4,8,128]{3,2,1,0:T(8,128)(2,1)S(1)}, f16[28,4,8,128]{3,2,1,0:T(8,128)(2,1)S(1)}, u32[]{:S(2)}, u32[]{:S(2)}) collective-permute-start(f16[28,4,8,128]{3,2,1,0:T(8,128)(2,1)S(1)} %select_select_fusion), channel_id=1, source_target_pairs={{0,4},{2,6},{4,0},{6,2},{8,12},{10,14},{12,8},{14,10},{16,20},{18,... | collective-permute-start | bytes 688136 | tf_op jit(solution)/shard_map/ppermute | solution.py:193
  40.0 0.1 collective-permute-start.14
  40.1 2.4 %collective-permute-start.12 = (f32[16,16,128]{2,1,0:T(8,128)S(1)}, f32[16,16,128]{2,1,0:T(8,128)S(1)}, u32[]{:S(2)}, u32[]{:S(2)}) collective-permute-start(f32[16,16,128]{2,1,0:T(8,128)S(1)} %get-tuple-element.48), channel_id=1, source_target_pairs={{0,2},{2,4},{4,6},{6,8},{8,10},{10,12},{12,14},{14,16},{16,18},{18... | collective-permute-start | bytes 393224 | tf_op jit(solution)/shard_map/ppermute | solution.py:198
  42.5 0.2 broadcast_in_dim.47
  42.7 0.1 fusion.3
  42.8 1.7 %collective-permute-done.10 = f16[28,4,8,128]{3,2,1,0:T(8,128)(2,1)S(1)} collective-permute-done((f16[28,4,8,128]{3,2,1,0:T(8,128)(2,1)S(1)}, f16[28,4,8,128]{3,2,1,0:T(8,128)(2,1)S(1)}, u32[]{:S(2)}, u32[]{:S(2)}) %collective-permute-start.10) | collective-permute-done | bytes 229408 | tf_op jit(solution)/shard_map/ppermute | solution.py:193
  44.6 0.1 fusion.5
  44.7 0.1 fusion.7
  44.9 1.2 %collective-permute-done.11 = f16[28,4,8,128]{3,2,1,0:T(8,128)(2,1)S(1)} collective-permute-done((f16[28,4,8,128]{3,2,1,0:T(8,128)(2,1)S(1)}, f16[28,4,8,128]{3,2,1,0:T(8,128)(2,1)S(1)}, u32[]{:S(2)}, u32[]{:S(2)}) %collective-permute-start.11) | collective-permute-done | bytes 229408 | tf_op jit(solution)/shard_map/ppermute | solution.py:193
  46.0 0.1 fusion.9
  46.2 0.0 copy-start.4
  46.2 0.1 collective-permute-done.13.other_ref
  46.3 0.9 %shard_map.63 = (bf16[16,16,128]{2,1,0:T(8,128)(2,1)}, bf16[2,16,32,128]{3,2,1,0:T(8,128)(2,1)}) custom-call(f32[16,16,128]{2,1,0:T(8,128)S(1)} %get-tuple-element.41.own_ref, f32[16,16,128]{2,1,0:T(8,128)S(1)} %collective-permute-done.12.below_ref, f32[2,16,32,128]{3,2,1,0:T(8,128)S(1)} %get-tuple-element.51.part_ref, ...), custom_call_target="tpu_custom_call" | custom-call | bytes 1638400 | tf_op jit(solution)/shard_map/pallas_call | solution.py:180
  47.2 0.3 copy-done.4
  (28 shorter events, 0.2 us)
Async XLA Ops:
  0.6 9.6 %collective-permute-start = (bf16[2,16,32,128]{3,2,1,0:T(8,128)(2,1)}, bf16[2,16,32,128]{3,2,1,0:T(8,128)(2,1)S(1)}, u32[]{:S(2)}, u32[]{:S(2)}) collective-permute-start(bf16[2,16,32,128]{3,2,1,0:T(8,128)(2,1)} %volume_ref.1), channel_id=1, source_target_pairs={{0,1},{1,0},{2,3},{3,2},{4,5},{5,4},{6,7},{7,6},{8,9},{9,8},{10,11... | collective-permute-start | bytes 786440 | tf_op jit(solution)/shard_map/ppermute | solution.py:193
  3.7 4.0 %collective-permute-start.1 = (bf16[1,16,16,128]{3,2,1,0:T(8,128)(2,1)}, bf16[1,16,16,128]{3,2,1,0:T(8,128)(2,1)S(1)}, u32[]{:S(2)}, u32[]{:S(2)}) collective-permute-start(bf16[1,16,16,128]{3,2,1,0:T(8,128)(2,1)} %param.5), channel_id=1, source_target_pairs={{2,0},{4,2},{6,4},{8,6},{10,8},{12,10},{14,12},{16,14},{18,16},{20... | collective-permute-start | bytes 196616 | tf_op jit(solution)/shard_map/ppermute | solution.py:198
  5.0 0.8 %copy-start.1 = (bf16[1,16,16,128]{3,2,1,0:T(8,128)(2,1)S(1)}, bf16[1,16,16,128]{3,2,1,0:T(8,128)(2,1)}, u32[]{:S(2)}) copy-start(bf16[1,16,16,128]{3,2,1,0:T(8,128)(2,1)} %param.5) | copy-start | bytes 196612
  5.9 0.9 %copy-start.3 = (bf16[2,16,32,128]{3,2,1,0:T(8,128)(2,1)S(1)}, bf16[2,16,32,128]{3,2,1,0:T(8,128)(2,1)}, u32[]{:S(2)}) copy-start(bf16[2,16,32,128]{3,2,1,0:T(8,128)(2,1)} %volume_ref.1) | copy-start | bytes 786436
  10.7 4.2 %copy-start = (bf16[3,3,3,128,128]{4,3,2,1,0:T(8,128)(2,1)S(1)}, bf16[3,3,3,128,128]{4,3,2,1,0:T(8,128)(2,1)}, u32[]{:S(2)}) copy-start(bf16[3,3,3,128,128]{4,3,2,1,0:T(8,128)(2,1)} %param.4) | copy-start | bytes 2654212
  10.9 5.2 %copy-start.2 = (bf16[1,16,16,128]{3,2,1,0:T(8,128)(2,1)S(1)}, bf16[1,16,16,128]{3,2,1,0:T(8,128)(2,1)}, u32[]{:S(2)}) copy-start(bf16[1,16,16,128]{3,2,1,0:T(8,128)(2,1)} %param.5) | copy-start | bytes 196612
  10.9 1.9 %collective-permute-start.2 = (f16[28,64,128]{2,1,0:T(8,128)(2,1)S(1)}, f16[28,64,128]{2,1,0:T(8,128)(2,1)S(1)}, u32[]{:S(2)}, u32[]{:S(2)}) collective-permute-start(f16[28,64,128]{2,1,0:T(8,128)(2,1)S(1)} %fusion), channel_id=1, source_target_pairs={{0,2},{2,0},{4,6},{6,4},{8,10},{10,8},{12,14},{14,12},{16,18},{18,... | collective-permute-start | bytes 1376264 | tf_op jit(solution)/shard_map/ppermute | solution.py:193
  13.1 7.9 %collective-permute-start.3 = (f16[28,32,128]{2,1,0:T(8,128)(2,1)S(1)}, f16[28,32,128]{2,1,0:T(8,128)(2,1)S(1)}, u32[]{:S(2)}, u32[]{:S(2)}) collective-permute-start(f16[28,32,128]{2,1,0:T(8,128)(2,1)S(1)} %fusion.1), channel_id=1, source_target_pairs={{0,4},{2,6},{4,0},{6,2},{8,12},{10,14},{12,8},{14,10},{16,20},{18,... | collective-permute-start | bytes 688136 | tf_op jit(solution)/shard_map/ppermute | solution.py:193
  21.5 6.6 %collective-permute-start.6 = (f16[28,8,128]{2,1,0:T(8,128)(2,1)S(1)}, f16[28,8,128]{2,1,0:T(8,128)(2,1)S(1)}, u32[]{:S(2)}, u32[]{:S(2)}) collective-permute-start(f16[28,8,128]{2,1,0:T(8,128)(2,1)S(1)} %get-tuple-element.56), channel_id=1, source_target_pairs={{0,24},{2,26},{4,28},{6,30},{8,16},{10,18},{12,20},{14,22},{16,8},... | collective-permute-start | bytes 172040 | tf_op jit(solution)/shard_map/ppermute | solution.py:193
  25.2 5.1 %collective-permute-start.5 = (f16[28,8,128]{2,1,0:T(8,128)(2,1)S(1)}, f16[28,8,128]{2,1,0:T(8,128)(2,1)S(1)}, u32[]{:S(2)}, u32[]{:S(2)}) collective-permute-start(f16[28,8,128]{2,1,0:T(8,128)(2,1)S(1)} %get-tuple-element.57), channel_id=1, source_target_pairs={{0,16},{2,18},{4,20},{6,22},{8,24},{10,26},{12,28},{14,30},{16,0},... | collective-permute-start | bytes 172040 | tf_op jit(solution)/shard_map/ppermute | solution.py:193
  25.2 5.1 %collective-permute-start.4 = (f16[28,8,128]{2,1,0:T(8,128)(2,1)S(1)}, f16[28,8,128]{2,1,0:T(8,128)(2,1)S(1)}, u32[]{:S(2)}, u32[]{:S(2)}) collective-permute-start(f16[28,8,128]{2,1,0:T(8,128)(2,1)S(1)} %get-tuple-element.55), channel_id=1, source_target_pairs={{0,8},{2,10},{4,12},{6,14},{8,0},{10,2},{12,4},{14,6},{16,24},{18,... | collective-permute-start | bytes 172040 | tf_op jit(solution)/shard_map/ppermute | solution.py:193
  30.6 7.7 %collective-permute-start.9 = (f16[28,8,128]{2,1,0:T(8,128)(2,1)S(1)}, f16[28,8,128]{2,1,0:T(8,128)(2,1)S(1)}, u32[]{:S(2)}, u32[]{:S(2)}) collective-permute-start(f16[28,8,128]{2,1,0:T(8,128)(2,1)S(1)} %fusion.13), channel_id=1, source_target_pairs={{0,24},{2,26},{4,28},{6,30},{8,16},{10,18},{12,20},{14,22},{16,8},... | collective-permute-start | bytes 172040 | tf_op jit(solution)/shard_map/ppermute | solution.py:193
  32.8 5.5 %collective-permute-start.8 = (f16[28,8,128]{2,1,0:T(8,128)(2,1)S(1)}, f16[28,8,128]{2,1,0:T(8,128)(2,1)S(1)}, u32[]{:S(2)}, u32[]{:S(2)}) collective-permute-start(f16[28,8,128]{2,1,0:T(8,128)(2,1)S(1)} %fusion.13), channel_id=1, source_target_pairs={{0,8},{2,10},{4,12},{6,14},{8,0},{10,2},{12,4},{14,6},{16,24},{18,... | collective-permute-start | bytes 172040 | tf_op jit(solution)/shard_map/ppermute | solution.py:193
  33.2 5.1 %collective-permute-start.7 = (f16[28,8,128]{2,1,0:T(8,128)(2,1)S(1)}, f16[28,8,128]{2,1,0:T(8,128)(2,1)S(1)}, u32[]{:S(2)}, u32[]{:S(2)}) collective-permute-start(f16[28,8,128]{2,1,0:T(8,128)(2,1)S(1)} %fusion.13), channel_id=1, source_target_pairs={{0,16},{2,18},{4,20},{6,22},{8,24},{10,26},{12,28},{14,30},{16,0},... | collective-permute-start | bytes 172040 | tf_op jit(solution)/shard_map/ppermute | solution.py:193
  35.0 11.3 %collective-permute-start.13 = (f32[2,16,32,128]{3,2,1,0:T(8,128)S(1)}, f32[2,16,32,128]{3,2,1,0:T(8,128)S(1)}, u32[]{:S(2)}, u32[]{:S(2)}) collective-permute-start(f32[2,16,32,128]{3,2,1,0:T(8,128)S(1)} %get-tuple-element.49), channel_id=1, source_target_pairs={{0,1},{1,0},{2,3},{3,2},{4,5},{5,4},{6,7},{7,6},{8,9},{9,8},{10,11... | collective-permute-start | bytes 1572872 | tf_op jit(solution)/shard_map/ppermute | solution.py:193
  38.4 6.1 %collective-permute-start.10 = (f16[28,4,8,128]{3,2,1,0:T(8,128)(2,1)S(1)}, f16[28,4,8,128]{3,2,1,0:T(8,128)(2,1)S(1)}, u32[]{:S(2)}, u32[]{:S(2)}) collective-permute-start(f16[28,4,8,128]{3,2,1,0:T(8,128)(2,1)S(1)} %select_select_fusion), channel_id=1, source_target_pairs={{0,4},{2,6},{4,0},{6,2},{8,12},{10,14},{12,8},{14,10},{16,20},{18,... | collective-permute-start | bytes 688136 | tf_op jit(solution)/shard_map/ppermute | solution.py:193
  40.0 4.5 %collective-permute-start.14 = (f16[28,4,8,128]{3,2,1,0:T(8,128)(2,1)S(1)}, f16[28,4,8,128]{3,2,1,0:T(8,128)(2,1)S(1)}, u32[]{:S(2)}, u32[]{:S(2)}) collective-permute-start(f16[28,4,8,128]{3,2,1,0:T(8,128)(2,1)S(1)} %select_select_fusion), channel_id=1, source_target_pairs={{0,2},{2,0},{4,6},{6,4},{8,10},{10,8},{12,14},{14,12},{16,18},{18,... | collective-permute-start | bytes 688136 | tf_op jit(solution)/shard_map/ppermute | solution.py:193
  40.1 6.1 %collective-permute-start.12 = (f32[16,16,128]{2,1,0:T(8,128)S(1)}, f32[16,16,128]{2,1,0:T(8,128)S(1)}, u32[]{:S(2)}, u32[]{:S(2)}) collective-permute-start(f32[16,16,128]{2,1,0:T(8,128)S(1)} %get-tuple-element.48), channel_id=1, source_target_pairs={{0,2},{2,4},{4,6},{6,8},{8,10},{10,12},{12,14},{14,16},{16,18},{18... | collective-permute-start | bytes 393224 | tf_op jit(solution)/shard_map/ppermute | solution.py:198
  44.5 1.5 %collective-permute-start.11 = (f16[28,4,8,128]{3,2,1,0:T(8,128)(2,1)S(1)}, f16[28,4,8,128]{3,2,1,0:T(8,128)(2,1)S(1)}, u32[]{:S(2)}, u32[]{:S(2)}) collective-permute-start(f16[28,4,8,128]{3,2,1,0:T(8,128)(2,1)S(1)} %collective-permute-done.10), channel_id=1, source_target_pairs={{0,2},{2,0},{4,6},{6,4},{8,10},{10,8},{12,14},{14,12},{16,18},{18,... | collective-permute-start | bytes 688136 | tf_op jit(solution)/shard_map/ppermute | solution.py:193
  46.2 1.3 %copy-start.4 = (f32[27,2,2,4,8,128]{5,4,3,2,1,0:T(8,128)}, f32[27,2,2,4,8,128]{5,4,3,2,1,0:T(8,128)S(1)}, u32[]{:S(2)}) copy-start(f32[27,2,2,4,8,128]{5,4,3,2,1,0:T(8,128)S(1)} %fusion.9) | copy-start | bytes 5308420

commit v5 on v4

--- a/solution.py
+++ b/solution.py
@@ -110,34 +110,46 @@
                         part_refs[block][p, 2 * j + r, pl.ds(q, oz, stride=2), :] = parts[q][at : at + oz]
 
 
-def weight_kernel(blocks, *refs):
-    own_ref, others = refs[0], refs[1:blocks]
-    gt0_ref, gt1_ref, near_ref, mid_ref, far_ref, class_ref, wide = refs[blocks:]
-    quarter, cin = near_ref.shape[1:]
-    cells = own_ref.shape[1]
-
-    def store(index, term):
-        near_ref[index] = term[:quarter]
-        mid_ref[index] = term[quarter : 2 * quarter]
-        far_ref[index] = term[2 * quarter :]
-
-    class_ref[:, :cells] = own_ref[...]
-    for block, ref in enumerate(others):
-        split_classes(ref, class_ref.at[:, pl.ds((block + 1) * cells, cells)], wide)
+def weight_terms(gt_refs, class_ref, rows, store):
+    cin = class_ref.shape[2] // 2
     largest = None
     for p in range(2):
         for r in range(2):
             patch = class_ref[p * 2 + r]
             for a, dx in uses(p):
-                gt_ref = (gt0_ref, gt1_ref)[dx]
                 for b, dy in uses(r):
-                    both = dot(gt_ref[shift_index(0, dy, 0)], patch, ((1,), (0,)))
-                    late = dot(gt_ref[shift_index(0, dy, 1)], patch[:, cin:], ((1,), (0,)))
+                    level, late = [gt_refs[dx][shift_index(0, dy, dz), rows] for dz in range(2)]
+                    both = dot(level, patch, ((1,), (0,)))
+                    late = dot(late, patch[:, cin:], ((1,), (0,)))
                     for c, term in ((0, late), (1, both[:, :cin]), (2, both[:, cin:])):
                         store(tap(a, b, c), term)
                         size = jnp.abs(term)
                         largest = size if largest is None else jnp.maximum(largest, size)
     store(TAPS, jnp.maximum(jnp.floor(jnp.log2(largest)) + 1.0, -100.0))
+
+
+def far_kernel(blocks, *refs):
+    own_ref, others = refs[0], refs[1:blocks]
+    gt0_ref, gt1_ref, far_ref, class_ref, wide = refs[blocks:]
+    cells, rows = own_ref.shape[1], far_ref.shape[1]
+
+    def store(index, term):
+        far_ref[index] = term
+
+    class_ref[:, :cells] = own_ref[...]
+    for block, ref in enumerate(others):
+        split_classes(ref, class_ref.at[:, pl.ds((block + 1) * cells, cells)], wide)
+    weight_terms((gt0_ref, gt1_ref), class_ref, pl.ds(rows, rows), store)
+
+
+def home_kernel(class_ref, gt0_ref, gt1_ref, near_ref, mid_ref):
+    rows = near_ref.shape[1]
+
+    def store(index, term):
+        near_ref[index] = term[:rows]
+        mid_ref[index] = term[rows:]
+
+    weight_terms((gt0_ref, gt1_ref), class_ref, pl.ds(0, 2 * rows), store)
 
 
 def feature_kernel(blocks, half, place, class_ref, w_ref, own_ref, send_ref, total):
@@ -225,22 +237,23 @@
 
 def sum_over_space(near, mid, far, where, factor, beside):
     core, x, z, nz = where
-    quarter = near.shape[1]
+    quarter, cin = near.shape[1:]
+    shape = (TAPS + 1, nz, quarter // nz, cin)
     got = beside("core", swap(encode(far), "space", 1))
-    sent = encode(add(mid, decode(got[:, quarter:])))
-    near = add(near, decode(got[:, :quarter]))
-    got = beside("x", swap(sent, "space", 2))
-    total = add(near, decode(got)).reshape(TAPS + 1, nz, quarter // nz, near.shape[2])
-    got = [beside(f"z{q}", swap(encode(total[:, q]), "space", 4 * q)) for q in range(1, nz)]
-    total = total[:, 0]
-    for piece in got:
-        total = add(total, decode(piece))
+    sent = encode(add(mid, decode(got[:, quarter:]))).reshape(shape)
+    near = add(near, decode(got[:, :quarter])).reshape(shape)
+    own, got = swap(sent[:, 0], "space", 2), beside("x", swap(sent[:, 1:], "space", 2))
+    total = add(near[:, 1:], decode(got))
+    got = {q: beside(f"z{q}", swap(encode(total[:, q - 1]), "space", 4 * q)) for q in range(1, nz)}
+    got[nz - 1], own = lax.optimization_barrier((got[nz - 1], own))
+    total = add(near[:, 0], decode(own))
+    for q in got:
+        total = add(total, decode(got[q]))
     total = beside("z", encode(jnp.where(is_level(total), total, total * factor)))
     total = arrange([total] + [beside(f"a{q}", swap(total, "space", 4 * q)) for q in range(1, nz)], z)
     total = beside("back", total)
-    across = beside("end", swap(total, "space", 2))
-    cin = near.shape[2]
-    out = jnp.zeros((TAPS, 2, 2, nz, quarter // nz, cin), F32)
+    across = swap(total, "space", 2)
+    out = jnp.zeros((TAPS, 2, 2) + shape[1:], F32)
     pieces = ((core, x, total), (core, 1 - x, across))
     pieces += tuple((1 - core, at, beside(f"c{i}", swap(piece, "space", 1))) for i, (_, at, piece) in enumerate(pieces))
     for half, at, piece in pieces:
@@ -288,17 +301,21 @@
         turn_scratch,
         placed=True,
     )
-    near, mid, far, classes = call(
-        functools.partial(weight_kernel, filt),
+    far, classes = call(
+        functools.partial(far_kernel, filt),
         [
-            jax.ShapeDtypeStruct((TAPS + 1, cout // 4, cin), F32),
-            jax.ShapeDtypeStruct((TAPS + 1, cout // 4, cin), F32),
             jax.ShapeDtypeStruct((TAPS + 1, cout // 2, cin), F32),
             jax.ShapeDtypeStruct((4, cells, 2 * cin), BF16),
         ],
         (own_classes, *volumes[1:], own_grads, above_grads),
         [pltpu.VMEM(volume.shape, F32)],
-        flops=flops,
+        flops=flops // 2,
+    )
+    near, mid = call(
+        home_kernel,
+        [jax.ShapeDtypeStruct((TAPS + 1, cout // 4, cin), F32)] * 2,
+        (classes, own_grads, above_grads),
+        flops=flops // 2,
     )
     held = {}
 
@@ -325,10 +342,10 @@
             value, *held["part"], held["own"], held["send"] = lax.optimization_barrier(
                 (value, *held["part"], held["own"], held["send"])
             )
-        if stage == "a2":
+        if stage == "a1":
             value, held["send"] = lax.optimization_barrier((value, held["send"]))
             held["below"] = move(held["send"], "space", 1)
-        if stage == "z3" and filt == 2:
+        if stage == f"z{nz - 1}" and filt == 2:
             value, held["part"][1] = lax.optimization_barrier((value, held["part"][1]))
             held["in"] = swap(held["part"][1], "filt", 1)
         if stage == "c1":

time: 47.7 us -> 47.3 us (level)
  waiting for transfers between devices: 15.8 us -> 14.5 us
    ppermute x13 -> x14, waiting for transfers between devices: 15.8 us -> 14.5 us  [swap(): return lax.ppermute(x, axis, [(i, i ^ bits) for i in range(peers)])]
    ppermute x13 -> x14, starting transfers between devices: 17.2 us -> 17.6 us  [swap(): return lax.ppermute(x, axis, [(i, i ^ bits) for i in range(peers)])]
    pallas_call x6 -> x7, Pallas kernels: 5.52 us -> 5.77 us  [call(): pl.pallas_call(kernel, out_shape=out_shape, in_specs=[smem if placed and...]
    unnamed x10 -> x11, local copies, waits for them, and re-layouts: 2.09 us -> 2.24 us
  transfers between devices with their start and end apart: 15 -> 16, of which waited for: 9 -> 8; matrix products, arithmetic and copies ran while one was open for 2% -> 3% of each run, Pallas kernels for 9% -> 9%
where the time goes in v5:
time: 47.3 us; the launch traced here: 47 us
  starting transfers between devices  21.3 us (45%)
  waiting for transfers between devices  14.5 us (31%)
  Pallas kernels  5.77 us (12%)
  local copies, waits for them, and re-layouts  2.5 us (5%)
  other arithmetic  2.02 us (4%)
  between operations  0.95 us (2%)
    ppermute x14, starting transfers between devices, swap(): return lax.ppermute(x, axis, [(i, i ^ bits) for i in range(peers)])  17.6 us
    ppermute x14, waiting for transfers between devices, swap(): return lax.ppermute(x, axis, [(i, i ^ bits) for i in range(peers)])  14.5 us
    pallas_call x7, Pallas kernels, call(): pl.pallas_call(kernel, out_shape=out_shape, in_specs=[smem if placed and...  5.77 us
    ppermute x2, starting transfers between devices, move(): lax.ppermute(x, axis, [(i, i + by) for i in range(peers) if 0 <= i + by <...  3.68 us
    unnamed x11, local copies, waits for them, and re-layouts  2.24 us
  transfers between devices with their start and end apart: 16, of which 8 were waited for; matrix products, arithmetic and copies ran while one was open for 3% of the time, Pallas kernels for 9%

profile of v5, /device:TPU:0, one launch (start us, length us, event | category | flops | bytes accessed | tf_op | source)
XLA Modules:
  0.0 47.0 jit_solution(12881336089040109647)
XLA Ops:
  0.6 3.0 %collective-permute-start = (bf16[2,16,32,128]{3,2,1,0:T(8,128)(2,1)}, bf16[2,16,32,128]{3,2,1,0:T(8,128)(2,1)S(1)}, u32[]{:S(2)}, u32[]{:S(2)}) collective-permute-start(bf16[2,16,32,128]{3,2,1,0:T(8,128)(2,1)} %volume_ref.1), channel_id=1, source_target_pairs={{0,1},{1,0},{2,3},{3,2},{4,5},{5,4},{6,7},{7,6},{8,9},{9,8},{10,11... | collective-permute-start | bytes 786440 | tf_op jit(solution)/shard_map/ppermute | solution.py:205
  3.7 1.3 %collective-permute-start.1 = (bf16[1,16,16,128]{3,2,1,0:T(8,128)(2,1)}, bf16[1,16,16,128]{3,2,1,0:T(8,128)(2,1)S(1)}, u32[]{:S(2)}, u32[]{:S(2)}) collective-permute-start(bf16[1,16,16,128]{3,2,1,0:T(8,128)(2,1)} %param.5), channel_id=1, source_target_pairs={{2,0},{4,2},{6,4},{8,6},{10,8},{12,10},{14,12},{16,14},{18,16},{20... | collective-permute-start | bytes 196616 | tf_op jit(solution)/shard_map/ppermute | solution.py:210
  5.0 0.1 pad_add_fusion.place
  5.0 0.8 %copy-done.1 = bf16[1,16,16,128]{3,2,1,0:T(8,128)(2,1)S(1)} copy-done((bf16[1,16,16,128]{3,2,1,0:T(8,128)(2,1)S(1)}, bf16[1,16,16,128]{3,2,1,0:T(8,128)(2,1)}, u32[]{:S(2)}) %copy-start.1) | copy-done | bytes 65560
  5.9 0.9 %copy-done.3 = bf16[2,16,32,128]{3,2,1,0:T(8,128)(2,1)S(1)} copy-done((bf16[2,16,32,128]{3,2,1,0:T(8,128)(2,1)S(1)}, bf16[2,16,32,128]{3,2,1,0:T(8,128)(2,1)}, u32[]{:S(2)}) %copy-start.3) | copy-done | bytes 262168
  6.8 0.9 %shard_map.58 = (bf16[4,128,256]{2,1,0:T(8,128)(2,1)S(1)}, bf16[4,128,256]{2,1,0:T(8,128)(2,1)S(1)}) custom-call(s32[3]{0:T(128)S(1)} %pad_add_fusion.place, bf16[16,16,128]{2,1,0:T(8,128)(2,1)S(1)} %bitcast.93, bf16[2,16,32,128]{3,2,1,0:T(8,128)(2,1)S(1)} %copy-done.3), custom_call_target="tpu_custom_call" | custom-call | bytes 851980 | tf_op jit(solution)/shard_map/pallas_call | solution.py:192
  7.7 0.8 %shard_map.59.refs_3_.gt1_ref = bf16[4,128,256]{2,1,0:T(8,128)(2,1)S(1)} custom-call(s32[3]{0:T(128)S(1)} %pad_add_fusion.place, bf16[16,16,128]{2,1,0:T(8,128)(2,1)S(1)} %bitcast.95), custom_call_target="tpu_custom_call" | custom-call | bytes 327692 | tf_op jit(solution)/shard_map/pallas_call | solution.py:192
  8.6 1.6 %collective-permute-done.refs_1_ = bf16[2,16,32,128]{3,2,1,0:T(8,128)(2,1)S(1)} collective-permute-done((bf16[2,16,32,128]{3,2,1,0:T(8,128)(2,1)}, bf16[2,16,32,128]{3,2,1,0:T(8,128)(2,1)S(1)}, u32[]{:S(2)}, u32[]{:S(2)}) %collective-permute-start) | collective-permute-done | bytes 262176 | tf_op jit(solution)/shard_map/ppermute | solution.py:205
  10.2 0.4 shard_map.60
  10.6 0.2 fusion
  10.8 0.4 collective-permute-start.2
  11.2 0.4 shard_map.61
  11.6 1.2 %shard_map.63 = (f32[16,16,128]{2,1,0:T(8,128)S(1)}, f32[16,16,128]{2,1,0:T(8,128)S(1)}) custom-call(s32[3]{0:T(128)S(1)} %pad_add_fusion.place, bf16[4,256,256]{2,1,0:T(8,128)(2,1)S(1)} %get-tuple-element.33.class_ref, bf16[27,128,128]{2,1,0:T(8,128)(2,1)S(1)} %bitcast.91), custom_call_target="tpu_custom_call" | custom-call | flops 226492416 | bytes 1671180 | tf_op jit(solution)/shard_map/pallas_call | solution.py:192
  12.8 0.0 copy-start.2
  12.8 0.3 select_bitcast_fusion
  13.1 0.1 fusion.10
  13.4 1.8 %collective-permute-start.3 = (f16[28,3,8,128]{3,2,0,1:T(8,128)(2,1)S(1)}, f16[28,3,8,128]{3,2,0,1:T(8,128)(2,1)S(1)}, u32[]{:S(2)}, u32[]{:S(2)}) collective-permute-start(f16[28,3,8,128]{3,2,0,1:T(8,128)(2,1)S(1)} %copy.12), channel_id=1, source_target_pairs={{0,4},{2,6},{4,0},{6,2},{8,12},{10,14},{12,8},{14,10},{16,20},{18,... | collective-permute-start | bytes 516104 | tf_op jit(solution)/shard_map/ppermute | solution.py:205
  15.2 0.3 collective-permute-start.5
  15.5 1.2 %shard_map.62 = (f32[2,16,32,128]{3,2,1,0:T(8,128)S(1)}, f32[2,16,32,128]{3,2,1,0:T(8,128)S(1)}) custom-call(s32[3]{0:T(128)S(1)} %pad_add_fusion.place, bf16[16,16,128]{2,1,0:T(8,128)(2,1)S(1)} %bitcast.94, bf16[16,16,128]{2,1,0:T(8,128)(2,1)S(1)} %bitcast.96, bf16[27,128,128]{2,1,0:T(8,128)(2,1)S(1)} %bitcast.92), custom_call_target="tpu_custom_call" | custom-call | flops 226492416 | bytes 2064396 | tf_op jit(solution)/shard_map/pallas_call | solution.py:192
  16.7 3.8 %collective-permute-done.3 = f16[28,3,8,128]{3,2,0,1:T(8,128)(2,1)S(1)} collective-permute-done((f16[28,3,8,128]{3,2,0,1:T(8,128)(2,1)S(1)}, f16[28,3,8,128]{3,2,0,1:T(8,128)(2,1)S(1)}, u32[]{:S(2)}, u32[]{:S(2)}) %collective-permute-start.3) | collective-permute-done | bytes 172064 | tf_op jit(solution)/shard_map/ppermute | solution.py:205
  20.6 0.1 add_select_fusion.1
  20.7 0.1 fusion.12
  20.8 3.9 %collective-permute-start.4 = (f16[28,8,128]{2,1,0:T(8,128)(2,1)S(1)}, f16[28,8,128]{2,1,0:T(8,128)(2,1)S(1)}, u32[]{:S(2)}, u32[]{:S(2)}) collective-permute-start(f16[28,8,128]{2,1,0:T(8,128)(2,1)S(1)} %get-tuple-element.65), channel_id=1, source_target_pairs={{0,24},{2,26},{4,28},{6,30},{8,16},{10,18},{12,20},{14,22},{16,8},... | collective-permute-start | bytes 172040 | tf_op jit(solution)/shard_map/ppermute | solution.py:205
  24.7 0.6 %collective-permute-start.6 = (f16[28,8,128]{2,1,0:T(8,128)(2,1)S(1)}, f16[28,8,128]{2,1,0:T(8,128)(2,1)S(1)}, u32[]{:S(2)}, u32[]{:S(2)}) collective-permute-start(f16[28,8,128]{2,1,0:T(8,128)(2,1)S(1)} %get-tuple-element.63), channel_id=1, source_target_pairs={{0,8},{2,10},{4,12},{6,14},{8,0},{10,2},{12,4},{14,6},{16,24},{18,... | collective-permute-start | bytes 172040 | tf_op jit(solution)/shard_map/ppermute | solution.py:205
  25.3 1.8 %collective-permute-done.4 = f16[28,8,128]{2,1,0:T(8,128)(2,1)S(1)} collective-permute-done((f16[28,8,128]{2,1,0:T(8,128)(2,1)S(1)}, f16[28,8,128]{2,1,0:T(8,128)(2,1)S(1)}, u32[]{:S(2)}, u32[]{:S(2)}) %collective-permute-start.4) | collective-permute-done | bytes 57376 | tf_op jit(solution)/shard_map/ppermute | solution.py:205
  27.2 2.6 %collective-permute-done.7 = f16[28,8,128]{2,1,0:T(8,128)(2,1)S(1)} collective-permute-done((f16[28,8,128]{2,1,0:T(8,128)(2,1)S(1)}, f16[28,8,128]{2,1,0:T(8,128)(2,1)S(1)}, u32[]{:S(2)}, u32[]{:S(2)}) %collective-permute-start.7) | collective-permute-done | bytes 57376 | tf_op jit(solution)/shard_map/ppermute | solution.py:205
  29.9 0.2 multiply_select_fusion.10
  30.1 0.1 fusion.14
  30.2 1.9 %collective-permute-start.10 = (f16[28,8,128]{2,1,0:T(8,128)(2,1)S(1)}, f16[28,8,128]{2,1,0:T(8,128)(2,1)S(1)}, u32[]{:S(2)}, u32[]{:S(2)}) collective-permute-start(f16[28,8,128]{2,1,0:T(8,128)(2,1)S(1)} %fusion.14), channel_id=1, source_target_pairs={{0,24},{2,26},{4,28},{6,30},{8,16},{10,18},{12,20},{14,22},{16,8},... | collective-permute-start | bytes 172040 | tf_op jit(solution)/shard_map/ppermute | solution.py:205
  32.1 0.7 %collective-permute-start.9 = (f16[28,8,128]{2,1,0:T(8,128)(2,1)S(1)}, f16[28,8,128]{2,1,0:T(8,128)(2,1)S(1)}, u32[]{:S(2)}, u32[]{:S(2)}) collective-permute-start(f16[28,8,128]{2,1,0:T(8,128)(2,1)S(1)} %fusion.14), channel_id=1, source_target_pairs={{0,8},{2,10},{4,12},{6,14},{8,0},{10,2},{12,4},{14,6},{16,24},{18,... | collective-permute-start | bytes 172040 | tf_op jit(solution)/shard_map/ppermute | solution.py:205
  32.7 1.9 %collective-permute-start.8 = (f16[28,8,128]{2,1,0:T(8,128)(2,1)S(1)}, f16[28,8,128]{2,1,0:T(8,128)(2,1)S(1)}, u32[]{:S(2)}, u32[]{:S(2)}) collective-permute-start(f16[28,8,128]{2,1,0:T(8,128)(2,1)S(1)} %fusion.14), channel_id=1, source_target_pairs={{0,16},{2,18},{4,20},{6,22},{8,24},{10,26},{12,28},{14,30},{16,0},... | collective-permute-start | bytes 172040 | tf_op jit(solution)/shard_map/ppermute | solution.py:205
  34.6 1.5 %collective-permute-start.14 = (f32[2,16,32,128]{3,2,1,0:T(8,128)S(1)}, f32[2,16,32,128]{3,2,1,0:T(8,128)S(1)}, u32[]{:S(2)}, u32[]{:S(2)}) collective-permute-start(f32[2,16,32,128]{3,2,1,0:T(8,128)S(1)} %get-tuple-element.53), channel_id=1, source_target_pairs={{0,1},{1,0},{2,3},{3,2},{4,5},{5,4},{6,7},{7,6},{8,9},{9,8},{10,11... | collective-permute-start | bytes 1572872 | tf_op jit(solution)/shard_map/ppermute | solution.py:205
  36.2 0.7 %collective-permute-done.9 = f16[28,8,128]{2,1,0:T(8,128)(2,1)S(1)} collective-permute-done((f16[28,8,128]{2,1,0:T(8,128)(2,1)S(1)}, f16[28,8,128]{2,1,0:T(8,128)(2,1)S(1)}, u32[]{:S(2)}, u32[]{:S(2)}) %collective-permute-start.9) | collective-permute-done | bytes 57376 | tf_op jit(solution)/shard_map/ppermute | solution.py:205
  36.8 1.0 %collective-permute-done.8 = f16[28,8,128]{2,1,0:T(8,128)(2,1)S(1)} collective-permute-done((f16[28,8,128]{2,1,0:T(8,128)(2,1)S(1)}, f16[28,8,128]{2,1,0:T(8,128)(2,1)S(1)}, u32[]{:S(2)}, u32[]{:S(2)}) %collective-permute-start.8) | collective-permute-done | bytes 57376 | tf_op jit(solution)/shard_map/ppermute | solution.py:205
  37.8 0.2 select_select_fusion
  38.0 1.6 %collective-permute-start.11 = (f16[28,4,8,128]{3,2,1,0:T(8,128)(2,1)S(1)}, f16[28,4,8,128]{3,2,1,0:T(8,128)(2,1)S(1)}, u32[]{:S(2)}, u32[]{:S(2)}) collective-permute-start(f16[28,4,8,128]{3,2,1,0:T(8,128)(2,1)S(1)} %select_select_fusion), channel_id=1, source_target_pairs={{0,4},{2,6},{4,0},{6,2},{8,12},{10,14},{12,8},{14,10},{16,20},{18,... | collective-permute-start | bytes 688136 | tf_op jit(solution)/shard_map/ppermute | solution.py:205
  39.6 0.1 collective-permute-start.15
  39.6 2.4 %collective-permute-start.13 = (f32[16,16,128]{2,1,0:T(8,128)S(1)}, f32[16,16,128]{2,1,0:T(8,128)S(1)}, u32[]{:S(2)}, u32[]{:S(2)}) collective-permute-start(f32[16,16,128]{2,1,0:T(8,128)S(1)} %get-tuple-element.52), channel_id=1, source_target_pairs={{0,2},{2,4},{4,6},{6,8},{8,10},{10,12},{12,14},{14,16},{16,18},{18... | collective-permute-start | bytes 393224 | tf_op jit(solution)/shard_map/ppermute | solution.py:210
  42.0 0.2 broadcast_in_dim.47
  42.2 0.1 fusion.3
  42.4 1.7 %collective-permute-done.11 = f16[28,4,8,128]{3,2,1,0:T(8,128)(2,1)S(1)} collective-permute-done((f16[28,4,8,128]{3,2,1,0:T(8,128)(2,1)S(1)}, f16[28,4,8,128]{3,2,1,0:T(8,128)(2,1)S(1)}, u32[]{:S(2)}, u32[]{:S(2)}) %collective-permute-start.11) | collective-permute-done | bytes 229408 | tf_op jit(solution)/shard_map/ppermute | solution.py:205
  44.1 0.1 fusion.5
  44.3 0.1 fusion.7
  44.4 1.2 %collective-permute-done.12 = f16[28,4,8,128]{3,2,1,0:T(8,128)(2,1)S(1)} collective-permute-done((f16[28,4,8,128]{3,2,1,0:T(8,128)(2,1)S(1)}, f16[28,4,8,128]{3,2,1,0:T(8,128)(2,1)S(1)}, u32[]{:S(2)}, u32[]{:S(2)}) %collective-permute-start.12) | collective-permute-done | bytes 229408 | tf_op jit(solution)/shard_map/ppermute | solution.py:205
  45.6 0.1 fusion.9
  45.7 0.0 copy-start.4
  45.7 0.9 %shard_map.64 = (bf16[16,16,128]{2,1,0:T(8,128)(2,1)}, bf16[2,16,32,128]{3,2,1,0:T(8,128)(2,1)}) custom-call(f32[16,16,128]{2,1,0:T(8,128)S(1)} %get-tuple-element.43.own_ref, f32[16,16,128]{2,1,0:T(8,128)S(1)} %collective-permute-done.13.below_ref, f32[2,16,32,128]{3,2,1,0:T(8,128)S(1)} %get-tuple-element.55.part_ref, ...), custom_call_target="tpu_custom_call" | custom-call | bytes 1638400 | tf_op jit(solution)/shard_map/pallas_call | solution.py:192
  46.6 0.4 copy-done.4
  (34 shorter events, 0.3 us)
Async XLA Ops:
  0.6 9.6 %collective-permute-start = (bf16[2,16,32,128]{3,2,1,0:T(8,128)(2,1)}, bf16[2,16,32,128]{3,2,1,0:T(8,128)(2,1)S(1)}, u32[]{:S(2)}, u32[]{:S(2)}) collective-permute-start(bf16[2,16,32,128]{3,2,1,0:T(8,128)(2,1)} %volume_ref.1), channel_id=1, source_target_pairs={{0,1},{1,0},{2,3},{3,2},{4,5},{5,4},{6,7},{7,6},{8,9},{9,8},{10,11... | collective-permute-start | bytes 786440 | tf_op jit(solution)/shard_map/ppermute | solution.py:205
  3.7 4.0 %collective-permute-start.1 = (bf16[1,16,16,128]{3,2,1,0:T(8,128)(2,1)}, bf16[1,16,16,128]{3,2,1,0:T(8,128)(2,1)S(1)}, u32[]{:S(2)}, u32[]{:S(2)}) collective-permute-start(bf16[1,16,16,128]{3,2,1,0:T(8,128)(2,1)} %param.5), channel_id=1, source_target_pairs={{2,0},{4,2},{6,4},{8,6},{10,8},{12,10},{14,12},{16,14},{18,16},{20... | collective-permute-start | bytes 196616 | tf_op jit(solution)/shard_map/ppermute | solution.py:210
  5.0 0.8 %copy-start.1 = (bf16[1,16,16,128]{3,2,1,0:T(8,128)(2,1)S(1)}, bf16[1,16,16,128]{3,2,1,0:T(8,128)(2,1)}, u32[]{:S(2)}) copy-start(bf16[1,16,16,128]{3,2,1,0:T(8,128)(2,1)} %param.5) | copy-start | bytes 196612
  5.9 0.9 %copy-start.3 = (bf16[2,16,32,128]{3,2,1,0:T(8,128)(2,1)S(1)}, bf16[2,16,32,128]{3,2,1,0:T(8,128)(2,1)}, u32[]{:S(2)}) copy-start(bf16[2,16,32,128]{3,2,1,0:T(8,128)(2,1)} %volume_ref.1) | copy-start | bytes 786436
  10.2 1.4 %copy-start = (bf16[3,3,3,128,128]{4,3,2,1,0:T(8,128)(2,1)S(1)}, bf16[3,3,3,128,128]{4,3,2,1,0:T(8,128)(2,1)}, u32[]{:S(2)}) copy-start(bf16[3,3,3,128,128]{4,3,2,1,0:T(8,128)(2,1)} %param.4) | copy-start | bytes 2654212
  10.8 2.0 %collective-permute-start.2 = (f16[28,64,128]{2,1,0:T(8,128)(2,1)S(1)}, f16[28,64,128]{2,1,0:T(8,128)(2,1)S(1)}, u32[]{:S(2)}, u32[]{:S(2)}) collective-permute-start(f16[28,64,128]{2,1,0:T(8,128)(2,1)S(1)} %fusion), channel_id=1, source_target_pairs={{0,2},{2,0},{4,6},{6,4},{8,10},{10,8},{12,14},{14,12},{16,18},{18,... | collective-permute-start | bytes 1376264 | tf_op jit(solution)/shard_map/ppermute | solution.py:205
  12.8 2.7 %copy-start.2 = (bf16[1,16,16,128]{3,2,1,0:T(8,128)(2,1)S(1)}, bf16[1,16,16,128]{3,2,1,0:T(8,128)(2,1)}, u32[]{:S(2)}) copy-start(bf16[1,16,16,128]{3,2,1,0:T(8,128)(2,1)} %param.5) | copy-start | bytes 196612
  13.4 7.2 %collective-permute-start.3 = (f16[28,3,8,128]{3,2,0,1:T(8,128)(2,1)S(1)}, f16[28,3,8,128]{3,2,0,1:T(8,128)(2,1)S(1)}, u32[]{:S(2)}, u32[]{:S(2)}) collective-permute-start(f16[28,3,8,128]{3,2,0,1:T(8,128)(2,1)S(1)} %copy.12), channel_id=1, source_target_pairs={{0,4},{2,6},{4,0},{6,2},{8,12},{10,14},{12,8},{14,10},{16,20},{18,... | collective-permute-start | bytes 516104 | tf_op jit(solution)/shard_map/ppermute | solution.py:205
  15.2 12.0 %collective-permute-start.5 = (f16[28,8,128]{2,1,0:T(8,128)(2,1)S(1)}, f16[28,8,128]{2,1,0:T(8,128)(2,1)S(1)}, u32[]{:S(2)}, u32[]{:S(2)}) collective-permute-start(f16[28,8,128]{2,1,0:T(8,128)(2,1)S(1)} %slice_bitcast_fusion.4), channel_id=1, source_target_pairs={{0,4},{2,6},{4,0},{6,2},{8,12},{10,14},{12,8},{14,10},{16,20},{18,... | collective-permute-start | bytes 172040 | tf_op jit(solution)/shard_map/ppermute | solution.py:205
  20.8 6.4 %collective-permute-start.4 = (f16[28,8,128]{2,1,0:T(8,128)(2,1)S(1)}, f16[28,8,128]{2,1,0:T(8,128)(2,1)S(1)}, u32[]{:S(2)}, u32[]{:S(2)}) collective-permute-start(f16[28,8,128]{2,1,0:T(8,128)(2,1)S(1)} %get-tuple-element.65), channel_id=1, source_target_pairs={{0,24},{2,26},{4,28},{6,30},{8,16},{10,18},{12,20},{14,22},{16,8},... | collective-permute-start | bytes 172040 | tf_op jit(solution)/shard_map/ppermute | solution.py:205
  24.7 5.2 %collective-permute-start.7 = (f16[28,8,128]{2,1,0:T(8,128)(2,1)S(1)}, f16[28,8,128]{2,1,0:T(8,128)(2,1)S(1)}, u32[]{:S(2)}, u32[]{:S(2)}) collective-permute-start(f16[28,8,128]{2,1,0:T(8,128)(2,1)S(1)} %get-tuple-element.64), channel_id=1, source_target_pairs={{0,16},{2,18},{4,20},{6,22},{8,24},{10,26},{12,28},{14,30},{16,0},... | collective-permute-start | bytes 172040 | tf_op jit(solution)/shard_map/ppermute | solution.py:205
  24.7 5.2 %collective-permute-start.6 = (f16[28,8,128]{2,1,0:T(8,128)(2,1)S(1)}, f16[28,8,128]{2,1,0:T(8,128)(2,1)S(1)}, u32[]{:S(2)}, u32[]{:S(2)}) collective-permute-start(f16[28,8,128]{2,1,0:T(8,128)(2,1)S(1)} %get-tuple-element.63), channel_id=1, source_target_pairs={{0,8},{2,10},{4,12},{6,14},{8,0},{10,2},{12,4},{14,6},{16,24},{18,... | collective-permute-start | bytes 172040 | tf_op jit(solution)/shard_map/ppermute | solution.py:205
  30.2 6.7 %collective-permute-start.10 = (f16[28,8,128]{2,1,0:T(8,128)(2,1)S(1)}, f16[28,8,128]{2,1,0:T(8,128)(2,1)S(1)}, u32[]{:S(2)}, u32[]{:S(2)}) collective-permute-start(f16[28,8,128]{2,1,0:T(8,128)(2,1)S(1)} %fusion.14), channel_id=1, source_target_pairs={{0,24},{2,26},{4,28},{6,30},{8,16},{10,18},{12,20},{14,22},{16,8},... | collective-permute-start | bytes 172040 | tf_op jit(solution)/shard_map/ppermute | solution.py:205
  32.1 4.8 %collective-permute-start.9 = (f16[28,8,128]{2,1,0:T(8,128)(2,1)S(1)}, f16[28,8,128]{2,1,0:T(8,128)(2,1)S(1)}, u32[]{:S(2)}, u32[]{:S(2)}) collective-permute-start(f16[28,8,128]{2,1,0:T(8,128)(2,1)S(1)} %fusion.14), channel_id=1, source_target_pairs={{0,8},{2,10},{4,12},{6,14},{8,0},{10,2},{12,4},{14,6},{16,24},{18,... | collective-permute-start | bytes 172040 | tf_op jit(solution)/shard_map/ppermute | solution.py:205
  32.7 5.1 %collective-permute-start.8 = (f16[28,8,128]{2,1,0:T(8,128)(2,1)S(1)}, f16[28,8,128]{2,1,0:T(8,128)(2,1)S(1)}, u32[]{:S(2)}, u32[]{:S(2)}) collective-permute-start(f16[28,8,128]{2,1,0:T(8,128)(2,1)S(1)} %fusion.14), channel_id=1, source_target_pairs={{0,16},{2,18},{4,20},{6,22},{8,24},{10,26},{12,28},{14,30},{16,0},... | collective-permute-start | bytes 172040 | tf_op jit(solution)/shard_map/ppermute | solution.py:205
  34.6 11.1 %collective-permute-start.14 = (f32[2,16,32,128]{3,2,1,0:T(8,128)S(1)}, f32[2,16,32,128]{3,2,1,0:T(8,128)S(1)}, u32[]{:S(2)}, u32[]{:S(2)}) collective-permute-start(f32[2,16,32,128]{3,2,1,0:T(8,128)S(1)} %get-tuple-element.53), channel_id=1, source_target_pairs={{0,1},{1,0},{2,3},{3,2},{4,5},{5,4},{6,7},{7,6},{8,9},{9,8},{10,11... | collective-permute-start | bytes 1572872 | tf_op jit(solution)/shard_map/ppermute | solution.py:205
  38.0 6.1 %collective-permute-start.11 = (f16[28,4,8,128]{3,2,1,0:T(8,128)(2,1)S(1)}, f16[28,4,8,128]{3,2,1,0:T(8,128)(2,1)S(1)}, u32[]{:S(2)}, u32[]{:S(2)}) collective-permute-start(f16[28,4,8,128]{3,2,1,0:T(8,128)(2,1)S(1)} %select_select_fusion), channel_id=1, source_target_pairs={{0,4},{2,6},{4,0},{6,2},{8,12},{10,14},{12,8},{14,10},{16,20},{18,... | collective-permute-start | bytes 688136 | tf_op jit(solution)/shard_map/ppermute | solution.py:205
  39.6 4.5 %collective-permute-start.15 = (f16[28,4,8,128]{3,2,1,0:T(8,128)(2,1)S(1)}, f16[28,4,8,128]{3,2,1,0:T(8,128)(2,1)S(1)}, u32[]{:S(2)}, u32[]{:S(2)}) collective-permute-start(f16[28,4,8,128]{3,2,1,0:T(8,128)(2,1)S(1)} %select_select_fusion), channel_id=1, source_target_pairs={{0,2},{2,0},{4,6},{6,4},{8,10},{10,8},{12,14},{14,12},{16,18},{18,... | collective-permute-start | bytes 688136 | tf_op jit(solution)/shard_map/ppermute | solution.py:205
  39.6 6.1 %collective-permute-start.13 = (f32[16,16,128]{2,1,0:T(8,128)S(1)}, f32[16,16,128]{2,1,0:T(8,128)S(1)}, u32[]{:S(2)}, u32[]{:S(2)}) collective-permute-start(f32[16,16,128]{2,1,0:T(8,128)S(1)} %get-tuple-element.52), channel_id=1, source_target_pairs={{0,2},{2,4},{4,6},{6,8},{8,10},{10,12},{12,14},{14,16},{16,18},{18... | collective-permute-start | bytes 393224 | tf_op jit(solution)/shard_map/ppermute | solution.py:210
  44.1 1.5 %collective-permute-start.12 = (f16[28,4,8,128]{3,2,1,0:T(8,128)(2,1)S(1)}, f16[28,4,8,128]{3,2,1,0:T(8,128)(2,1)S(1)}, u32[]{:S(2)}, u32[]{:S(2)}) collective-permute-start(f16[28,4,8,128]{3,2,1,0:T(8,128)(2,1)S(1)} %collective-permute-done.11), channel_id=1, source_target_pairs={{0,2},{2,0},{4,6},{6,4},{8,10},{10,8},{12,14},{14,12},{16,18},{18,... | collective-permute-start | bytes 688136 | tf_op jit(solution)/shard_map/ppermute | solution.py:205
  45.7 1.3 %copy-start.4 = (f32[27,2,2,4,8,128]{5,4,3,2,1,0:T(8,128)}, f32[27,2,2,4,8,128]{5,4,3,2,1,0:T(8,128)S(1)}, u32[]{:S(2)}) copy-start(f32[27,2,2,4,8,128]{5,4,3,2,1,0:T(8,128)S(1)} %fusion.9) | copy-start | bytes 5308420

commit v6 on v5

--- a/solution.py
+++ b/solution.py
@@ -222,8 +222,15 @@
     return jnp.where(is_level(x), x.astype(F32), x.astype(F32) * jnp.exp2(x[TAPS:].astype(F32) - TOP))
 
 
-def add(x, y):
-    return jnp.where(is_level(x), jnp.maximum(x, y) + 1.0, x + y)
+def merge(x, arrived, factor=1.0):
+    level = x[TAPS:]
+    for piece in arrived:
+        level = jnp.maximum(level, piece[TAPS:].astype(F32))
+    level = level + float(len(arrived))
+    total = x * (jnp.exp2(TOP - level) * factor)
+    for piece in arrived:
+        total = total + piece.astype(F32) * (jnp.exp2(piece[TAPS:].astype(F32) - level) * factor)
+    return jnp.where(is_level(x), level, total).astype(F16)
 
 
 def arrange(pieces, mine):
@@ -240,16 +247,15 @@
     quarter, cin = near.shape[1:]
     shape = (TAPS + 1, nz, quarter // nz, cin)
     got = beside("core", swap(encode(far), "space", 1))
-    sent = encode(add(mid, decode(got[:, quarter:]))).reshape(shape)
-    near = add(near, decode(got[:, :quarter])).reshape(shape)
+    here, there = jnp.split(got.reshape((TAPS + 1, 2) + shape[1:]), 2, axis=1)
+    here, there = here[:, 0], there[:, 0]
+    near, mid = near.reshape(shape), mid.reshape(shape)
+    sent = merge(mid, [there])
     own, got = swap(sent[:, 0], "space", 2), beside("x", swap(sent[:, 1:], "space", 2))
-    total = add(near[:, 1:], decode(got))
-    got = {q: beside(f"z{q}", swap(encode(total[:, q - 1]), "space", 4 * q)) for q in range(1, nz)}
+    ready = {q: merge(near[:, q], [here[:, q], got[:, q - 1]]) for q in range(1, nz)}
+    got = {q: beside(f"z{q}", swap(ready[q], "space", 4 * q)) for q in range(1, nz)}
     got[nz - 1], own = lax.optimization_barrier((got[nz - 1], own))
-    total = add(near[:, 0], decode(own))
-    for q in got:
-        total = add(total, decode(got[q]))
-    total = beside("z", encode(jnp.where(is_level(total), total, total * factor)))
+    total = beside("z", merge(near[:, 0], [here[:, 0], own] + [got[q] for q in got], factor))
     total = arrange([total] + [beside(f"a{q}", swap(total, "space", 4 * q)) for q in range(1, nz)], z)
     total = beside("back", total)
     across = swap(total, "space", 2)

time: 47.3 us -> 46.9 us (level)
  transfers between devices with their start and end apart: 16 -> 16, of which waited for: 8 -> 8; matrix products, arithmetic and copies ran while one was open for 3% -> 3% of each run, Pallas kernels for 9% -> 10%
where the time goes in v6:
time: 46.9 us; the launch traced here: 46.6 us
  starting transfers between devices  21.3 us (45%)
  waiting for transfers between devices  14.6 us (31%)
  Pallas kernels  5.76 us (12%)
  local copies, waits for them, and re-layouts  2.55 us (5%)
  other arithmetic  1.55 us (3%)
  between operations  0.95 us (2%)
    ppermute x14, starting transfers between devices, swap(): return lax.ppermute(x, axis, [(i, i ^ bits) for i in range(peers)])  17.6 us
    ppermute x14, waiting for transfers between devices, swap(): return lax.ppermute(x, axis, [(i, i ^ bits) for i in range(peers)])  14.6 us
    pallas_call x7, Pallas kernels, call(): pl.pallas_call(kernel, out_shape=out_shape, in_specs=[smem if placed and...  5.76 us
    ppermute x2, starting transfers between devices, move(): lax.ppermute(x, axis, [(i, i + by) for i in range(peers) if 0 <= i + by <...  3.68 us
    unnamed x11, local copies, waits for them, and re-layouts  2.24 us
  transfers between devices with their start and end apart: 16, of which 8 were waited for; matrix products, arithmetic and copies ran while one was open for 3% of the time, Pallas kernels for 10%

profile of v6, /device:TPU:0, one launch (start us, length us, event | category | flops | bytes accessed | tf_op | source)
XLA Modules:
  0.0 46.6 jit_solution(14093902660088215653)
XLA Ops:
  0.6 3.0 %collective-permute-start = (bf16[2,16,32,128]{3,2,1,0:T(8,128)(2,1)}, bf16[2,16,32,128]{3,2,1,0:T(8,128)(2,1)S(1)}, u32[]{:S(2)}, u32[]{:S(2)}) collective-permute-start(bf16[2,16,32,128]{3,2,1,0:T(8,128)(2,1)} %volume_ref.1), channel_id=1, source_target_pairs={{0,1},{1,0},{2,3},{3,2},{4,5},{5,4},{6,7},{7,6},{8,9},{9,8},{10,11... | collective-permute-start | bytes 786440 | tf_op jit(solution)/shard_map/ppermute | solution.py:205
  3.7 1.3 %collective-permute-start.1 = (bf16[1,16,16,128]{3,2,1,0:T(8,128)(2,1)}, bf16[1,16,16,128]{3,2,1,0:T(8,128)(2,1)S(1)}, u32[]{:S(2)}, u32[]{:S(2)}) collective-permute-start(bf16[1,16,16,128]{3,2,1,0:T(8,128)(2,1)} %param.5), channel_id=1, source_target_pairs={{2,0},{4,2},{6,4},{8,6},{10,8},{12,10},{14,12},{16,14},{18,16},{20... | collective-permute-start | bytes 196616 | tf_op jit(solution)/shard_map/ppermute | solution.py:210
  5.0 0.1 pad_add_fusion.place
  5.0 0.8 %copy-done.1 = bf16[1,16,16,128]{3,2,1,0:T(8,128)(2,1)S(1)} copy-done((bf16[1,16,16,128]{3,2,1,0:T(8,128)(2,1)S(1)}, bf16[1,16,16,128]{3,2,1,0:T(8,128)(2,1)}, u32[]{:S(2)}) %copy-start.1) | copy-done | bytes 65560
  5.9 0.9 %copy-done.3 = bf16[2,16,32,128]{3,2,1,0:T(8,128)(2,1)S(1)} copy-done((bf16[2,16,32,128]{3,2,1,0:T(8,128)(2,1)S(1)}, bf16[2,16,32,128]{3,2,1,0:T(8,128)(2,1)}, u32[]{:S(2)}) %copy-start.3) | copy-done | bytes 262168
  6.8 0.9 %shard_map.58 = (bf16[4,128,256]{2,1,0:T(8,128)(2,1)S(1)}, bf16[4,128,256]{2,1,0:T(8,128)(2,1)S(1)}) custom-call(s32[3]{0:T(128)S(1)} %pad_add_fusion.place, bf16[16,16,128]{2,1,0:T(8,128)(2,1)S(1)} %bitcast.261, bf16[2,16,32,128]{3,2,1,0:T(8,128)(2,1)S(1)} %copy-done.3), custom_call_target="tpu_custom_call" | custom-call | bytes 851980 | tf_op jit(solution)/shard_map/pallas_call | solution.py:192
  7.7 0.0 collective-permute-done.1
  7.7 0.8 %shard_map.59.refs_3_.gt1_ref = bf16[4,128,256]{2,1,0:T(8,128)(2,1)S(1)} custom-call(s32[3]{0:T(128)S(1)} %pad_add_fusion.place, bf16[16,16,128]{2,1,0:T(8,128)(2,1)S(1)} %bitcast.263), custom_call_target="tpu_custom_call" | custom-call | bytes 327692 | tf_op jit(solution)/shard_map/pallas_call | solution.py:192
  8.6 1.6 %collective-permute-done.refs_1_ = bf16[2,16,32,128]{3,2,1,0:T(8,128)(2,1)S(1)} collective-permute-done((bf16[2,16,32,128]{3,2,1,0:T(8,128)(2,1)}, bf16[2,16,32,128]{3,2,1,0:T(8,128)(2,1)S(1)}, u32[]{:S(2)}, u32[]{:S(2)}) %collective-permute-start) | collective-permute-done | bytes 262176 | tf_op jit(solution)/shard_map/ppermute | solution.py:205
  10.2 0.4 shard_map.60
  10.6 0.2 fusion
  10.8 0.4 collective-permute-start.2
  11.2 0.4 shard_map.61
  11.6 0.0 copy-start.2
  11.6 1.2 %shard_map.63 = (f32[16,16,128]{2,1,0:T(8,128)S(1)}, f32[16,16,128]{2,1,0:T(8,128)S(1)}) custom-call(s32[3]{0:T(128)S(1)} %pad_add_fusion.place, bf16[4,256,256]{2,1,0:T(8,128)(2,1)S(1)} %get-tuple-element.33.class_ref, bf16[27,128,128]{2,1,0:T(8,128)(2,1)S(1)} %bitcast.254), custom_call_target="tpu_custom_call" | custom-call | flops 226492416 | bytes 1671180 | tf_op jit(solution)/shard_map/pallas_call | solution.py:192
  12.8 0.1 fusion.3
  13.1 1.8 %collective-permute-start.3 = (f16[28,3,8,128]{3,2,0,1:T(8,128)(2,1)S(1)}, f16[28,3,8,128]{3,2,0,1:T(8,128)(2,1)S(1)}, u32[]{:S(2)}, u32[]{:S(2)}) collective-permute-start(f16[28,3,8,128]{3,2,0,1:T(8,128)(2,1)S(1)} %copy.21), channel_id=1, source_target_pairs={{0,4},{2,6},{4,0},{6,2},{8,12},{10,14},{12,8},{14,10},{16,20},{18,... | collective-permute-start | bytes 516104 | tf_op jit(solution)/shard_map/ppermute | solution.py:205
  14.9 0.2 collective-permute-start.5
  15.2 1.2 %shard_map.62 = (f32[2,16,32,128]{3,2,1,0:T(8,128)S(1)}, f32[2,16,32,128]{3,2,1,0:T(8,128)S(1)}) custom-call(s32[3]{0:T(128)S(1)} %pad_add_fusion.place, bf16[16,16,128]{2,1,0:T(8,128)(2,1)S(1)} %bitcast.262, bf16[16,16,128]{2,1,0:T(8,128)(2,1)S(1)} %bitcast.264, bf16[27,128,128]{2,1,0:T(8,128)(2,1)S(1)} %bitcast.255), custom_call_target="tpu_custom_call" | custom-call | flops 226492416 | bytes 2064396 | tf_op jit(solution)/shard_map/pallas_call | solution.py:192
  16.4 3.8 %collective-permute-done.3 = f16[28,3,8,128]{3,2,0,1:T(8,128)(2,1)S(1)} collective-permute-done((f16[28,3,8,128]{3,2,0,1:T(8,128)(2,1)S(1)}, f16[28,3,8,128]{3,2,0,1:T(8,128)(2,1)S(1)}, u32[]{:S(2)}, u32[]{:S(2)}) %collective-permute-start.3) | collective-permute-done | bytes 172064 | tf_op jit(solution)/shard_map/ppermute | solution.py:205
  20.3 0.1 fusion.34
  20.4 3.8 %collective-permute-start.4 = (f16[28,8,128]{2,1,0:T(8,128)(2,1)S(1)}, f16[28,8,128]{2,1,0:T(8,128)(2,1)S(1)}, u32[]{:S(2)}, u32[]{:S(2)}) collective-permute-start(f16[28,8,128]{2,1,0:T(8,128)(2,1)S(1)} %fusion.34), channel_id=1, source_target_pairs={{0,24},{2,26},{4,28},{6,30},{8,16},{10,18},{12,20},{14,22},{16,8},... | collective-permute-start | bytes 172040 | tf_op jit(solution)/shard_map/ppermute | solution.py:205
  24.3 0.1 fusion.29
  24.4 0.1 collective-permute-start.7
  24.5 0.6 %collective-permute-start.6 = (f16[28,8,128]{2,1,0:T(8,128)(2,1)S(1)}, f16[28,8,128]{2,1,0:T(8,128)(2,1)S(1)}, u32[]{:S(2)}, u32[]{:S(2)}) collective-permute-start(f16[28,8,128]{2,1,0:T(8,128)(2,1)S(1)} %get-tuple-element.69), channel_id=1, source_target_pairs={{0,8},{2,10},{4,12},{6,14},{8,0},{10,2},{12,4},{14,6},{16,24},{18,... | collective-permute-start | bytes 172040 | tf_op jit(solution)/shard_map/ppermute | solution.py:205
  25.1 2.0 %collective-permute-done.4 = f16[28,8,128]{2,1,0:T(8,128)(2,1)S(1)} collective-permute-done((f16[28,8,128]{2,1,0:T(8,128)(2,1)S(1)}, f16[28,8,128]{2,1,0:T(8,128)(2,1)S(1)}, u32[]{:S(2)}, u32[]{:S(2)}) %collective-permute-start.4) | collective-permute-done | bytes 57376 | tf_op jit(solution)/shard_map/ppermute | solution.py:205
  27.0 2.6 %collective-permute-done.7 = f16[28,8,128]{2,1,0:T(8,128)(2,1)S(1)} collective-permute-done((f16[28,8,128]{2,1,0:T(8,128)(2,1)S(1)}, f16[28,8,128]{2,1,0:T(8,128)(2,1)S(1)}, u32[]{:S(2)}, u32[]{:S(2)}) %collective-permute-start.7) | collective-permute-done | bytes 57376 | tf_op jit(solution)/shard_map/ppermute | solution.py:205
  29.7 0.1 fusion.19
  29.8 1.8 %collective-permute-start.10 = (f16[28,8,128]{2,1,0:T(8,128)(2,1)S(1)}, f16[28,8,128]{2,1,0:T(8,128)(2,1)S(1)}, u32[]{:S(2)}, u32[]{:S(2)}) collective-permute-start(f16[28,8,128]{2,1,0:T(8,128)(2,1)S(1)} %fusion.19), channel_id=1, source_target_pairs={{0,24},{2,26},{4,28},{6,30},{8,16},{10,18},{12,20},{14,22},{16,8},... | collective-permute-start | bytes 172040 | tf_op jit(solution)/shard_map/ppermute | solution.py:205
  31.5 0.8 %collective-permute-start.9 = (f16[28,8,128]{2,1,0:T(8,128)(2,1)S(1)}, f16[28,8,128]{2,1,0:T(8,128)(2,1)S(1)}, u32[]{:S(2)}, u32[]{:S(2)}) collective-permute-start(f16[28,8,128]{2,1,0:T(8,128)(2,1)S(1)} %fusion.19), channel_id=1, source_target_pairs={{0,8},{2,10},{4,12},{6,14},{8,0},{10,2},{12,4},{14,6},{16,24},{18,... | collective-permute-start | bytes 172040 | tf_op jit(solution)/shard_map/ppermute | solution.py:205
  32.3 1.9 %collective-permute-start.8 = (f16[28,8,128]{2,1,0:T(8,128)(2,1)S(1)}, f16[28,8,128]{2,1,0:T(8,128)(2,1)S(1)}, u32[]{:S(2)}, u32[]{:S(2)}) collective-permute-start(f16[28,8,128]{2,1,0:T(8,128)(2,1)S(1)} %fusion.19), channel_id=1, source_target_pairs={{0,16},{2,18},{4,20},{6,22},{8,24},{10,26},{12,28},{14,30},{16,0},... | collective-permute-start | bytes 172040 | tf_op jit(solution)/shard_map/ppermute | solution.py:205
  34.2 1.5 %collective-permute-start.14 = (f32[2,16,32,128]{3,2,1,0:T(8,128)S(1)}, f32[2,16,32,128]{3,2,1,0:T(8,128)S(1)}, u32[]{:S(2)}, u32[]{:S(2)}) collective-permute-start(f32[2,16,32,128]{3,2,1,0:T(8,128)S(1)} %get-tuple-element.53), channel_id=1, source_target_pairs={{0,1},{1,0},{2,3},{3,2},{4,5},{5,4},{6,7},{7,6},{8,9},{9,8},{10,11... | collective-permute-start | bytes 1572872 | tf_op jit(solution)/shard_map/ppermute | solution.py:205
  35.8 0.6 %collective-permute-done.9 = f16[28,8,128]{2,1,0:T(8,128)(2,1)S(1)} collective-permute-done((f16[28,8,128]{2,1,0:T(8,128)(2,1)S(1)}, f16[28,8,128]{2,1,0:T(8,128)(2,1)S(1)}, u32[]{:S(2)}, u32[]{:S(2)}) %collective-permute-start.9) | collective-permute-done | bytes 57376 | tf_op jit(solution)/shard_map/ppermute | solution.py:205
  36.4 1.1 %collective-permute-done.8 = f16[28,8,128]{2,1,0:T(8,128)(2,1)S(1)} collective-permute-done((f16[28,8,128]{2,1,0:T(8,128)(2,1)S(1)}, f16[28,8,128]{2,1,0:T(8,128)(2,1)S(1)}, u32[]{:S(2)}, u32[]{:S(2)}) %collective-permute-start.8) | collective-permute-done | bytes 57376 | tf_op jit(solution)/shard_map/ppermute | solution.py:205
  37.4 0.2 select_select_fusion
  37.6 1.6 %collective-permute-start.11 = (f16[28,4,8,128]{3,2,1,0:T(8,128)(2,1)S(1)}, f16[28,4,8,128]{3,2,1,0:T(8,128)(2,1)S(1)}, u32[]{:S(2)}, u32[]{:S(2)}) collective-permute-start(f16[28,4,8,128]{3,2,1,0:T(8,128)(2,1)S(1)} %select_select_fusion), channel_id=1, source_target_pairs={{0,4},{2,6},{4,0},{6,2},{8,12},{10,14},{12,8},{14,10},{16,20},{18,... | collective-permute-start | bytes 688136 | tf_op jit(solution)/shard_map/ppermute | solution.py:205
  39.1 0.1 collective-permute-start.15
  39.2 2.4 %collective-permute-start.13 = (f32[16,16,128]{2,1,0:T(8,128)S(1)}, f32[16,16,128]{2,1,0:T(8,128)S(1)}, u32[]{:S(2)}, u32[]{:S(2)}) collective-permute-start(f32[16,16,128]{2,1,0:T(8,128)S(1)} %get-tuple-element.52), channel_id=1, source_target_pairs={{0,2},{2,4},{4,6},{6,8},{8,10},{10,12},{12,14},{14,16},{16,18},{18... | collective-permute-start | bytes 393224 | tf_op jit(solution)/shard_map/ppermute | solution.py:210
  41.6 0.2 broadcast_in_dim.86
  41.8 0.1 fusion.5
  42.0 1.7 %collective-permute-done.11 = f16[28,4,8,128]{3,2,1,0:T(8,128)(2,1)S(1)} collective-permute-done((f16[28,4,8,128]{3,2,1,0:T(8,128)(2,1)S(1)}, f16[28,4,8,128]{3,2,1,0:T(8,128)(2,1)S(1)}, u32[]{:S(2)}, u32[]{:S(2)}) %collective-permute-start.11) | collective-permute-done | bytes 229408 | tf_op jit(solution)/shard_map/ppermute | solution.py:205
  43.7 0.1 fusion.7
  43.8 0.1 fusion.9
  44.0 1.2 %collective-permute-done.12 = f16[28,4,8,128]{3,2,1,0:T(8,128)(2,1)S(1)} collective-permute-done((f16[28,4,8,128]{3,2,1,0:T(8,128)(2,1)S(1)}, f16[28,4,8,128]{3,2,1,0:T(8,128)(2,1)S(1)}, u32[]{:S(2)}, u32[]{:S(2)}) %collective-permute-start.12) | collective-permute-done | bytes 229408 | tf_op jit(solution)/shard_map/ppermute | solution.py:205
  45.2 0.1 fusion.11
  45.3 0.0 copy-start.4
  45.3 0.9 %shard_map.64 = (bf16[16,16,128]{2,1,0:T(8,128)(2,1)}, bf16[2,16,32,128]{3,2,1,0:T(8,128)(2,1)}) custom-call(f32[16,16,128]{2,1,0:T(8,128)S(1)} %get-tuple-element.43.own_ref, f32[16,16,128]{2,1,0:T(8,128)S(1)} %collective-permute-done.13.below_ref, f32[2,16,32,128]{3,2,1,0:T(8,128)S(1)} %get-tuple-element.55.part_ref, ...), custom_call_target="tpu_custom_call" | custom-call | bytes 1638400 | tf_op jit(solution)/shard_map/pallas_call | solution.py:192
  46.2 0.4 copy-done.4
  (31 shorter events, 0.3 us)
Async XLA Ops:
  0.6 9.6 %collective-permute-start = (bf16[2,16,32,128]{3,2,1,0:T(8,128)(2,1)}, bf16[2,16,32,128]{3,2,1,0:T(8,128)(2,1)S(1)}, u32[]{:S(2)}, u32[]{:S(2)}) collective-permute-start(bf16[2,16,32,128]{3,2,1,0:T(8,128)(2,1)} %volume_ref.1), channel_id=1, source_target_pairs={{0,1},{1,0},{2,3},{3,2},{4,5},{5,4},{6,7},{7,6},{8,9},{9,8},{10,11... | collective-permute-start | bytes 786440 | tf_op jit(solution)/shard_map/ppermute | solution.py:205
  3.7 4.0 %collective-permute-start.1 = (bf16[1,16,16,128]{3,2,1,0:T(8,128)(2,1)}, bf16[1,16,16,128]{3,2,1,0:T(8,128)(2,1)S(1)}, u32[]{:S(2)}, u32[]{:S(2)}) collective-permute-start(bf16[1,16,16,128]{3,2,1,0:T(8,128)(2,1)} %param.5), channel_id=1, source_target_pairs={{2,0},{4,2},{6,4},{8,6},{10,8},{12,10},{14,12},{16,14},{18,16},{20... | collective-permute-start | bytes 196616 | tf_op jit(solution)/shard_map/ppermute | solution.py:210
  5.0 0.8 %copy-start.1 = (bf16[1,16,16,128]{3,2,1,0:T(8,128)(2,1)S(1)}, bf16[1,16,16,128]{3,2,1,0:T(8,128)(2,1)}, u32[]{:S(2)}) copy-start(bf16[1,16,16,128]{3,2,1,0:T(8,128)(2,1)} %param.5) | copy-start | bytes 196612
  5.9 0.9 %copy-start.3 = (bf16[2,16,32,128]{3,2,1,0:T(8,128)(2,1)S(1)}, bf16[2,16,32,128]{3,2,1,0:T(8,128)(2,1)}, u32[]{:S(2)}) copy-start(bf16[2,16,32,128]{3,2,1,0:T(8,128)(2,1)} %volume_ref.1) | copy-start | bytes 786436
  10.2 1.4 %copy-start = (bf16[3,3,3,128,128]{4,3,2,1,0:T(8,128)(2,1)S(1)}, bf16[3,3,3,128,128]{4,3,2,1,0:T(8,128)(2,1)}, u32[]{:S(2)}) copy-start(bf16[3,3,3,128,128]{4,3,2,1,0:T(8,128)(2,1)} %param.4) | copy-start | bytes 2654212
  10.8 2.0 %collective-permute-start.2 = (f16[28,64,128]{2,1,0:T(8,128)(2,1)S(1)}, f16[28,64,128]{2,1,0:T(8,128)(2,1)S(1)}, u32[]{:S(2)}, u32[]{:S(2)}) collective-permute-start(f16[28,64,128]{2,1,0:T(8,128)(2,1)S(1)} %fusion), channel_id=1, source_target_pairs={{0,2},{2,0},{4,6},{6,4},{8,10},{10,8},{12,14},{14,12},{16,18},{18,... | collective-permute-start | bytes 1376264 | tf_op jit(solution)/shard_map/ppermute | solution.py:205
  11.6 3.6 %copy-start.2 = (bf16[1,16,16,128]{3,2,1,0:T(8,128)(2,1)S(1)}, bf16[1,16,16,128]{3,2,1,0:T(8,128)(2,1)}, u32[]{:S(2)}) copy-start(bf16[1,16,16,128]{3,2,1,0:T(8,128)(2,1)} %param.5) | copy-start | bytes 196612
  13.1 7.2 %collective-permute-start.3 = (f16[28,3,8,128]{3,2,0,1:T(8,128)(2,1)S(1)}, f16[28,3,8,128]{3,2,0,1:T(8,128)(2,1)S(1)}, u32[]{:S(2)}, u32[]{:S(2)}) collective-permute-start(f16[28,3,8,128]{3,2,0,1:T(8,128)(2,1)S(1)} %copy.21), channel_id=1, source_target_pairs={{0,4},{2,6},{4,0},{6,2},{8,12},{10,14},{12,8},{14,10},{16,20},{18,... | collective-permute-start | bytes 516104 | tf_op jit(solution)/shard_map/ppermute | solution.py:205
  14.9 12.1 %collective-permute-start.5 = (f16[28,8,128]{2,1,0:T(8,128)(2,1)S(1)}, f16[28,8,128]{2,1,0:T(8,128)(2,1)S(1)}, u32[]{:S(2)}, u32[]{:S(2)}) collective-permute-start(f16[28,8,128]{2,1,0:T(8,128)(2,1)S(1)} %slice_bitcast_fusion.8), channel_id=1, source_target_pairs={{0,4},{2,6},{4,0},{6,2},{8,12},{10,14},{12,8},{14,10},{16,20},{18,... | collective-permute-start | bytes 172040 | tf_op jit(solution)/shard_map/ppermute | solution.py:205
  20.4 6.6 %collective-permute-start.4 = (f16[28,8,128]{2,1,0:T(8,128)(2,1)S(1)}, f16[28,8,128]{2,1,0:T(8,128)(2,1)S(1)}, u32[]{:S(2)}, u32[]{:S(2)}) collective-permute-start(f16[28,8,128]{2,1,0:T(8,128)(2,1)S(1)} %fusion.34), channel_id=1, source_target_pairs={{0,24},{2,26},{4,28},{6,30},{8,16},{10,18},{12,20},{14,22},{16,8},... | collective-permute-start | bytes 172040 | tf_op jit(solution)/shard_map/ppermute | solution.py:205
  24.4 5.3 %collective-permute-start.7 = (f16[28,8,128]{2,1,0:T(8,128)(2,1)S(1)}, f16[28,8,128]{2,1,0:T(8,128)(2,1)S(1)}, u32[]{:S(2)}, u32[]{:S(2)}) collective-permute-start(f16[28,8,128]{2,1,0:T(8,128)(2,1)S(1)} %get-tuple-element.70), channel_id=1, source_target_pairs={{0,16},{2,18},{4,20},{6,22},{8,24},{10,26},{12,28},{14,30},{16,0},... | collective-permute-start | bytes 172040 | tf_op jit(solution)/shard_map/ppermute | solution.py:205
  24.5 5.2 %collective-permute-start.6 = (f16[28,8,128]{2,1,0:T(8,128)(2,1)S(1)}, f16[28,8,128]{2,1,0:T(8,128)(2,1)S(1)}, u32[]{:S(2)}, u32[]{:S(2)}) collective-permute-start(f16[28,8,128]{2,1,0:T(8,128)(2,1)S(1)} %get-tuple-element.69), channel_id=1, source_target_pairs={{0,8},{2,10},{4,12},{6,14},{8,0},{10,2},{12,4},{14,6},{16,24},{18,... | collective-permute-start | bytes 172040 | tf_op jit(solution)/shard_map/ppermute | solution.py:205
  29.8 6.6 %collective-permute-start.10 = (f16[28,8,128]{2,1,0:T(8,128)(2,1)S(1)}, f16[28,8,128]{2,1,0:T(8,128)(2,1)S(1)}, u32[]{:S(2)}, u32[]{:S(2)}) collective-permute-start(f16[28,8,128]{2,1,0:T(8,128)(2,1)S(1)} %fusion.19), channel_id=1, source_target_pairs={{0,24},{2,26},{4,28},{6,30},{8,16},{10,18},{12,20},{14,22},{16,8},... | collective-permute-start | bytes 172040 | tf_op jit(solution)/shard_map/ppermute | solution.py:205
  31.5 4.8 %collective-permute-start.9 = (f16[28,8,128]{2,1,0:T(8,128)(2,1)S(1)}, f16[28,8,128]{2,1,0:T(8,128)(2,1)S(1)}, u32[]{:S(2)}, u32[]{:S(2)}) collective-permute-start(f16[28,8,128]{2,1,0:T(8,128)(2,1)S(1)} %fusion.19), channel_id=1, source_target_pairs={{0,8},{2,10},{4,12},{6,14},{8,0},{10,2},{12,4},{14,6},{16,24},{18,... | collective-permute-start | bytes 172040 | tf_op jit(solution)/shard_map/ppermute | solution.py:205
  32.3 5.1 %collective-permute-start.8 = (f16[28,8,128]{2,1,0:T(8,128)(2,1)S(1)}, f16[28,8,128]{2,1,0:T(8,128)(2,1)S(1)}, u32[]{:S(2)}, u32[]{:S(2)}) collective-permute-start(f16[28,8,128]{2,1,0:T(8,128)(2,1)S(1)} %fusion.19), channel_id=1, source_target_pairs={{0,16},{2,18},{4,20},{6,22},{8,24},{10,26},{12,28},{14,30},{16,0},... | collective-permute-start | bytes 172040 | tf_op jit(solution)/shard_map/ppermute | solution.py:205
  34.2 11.1 %collective-permute-start.14 = (f32[2,16,32,128]{3,2,1,0:T(8,128)S(1)}, f32[2,16,32,128]{3,2,1,0:T(8,128)S(1)}, u32[]{:S(2)}, u32[]{:S(2)}) collective-permute-start(f32[2,16,32,128]{3,2,1,0:T(8,128)S(1)} %get-tuple-element.53), channel_id=1, source_target_pairs={{0,1},{1,0},{2,3},{3,2},{4,5},{5,4},{6,7},{7,6},{8,9},{9,8},{10,11... | collective-permute-start | bytes 1572872 | tf_op jit(solution)/shard_map/ppermute | solution.py:205
  37.6 6.1 %collective-permute-start.11 = (f16[28,4,8,128]{3,2,1,0:T(8,128)(2,1)S(1)}, f16[28,4,8,128]{3,2,1,0:T(8,128)(2,1)S(1)}, u32[]{:S(2)}, u32[]{:S(2)}) collective-permute-start(f16[28,4,8,128]{3,2,1,0:T(8,128)(2,1)S(1)} %select_select_fusion), channel_id=1, source_target_pairs={{0,4},{2,6},{4,0},{6,2},{8,12},{10,14},{12,8},{14,10},{16,20},{18,... | collective-permute-start | bytes 688136 | tf_op jit(solution)/shard_map/ppermute | solution.py:205
  39.1 4.5 %collective-permute-start.15 = (f16[28,4,8,128]{3,2,1,0:T(8,128)(2,1)S(1)}, f16[28,4,8,128]{3,2,1,0:T(8,128)(2,1)S(1)}, u32[]{:S(2)}, u32[]{:S(2)}) collective-permute-start(f16[28,4,8,128]{3,2,1,0:T(8,128)(2,1)S(1)} %select_select_fusion), channel_id=1, source_target_pairs={{0,2},{2,0},{4,6},{6,4},{8,10},{10,8},{12,14},{14,12},{16,18},{18,... | collective-permute-start | bytes 688136 | tf_op jit(solution)/shard_map/ppermute | solution.py:205
  39.2 6.1 %collective-permute-start.13 = (f32[16,16,128]{2,1,0:T(8,128)S(1)}, f32[16,16,128]{2,1,0:T(8,128)S(1)}, u32[]{:S(2)}, u32[]{:S(2)}) collective-permute-start(f32[16,16,128]{2,1,0:T(8,128)S(1)} %get-tuple-element.52), channel_id=1, source_target_pairs={{0,2},{2,4},{4,6},{6,8},{8,10},{10,12},{12,14},{14,16},{16,18},{18... | collective-permute-start | bytes 393224 | tf_op jit(solution)/shard_map/ppermute | solution.py:210
  43.7 1.5 %collective-permute-start.12 = (f16[28,4,8,128]{3,2,1,0:T(8,128)(2,1)S(1)}, f16[28,4,8,128]{3,2,1,0:T(8,128)(2,1)S(1)}, u32[]{:S(2)}, u32[]{:S(2)}) collective-permute-start(f16[28,4,8,128]{3,2,1,0:T(8,128)(2,1)S(1)} %collective-permute-done.11), channel_id=1, source_target_pairs={{0,2},{2,0},{4,6},{6,4},{8,10},{10,8},{12,14},{14,12},{16,18},{18,... | collective-permute-start | bytes 688136 | tf_op jit(solution)/shard_map/ppermute | solution.py:205
  45.3 1.3 %copy-start.4 = (f32[27,2,2,4,8,128]{5,4,3,2,1,0:T(8,128)}, f32[27,2,2,4,8,128]{5,4,3,2,1,0:T(8,128)S(1)}, u32[]{:S(2)}) copy-start(f32[27,2,2,4,8,128]{5,4,3,2,1,0:T(8,128)S(1)} %fusion.11) | copy-start | bytes 5308420
